TPU v7x, 512 devices: a whole 4x8x8 slice. The times are simulated.
512 devices in a mesh: section: 4 (over x), seq: 128 (over z, y, core).
Axes of the slice: x: 4, y: 8, z: 8, core: 2. Of those that a mesh axis runs over, the one named last changes fastest.
Arguments:
- hidden: bfloat16 [65536, 4096], P('seq', 'section'), may hold values from -6 to 6
- norm_gain: bfloat16 [4096], P('section'), may hold values from 0.25 to 1.75
- query_weight: bfloat16 [4096, 512], P(None, 'section')
- key_weight: bfloat16 [4096, 128], P('section')
- value_weight: bfloat16 [4096, 128], P('section'), may hold values from -0.5 to 0.5
- output_weight: bfloat16 [512, 4096], P(None, 'section'), may hold values from -0.25 to 0.25
- block_reach: int32 [512], P('seq'), may hold values from 0 to 2
- header_ids: int32 [2], replicated, may hold values from 0 to 511, as said below
Outputs:
- attention_out: bfloat16 [65536, 4096], P('seq', 'section')
Inputs may be any that keep to these rules, and one draw needn't show every extreme that they name: `header_ids`: the 2 indices are distinct block indices, and the last block, 511, is always one of them, at any position.
All inputs are finite; a program needn't handle non-finite values.
Results may differ from a plain program's by a relative error of at most 0.014.
Values may be sent and summed in bfloat16 or wider, within the bound.
No kernel may reach another device: no remote copies, remote signals or barrier semaphores. Data moves between devices by JAX's collectives and lax.ppermute only.
A program may use at most 64 MiB of HBM per device.

v0:
```python
import math

import jax
import jax.numpy as jnp
from jax import lax
from jax.sharding import PartitionSpec as P

BLOCK = 128
REACH = 2


EPSILON = 1e-05
THETA = 500000.0


def merged(value, axis, combine):
    everything = jax.tree.map(lambda part: lax.all_gather(part, axis), value)
    leading = jax.tree.map(lambda part: part[0], everything)

    def lap(k, so_far):
        return combine(so_far, jax.tree.map(lambda part: part[k], everything))

    return lax.fori_loop(1, lax.axis_size(axis), lap, leading)


def padded(cells, sides, width):
    for axis, dim in sides:
        count = lax.axis_size(axis)
        ends = count - 1
        head = lax.slice_in_dim(cells, 0, width, axis=dim)
        tail = lax.slice_in_dim(cells, cells.shape[dim] - width, cells.shape[dim], axis=dim)
        cells = jnp.concatenate(
            [
                lax.ppermute(tail, axis, [(i, (i + 1) % count) for i in range(ends)]),
                cells,
                lax.ppermute(head, axis, [((i + 1) % count, i) for i in range(ends)]),
            ],
            axis=dim,
        )
    return cells


def tables(positions, head_width):
    middle = head_width // 2
    frequency = jnp.exp(
        -(2.0 / head_width) * math.log(THETA) * jnp.arange(middle, dtype=jnp.float32)
    )
    angles = positions.astype(jnp.float32)[:, None] * frequency[None, :]
    angles = jnp.concatenate([angles, angles], axis=1)
    return (jnp.cos(angles), jnp.sin(angles))


def rotate(values, cosine_table, sine_table):
    middle = values.shape[-1] // 2
    turned = jnp.concatenate([-values[..., middle:], values[..., :middle]], axis=-1)
    return values * cosine_table + turned * sine_table


def combine_parts(earlier, later):
    first_max, first_total, first_out = earlier
    second_max, second_total, second_out = later
    overall = jnp.maximum(first_max, second_max)
    first_factor = jnp.exp(first_max - overall)
    second_factor = jnp.exp(second_max - overall)
    return (
        overall,
        first_total * first_factor + second_total * second_factor,
        first_out * first_factor[:, None] + second_out * second_factor[:, None],
    )


def on_device(
    hidden,
    norm_gain,
    query_weight,
    key_weight,
    value_weight,
    output_weight,
    block_reach,
    header_ids,
):
    row_count = hidden.shape[0]
    part_width = hidden.shape[1]
    head_width = key_weight.shape[1]
    local_blocks = row_count // BLOCK
    total_blocks = local_blocks * lax.axis_size("seq")
    seq_place = lax.axis_index("seq")
    floats = hidden.astype(jnp.float32)
    squares = lax.psum(jnp.sum(floats * floats, axis=1), "section")
    scaling = lax.rsqrt(squares / (part_width * lax.axis_size("section")) + EPSILON)
    normed_part = (floats * scaling[:, None] * norm_gain.astype(jnp.float32)[None, :]).astype(
        jnp.bfloat16
    )
    weight_rows = query_weight
    query_sum = jnp.dot(
        lax.all_gather(normed_part, "section", axis=1, tiled=True),
        weight_rows,
        preferred_element_type=jnp.float32,
    )
    key_sum, value_sum = lax.psum(
        (
            jnp.dot(normed_part, key_weight, preferred_element_type=jnp.float32),
            jnp.dot(normed_part, value_weight, preferred_element_type=jnp.float32),
        ),
        "section",
    )
    positions = seq_place * row_count + jnp.arange(row_count, dtype=jnp.int32)
    cosine_table, sine_table = tables(positions, head_width)
    queries = rotate(query_sum, cosine_table, sine_table).astype(jnp.bfloat16)
    keys_here = rotate(key_sum, cosine_table, sine_table).astype(jnp.bfloat16)
    values_here = value_sum.astype(jnp.bfloat16)
    packed = jnp.concatenate([queries, keys_here, values_here], axis=1)
    block_numbers = seq_place * local_blocks + jnp.arange(local_blocks, dtype=jnp.int32)
    select = header_ids[:, None] == block_numbers[None, :]
    shaped = packed.reshape(local_blocks, BLOCK, 3 * head_width)
    picked = jnp.einsum(
        "hb,bre->hre", select.astype(jnp.bfloat16), shaped, preferred_element_type=jnp.float32
    )
    header_pack = lax.psum(picked, "seq").astype(jnp.bfloat16).reshape(-1, 3 * head_width)
    head_queries = header_pack[:, :head_width]
    head_keys = header_pack[:, head_width : 2 * head_width]
    head_values = header_pack[:, 2 * head_width :]
    inverse_root = 1.0 / math.sqrt(head_width)
    far_scores = (
        jnp.einsum("qd,kd->qk", head_queries, keys_here, preferred_element_type=jnp.float32)
        * inverse_root
    )
    far_max = jnp.max(far_scores, axis=1)
    far_weights = jnp.exp(far_scores - far_max[:, None])
    far_total = jnp.sum(far_weights, axis=1)
    far_out = jnp.dot(
        far_weights.astype(jnp.bfloat16), values_here, preferred_element_type=jnp.float32
    )
    merged_max, merged_total, merged_out = merged(
        (far_max, far_total, far_out), "seq", combine_parts
    )
    header_result = merged_out / merged_total[:, None]
    margin_rows = REACH * BLOCK
    stacked = jnp.concatenate([keys_here, values_here], axis=1)
    extended = padded(stacked, (("seq", 0),), margin_rows)
    near_keys = extended[:, :head_width]
    near_values = extended[:, head_width:]
    extent = row_count + 2 * margin_rows
    key_blocks = seq_place * local_blocks - REACH + jnp.arange(extent, dtype=jnp.int32) // BLOCK
    query_blocks = seq_place * local_blocks + jnp.arange(row_count, dtype=jnp.int32) // BLOCK
    limits = jnp.repeat(block_reach, BLOCK)
    key_header = jnp.any(header_ids[:, None] == key_blocks[None, :], axis=0)
    allowed = (key_blocks >= 0)[None, :] & (key_blocks < total_blocks)[None, :]
    allowed = allowed & (jnp.abs(key_blocks[None, :] - query_blocks[:, None]) <= limits[:, None])
    allowed = allowed & jnp.logical_not(key_header)[None, :]
    near_scores = (
        jnp.einsum("qd,kd->qk", queries, near_keys, preferred_element_type=jnp.float32)
        * inverse_root
    )
    near_scores = jnp.where(allowed, near_scores, -jnp.inf)
    head_scores = (
        jnp.einsum("qd,kd->qk", queries, head_keys, preferred_element_type=jnp.float32)
        * inverse_root
    )
    scores = jnp.concatenate([near_scores, head_scores], axis=1)
    row_top = jnp.max(scores, axis=1)
    weights = jnp.exp(scores - row_top[:, None])
    row_sums = jnp.sum(weights, axis=1)
    joined = jnp.concatenate([near_values, head_values], axis=0)
    mixed_out = (
        jnp.dot(weights.astype(jnp.bfloat16), joined, preferred_element_type=jnp.float32)
        / row_sums[:, None]
    )
    header_local = jnp.einsum(
        "hb,hre->bre", select.astype(jnp.float32), header_result.reshape(-1, BLOCK, head_width)
    )
    is_local_header = jnp.any(select, axis=0)
    attended = jnp.where(
        is_local_header[:, None, None],
        header_local,
        mixed_out.reshape(local_blocks, BLOCK, head_width),
    )
    attended = attended.reshape(row_count, head_width).astype(jnp.bfloat16)
    weight_rows = output_weight
    result = jnp.dot(
        lax.all_gather(attended, "section", axis=1, tiled=True),
        weight_rows,
        preferred_element_type=jnp.float32,
    )
    return result.astype(jnp.bfloat16)


def solution(mesh):
    return jax.shard_map(
        on_device,
        mesh=mesh,
        in_specs=(
            P("seq", "section"),
            P("section"),
            P(None, "section"),
            P("section", None),
            P("section", None),
            P(None, "section"),
            P("seq"),
            P(),
        ),
        out_specs=P("seq", "section"),
        check_vma=False,
    )
```

profile of v0, /device:TPU:1, one launch (start us, length us, event | category | flops | bytes accessed | tf_op | source)
XLA Modules:
  0.0 911.5 jit_solution(16988144689448362159)
XLA Ops:
  7.3 1.5 fusion.2
  8.8 9.3 %psum.28 = f32[512]{0:T(512)S(1)} all-reduce(f32[512]{0:T(512)S(1)} %fusion.2), channel_id=1, replica_groups=mesh['section'=4,'seq'=128] {'section'}, use_global_device_ids=true, to_apply=%region_2.0 | all-reduce | flops 512 | bytes 4096 | tf_op jit(solution)/shard_map/psum | solution.py:89
  18.1 1.6 fusion.4
  19.8 1.2 fusion.53
  21.8 1.7 fusion.54
  23.6 13.6 %all-reduce.5 = bf16[512,128]{0,1:T(8,128)(2,1)S(1)} all-reduce(f32[512,128]{0,1:T(8,128)S(1)} %fusion.54), channel_id=1, replica_groups=mesh['section'=4,'seq'=128] {'section'}, use_global_device_ids=true, to_apply=%region_4.0 | all-reduce | flops 65536 | bytes 393216 | tf_op jit(solution)/shard_map/psum | solution.py:100
  37.2 38.7 %all-reduce.4.cloned.1.call-done = f32[512,128]{0,1:T(8,128)} async-done(((f32[512,128]{0,1:T(8,128)}), f32[512,128]{0,1:T(8,128)}) %all-reduce.4.cloned.1.call-update) | async-done | bytes 262160 | tf_op jit(solution)/shard_map/psum | solution.py:100
  77.0 57.6 %all-gather.8.cloned.1.call-done = bf16[512,4096]{1,0:T(8,128)(2,1)} async-done(((bf16[512,1024]{1,0:T(8,128)(2,1)}), bf16[512,4096]{1,0:T(8,128)(2,1)}) %all-gather.8.cloned.1.call-update) | async-done | bytes 4194320 | tf_op jit(solution)/shard_map/all_gather | solution.py:96
  134.5 3.7 fusion.52
  140.2 491.6 %all-reduce.6 = bf16[2,128,384]{2,0,1:T(2,128)(2,1)S(1)} all-reduce(f32[2,128,384]{2,0,1:T(2,128)S(1)} %fusion.48), channel_id=1, replica_groups=mesh['section'=4,'seq'=128] {'seq'}, use_global_device_ids=true, to_apply=%region_5.0 | all-reduce | flops 98304 | bytes 589824 | tf_op jit(solution)/shard_map/psum | solution.py:119
  633.7 51.2 %all-gather.3 = f32[128,1,256]{2,1,0:T(1,128)S(1)} all-gather(f32[1,1,256]{2,1,0:T(1,128)S(1)} %bitcast.66), channel_id=2, replica_groups=mesh['section'=4,'seq'=128] {'seq'}, dimensions={0}, use_global_device_ids=true | all-gather | bytes 132096 | tf_op jit(solution)/shard_map/all_gather | solution.py:17
  685.2 50.8 %all-gather.4 = f32[128,1,256]{2,1,0:T(1,128)S(1)} all-gather(f32[1,1,256]{2,1,0:T(1,128)S(1)} %bitcast.67), channel_id=3, replica_groups=mesh['section'=4,'seq'=128] {'seq'}, dimensions={0}, use_global_device_ids=true | all-gather | bytes 132096 | tf_op jit(solution)/shard_map/all_gather | solution.py:17
  736.1 2.1 collective-permute-start.1
  738.1 3.5 collective-permute-start
  742.3 1.2 collective-permute-done
  747.2 144.2 %while.19 = (s32[]{:T(128)}, f32[256]{0:T(256)S(1)}, f32[256]{0:T(256)S(1)}, f32[256,128]{1,0:T(8,128)S(1)}, f32[128,256]{1,0:T(8,128)S(1)}, /*index=5*/f32[128,...) while((s32[]{:T(128)}, f32[256]{0:T(256)S(1)}, f32[256]{0:T(256)S(1)}, ...), condition=%wide.region_9.10_spmd, body=%wide.region_8.0_spmd.sunk | while | flops 99845 | bytes 407703 | solution.py:23
  747.3 1.1 fusion.69
  748.4 1.1 fusion.69
  750.7 1.1 fusion.69
  752.9 1.1 fusion.69
  755.2 1.1 fusion.69
  757.5 1.1 fusion.69
  759.8 1.1 fusion.69
  762.0 1.1 fusion.69
  764.3 1.1 fusion.69
  765.4 1.1 fusion.69
  766.6 1.1 fusion.69
  767.7 1.1 fusion.69
  768.8 1.1 fusion.69
  770.0 1.1 fusion.69
  891.9 11.3 %all_gather.31 = bf16[512,512]{1,0:T(8,128)(2,1)S(1)} all-gather(bf16[512,128]{1,0:T(8,128)(2,1)S(1)} %bitcast.59), channel_id=1, replica_groups=mesh['section'=4,'seq'=128] {'section'}, dimensions={1}, use_global_device_ids=true | all-gather | bytes 655360 | tf_op jit(solution)/shard_map/all_gather | solution.py:181
  903.2 1.7 convolution_convert_fusion
  (442 shorter events, 136.6 us)
Async XLA Ops:
  6.5 896.7 %copy-start = (bf16[512,1024]{1,0:T(8,128)(2,1)S(1)}, bf16[512,1024]{1,0:T(8,128)(2,1)}, u32[]{:S(2)}) copy-start(bf16[512,1024]{1,0:T(8,128)(2,1)} %param.15) | copy-start | bytes 3145732
  6.5 13.2 %copy-start.7 = (bf16[1024,128]{1,0:T(8,128)(2,1)S(1)}, bf16[1024,128]{1,0:T(8,128)(2,1)}, u32[]{:S(2)}) copy-start(bf16[1024,128]{1,0:T(8,128)(2,1)} %param.13) | copy-start | bytes 786436
  6.5 69.4 %all-reduce.4.cloned.1.call-start = ((), (), s32[]{:S(2)}) async-start(), calls=%async_computation.1 | async-start | bytes 524288 | tf_op jit(solution)/shard_map/psum | solution.py:100
  18.1 3.6 copy-start.8
  19.7 1.3 copy-start.1
  20.9 113.6 %copy-start.4 = (bf16[4096,128]{1,0:T(8,128)(2,1)S(1)}, bf16[4096,128]{1,0:T(8,128)(2,1)}, u32[]{:S(2)}) copy-start(bf16[4096,128]{1,0:T(8,128)(2,1)} %param.12) | copy-start | bytes 3145732
  21.0 113.5 %all-gather.8.cloned.1.call-start = ((), (), s32[]{:S(2)}) async-start(), calls=%async_computation | async-start | bytes 5242880 | tf_op jit(solution)/shard_map/all_gather | solution.py:96
  21.7 724.5 %all-gather.10.cloned.1.call-start = ((), (), s32[]{:S(2)}) async-start(), calls=%async_computation.2 | async-start | bytes 16908288 | tf_op jit(solution)/shard_map/all_gather | solution.py:17
  77.0 61.3 %copy-start.3 = (f32[512,128]{0,1:T(8,128)S(1)}, f32[512,128]{0,1:T(8,128)}, u32[]{:S(2)}) copy-start(f32[512,128]{0,1:T(8,128)} %all-reduce.4.cloned.1.call-done) | copy-start | bytes 786436
  138.2 1.6 copy-start.9
  139.8 493.9 %copy-start.10 = (s32[4]{0:T(128)S(1)}, s32[4]{0:T(128)}, u32[]{:S(2)}) copy-start(s32[4]{0:T(128)} %param.16) | copy-start | bytes 52
  685.0 59.7 %copy-start.6 = (f32[128,1,256]{2,1,0:T(1,128)}, f32[128,1,256]{2,1,0:T(1,128)S(1)}, u32[]{:S(2)}) copy-start(f32[128,1,256]{2,1,0:T(1,128)S(1)} %all-gather.3) | copy-start | bytes 393220
  736.0 8.7 copy-start.5
  736.1 6.3 collective-permute-start.1
  738.1 5.4 collective-permute-start
  743.6 1.1 copy-start.2
  744.7 1.0 slice-start
  745.7 1.5 slice-start.1
  745.7 1.5 slice-start.2
Sparse Core Ops, SparseCore 0:
  21.1 54.8 all-reduce.3
  78.3 56.1 all-gather.7
  633.5 98.3 all-gather.9
where the time goes:
time: 916 us; the launch traced here: 911 us
  blocking collectives  628 us (69%)
  other arithmetic  146 us (16%)
  waiting for transfers between devices  98.6 us (11%)
  between operations  13.5 us (1%)
  matrix products  12.3 us (1%)
    psum x1, blocking collectives, on_device(): lax.psum(picked, 'seq').astype(jnp.bfloat16).reshape(-1, 3 * head_width)  492 us
    add x127, other arithmetic, combine_parts(): first_out * first_factor[:, None] + second_out * second_factor[:, None]  136 us
    all_gather x2, blocking collectives, merged(): everything = jax.tree.map(lambda part: lax.all_gather(part, axis), value)  102 us
    all_gather x1, waiting for transfers between devices, on_device(): lax.all_gather(normed_part, 'section', axis=1, tiled=True)  57.6 us
    psum x1, waiting for transfers between devices, on_device(): lax.psum((jnp.dot(normed_part, key_weight, preferred_element_type=jnp.flo...  38.7 us
  transfers between devices with their start and end apart: 5, of which 4 were waited for; matrix products, arithmetic and copies ran while one was open for 1% of the time, Pallas kernels for 0%

commit v1 on v0

v1 whole, which is shorter than its diff:
```python
import math

import jax
import jax.numpy as jnp
from jax import lax
from jax.sharding import PartitionSpec as P

BLOCK = 128
REACH = 2

EPSILON = 1e-05
THETA = 500000.0


def padded(cells, axis, width):
    count = lax.axis_size(axis)
    ends = count - 1
    head = cells[:width]
    tail = cells[cells.shape[0] - width :]
    return jnp.concatenate(
        [
            lax.ppermute(tail, axis, [(i, i + 1) for i in range(ends)]),
            cells,
            lax.ppermute(head, axis, [(i + 1, i) for i in range(ends)]),
        ],
        axis=0,
    )


def tables(positions, head_width):
    middle = head_width // 2
    frequency = jnp.exp(
        -(2.0 / head_width) * math.log(THETA) * jnp.arange(middle, dtype=jnp.float32)
    )
    angles = positions.astype(jnp.float32)[:, None] * frequency[None, :]
    cosine, sine = jnp.cos(angles), jnp.sin(angles)
    return jnp.concatenate([cosine, cosine], axis=1), jnp.concatenate([-sine, sine], axis=1)


def rotate(values, cosine, signed_sine):
    middle = values.shape[-1] // 2
    turned = jnp.concatenate([values[..., middle:], values[..., :middle]], axis=-1)
    return values * cosine + turned * signed_sine


def split_float(value):
    high = value.astype(jnp.bfloat16)
    low = (value - high.astype(jnp.float32)).astype(jnp.bfloat16)
    return high, low


def to_all(chunk, axis):
    copies = jnp.broadcast_to(chunk[None], (lax.axis_size(axis),) + chunk.shape)
    return lax.all_to_all(copies, axis, 0, 0)


def on_device(
    hidden,
    norm_gain,
    query_weight,
    key_weight,
    value_weight,
    output_weight,
    block_reach,
    header_ids,
):
    bf16, f32 = jnp.bfloat16, jnp.float32
    rows, part = hidden.shape
    head_width = key_weight.shape[1]
    sections = lax.axis_size("section")
    shards = lax.axis_size("seq")
    local_blocks = rows // BLOCK
    total_blocks = local_blocks * shards
    seq_place = lax.axis_index("seq")
    headers = header_ids.shape[0]
    lines = headers * BLOCK // shards // headers
    owners = header_ids // local_blocks
    slots = header_ids % local_blocks

    candidates = jnp.stack(
        [
            lax.dynamic_slice_in_dim(hidden, slots[h] * BLOCK, BLOCK, axis=0)
            for h in range(headers)
        ]
    )
    spread = lax.all_to_all(
        candidates.reshape(headers, shards, lines, part).transpose(1, 0, 2, 3), "seq", 0, 0
    )
    header_rows = jnp.concatenate(
        [
            lax.dynamic_slice_in_dim(spread[:, h], owners[h], 1, axis=0)[0]
            for h in range(headers)
        ]
    )
    head_weights = lax.all_to_all(
        query_weight.reshape(sections, part, head_width), "section", 0, 0
    )

    mine = headers * lines
    everything = jnp.concatenate([hidden, header_rows], axis=0)
    floats = everything.astype(f32)
    gained = (floats * norm_gain.astype(f32)[None, :]).astype(bf16)
    squares = jnp.sum(floats * floats, axis=1)
    high, low = split_float(squares)
    extra = jnp.concatenate(
        [
            jnp.pad(high, (0, -high.shape[0] % head_width)).reshape(-1, head_width),
            jnp.pad(low, (0, -low.shape[0] % head_width)).reshape(-1, head_width),
        ]
    )
    extra = jnp.pad(extra, ((0, 0), (0, 2 * head_width)))
    keyval_weight = jnp.concatenate([key_weight, value_weight], axis=1)
    keyval = jnp.dot(gained, keyval_weight, preferred_element_type=f32).astype(bf16)
    queries_part = jnp.einsum(
        "rd,hde->hre", gained, head_weights, preferred_element_type=f32
    ).astype(bf16)
    payload = jnp.concatenate(
        [
            queries_part,
            jnp.broadcast_to(keyval[None], (sections,) + keyval.shape),
        ],
        axis=2,
    )
    payload = jnp.concatenate(
        [payload, jnp.broadcast_to(extra[None], (sections,) + extra.shape)], axis=1
    )
    arrived = lax.all_to_all(payload, "section", 0, 0)
    total = jnp.sum(arrived.astype(f32), axis=0)
    count = rows + mine
    sums = total[count:, :head_width]
    half = sums.shape[0] // 2
    squares_all = (sums[:half] + sums[half:]).reshape(-1)[:count]
    scaling = lax.rsqrt(squares_all / (part * sections) + EPSILON)
    total = total[:count] * scaling[:, None]

    own_positions = seq_place * rows + jnp.arange(rows, dtype=jnp.int32)
    header_positions = (
        header_ids[:, None] * BLOCK + seq_place * lines + jnp.arange(lines, dtype=jnp.int32)[None]
    ).reshape(-1)
    cosine, sine = tables(jnp.concatenate([own_positions, header_positions]), head_width)
    queries = rotate(total[:, :head_width], cosine, sine).astype(bf16)
    keys = rotate(total[:, head_width : 2 * head_width], cosine, sine).astype(bf16)
    values = total[:, 2 * head_width :].astype(bf16)
    header_chunk = jnp.concatenate([queries[rows:], keys[rows:], values[rows:]], axis=1)
    header_pack = to_all(header_chunk, "seq").reshape(-1, 3 * head_width)
    queries, keys, values = queries[:rows], keys[:rows], values[:rows]
    head_queries = header_pack[:, :head_width]
    head_keys = header_pack[:, head_width : 2 * head_width]
    head_values = header_pack[:, 2 * head_width :]

    inverse_root = 1.0 / math.sqrt(head_width)
    far_scores = (
        jnp.einsum("qd,kd->qk", head_queries, keys, preferred_element_type=f32) * inverse_root
    )
    far_max = jnp.max(far_scores, axis=1, keepdims=True)
    far_weights = jnp.exp(far_scores - far_max)
    far_total = jnp.sum(far_weights, axis=1, keepdims=True)
    far_out = jnp.dot(far_weights.astype(bf16), values, preferred_element_type=f32)
    half_lanes = (far_out.shape[0], head_width // 2)
    partial = jnp.concatenate(
        [
            far_out,
            jnp.broadcast_to(far_max, half_lanes),
            jnp.broadcast_to(far_total, half_lanes),
        ],
        axis=1,
    )
    parts = lax.all_to_all(partial.reshape(shards, mine, 2 * head_width), "seq", 0, 0)
    part_max = parts[..., head_width : head_width + 1]
    part_total = parts[..., head_width + head_width // 2 : head_width + head_width // 2 + 1]
    factor = jnp.exp(part_max - jnp.max(part_max, axis=0, keepdims=True))
    header_result = jnp.sum(parts[..., :head_width] * factor, axis=0) / jnp.sum(
        part_total * factor, axis=0
    )
    header_all = to_all(header_result.astype(bf16), "seq").reshape(
        shards, headers, lines, head_width
    )

    margin_rows = REACH * BLOCK
    extended = padded(jnp.concatenate([keys, values], axis=1), "seq", margin_rows)
    near_keys = extended[:, :head_width]
    near_values = extended[:, head_width:]
    extent = rows + 2 * margin_rows
    key_blocks = seq_place * local_blocks - REACH + jnp.arange(extent, dtype=jnp.int32) // BLOCK
    query_blocks = seq_place * local_blocks + jnp.arange(rows, dtype=jnp.int32) // BLOCK
    limits = jnp.repeat(block_reach, BLOCK)
    key_header = jnp.any(header_ids[:, None] == key_blocks[None, :], axis=0)
    allowed = (key_blocks >= 0)[None, :] & (key_blocks < total_blocks)[None, :]
    allowed = allowed & (jnp.abs(key_blocks[None, :] - query_blocks[:, None]) <= limits[:, None])
    allowed = allowed & jnp.logical_not(key_header)[None, :]
    near_scores = (
        jnp.einsum("qd,kd->qk", queries, near_keys, preferred_element_type=f32) * inverse_root
    )
    near_scores = jnp.where(allowed, near_scores, -jnp.inf)
    head_scores = (
        jnp.einsum("qd,kd->qk", queries, head_keys, preferred_element_type=f32) * inverse_root
    )
    scores = jnp.concatenate([near_scores, head_scores], axis=1)
    row_top = jnp.max(scores, axis=1)
    weights = jnp.exp(scores - row_top[:, None])
    row_sums = jnp.sum(weights, axis=1)
    joined = jnp.concatenate([near_values, head_values], axis=0)
    mixed = (
        jnp.dot(weights.astype(bf16), joined, preferred_element_type=f32) / row_sums[:, None]
    ).astype(bf16)

    blocks = []
    for b in range(local_blocks):
        block = mixed[b * BLOCK : (b + 1) * BLOCK]
        for h in range(headers):
            here = header_ids[h] == seq_place * local_blocks + b
            block = jnp.where(here, header_all[:, h].reshape(BLOCK, head_width), block)
        blocks.append(block)
    attended = jnp.concatenate(blocks, axis=0)
    gathered = lax.all_gather(attended, "section", axis=1, tiled=True)
    return jnp.dot(gathered, output_weight, preferred_element_type=f32).astype(bf16)


def solution(mesh):
    return jax.shard_map(
        on_device,
        mesh=mesh,
        in_specs=(
            P("seq", "section"),
            P("section"),
            P(None, "section"),
            P("section", None),
            P("section", None),
            P(None, "section"),
            P("seq"),
            P(),
        ),
        out_specs=P("seq", "section"),
        check_vma=False,
    )
```

time: 916 us -> 183 us (0.20)
  blocking collectives: 628 us -> 12 us
  other arithmetic: 146 us -> 8.73 us
  starting transfers between devices: 5.64 us -> 57.7 us
  waiting for transfers between devices: 98.6 us -> 71.9 us
    psum x3 -> x0, blocking collectives: 515 us -> none  [the longest x1 492 us: on_device(): lax.psum(picked, 'seq').astype(jnp.bfloat16).reshape(-1, 3 * head_width)]
    add x256 -> x3, other arithmetic: 139 us -> 0.76 us  [the longest x1 0.75 us: on_device(): header_ids[:, None] * BLOCK + seq_place * lines]
    all_gather x3 -> x1, blocking collectives: 113 us -> 12 us  [on_device(): gathered = lax.all_gather(attended, 'section', axis=1, tiled=True)]
    all_to_all x0 -> x6, waiting for transfers between devices: none -> 71.9 us  [the longest x1 18.9 us: on_device(): arrived = lax.all_to_all(payload, 'section', 0, 0)]
    all_gather x2 -> x0, waiting for transfers between devices: 57.6 us -> none  [the longest x1 57.6 us: on_device(): lax.all_gather(normed_part, 'section', axis=1, tiled=True)]
    all_to_all x0 -> x6, starting transfers between devices: none -> 52.2 us  [the longest x1 18.4 us: on_device(): lax.all_to_all(candidates.reshape(headers, shards, lines, part).transpose...]
    psum x1 -> x0, waiting for transfers between devices: 38.7 us -> none  [on_device(): lax.psum((jnp.dot(normed_part, key_weight, preferred_element_type=jnp.flo...]
  transfers between devices with their start and end apart: 5 -> 8, of which waited for: 4 -> 6; matrix products, arithmetic and copies ran while one was open for 1% -> 6% of each run, Pallas kernels for 0% -> 0%
where the time goes in v1:
time: 183 us; the launch traced here: 181 us
  waiting for transfers between devices  71.9 us (39%)
  starting transfers between devices  57.7 us (32%)
  blocking collectives  12 us (7%)
  local copies, waits for them, and re-layouts  11.7 us (6%)
  between operations  10.7 us (6%)
  matrix products  8.76 us (5%)
  other arithmetic  8.73 us (5%)
    all_to_all x1, waiting for transfers between devices, on_device(): arrived = lax.all_to_all(payload, 'section', 0, 0)  18.9 us
    all_to_all x1, starting transfers between devices, on_device(): lax.all_to_all(candidates.reshape(headers, shards, lines, part).transpose...  18.4 us
    all_to_all x1, waiting for transfers between devices, on_device(): lax.all_to_all(candidates.reshape(headers, shards, lines, part).transpose...  17 us
    all_to_all x1, waiting for transfers between devices, on_device(): lax.all_to_all(query_weight.reshape(sections, part, head_width), 'section...  13.9 us
    all_to_all x1, starting transfers between devices, on_device(): lax.all_to_all(partial.reshape(shards, mine, 2 * head_width), 'seq', 0, 0)  13.7 us
    all_to_all x2, starting transfers between devices, to_all(): return lax.all_to_all(copies, axis, 0, 0)  12 us
    all_gather x1, blocking collectives, on_device(): gathered = lax.all_gather(attended, 'section', axis=1, tiled=True)  12 us
    all_to_all x2, waiting for transfers between devices, to_all(): return lax.all_to_all(copies, axis, 0, 0)  11.3 us
  transfers between devices with their start and end apart: 8, of which 6 were waited for; matrix products, arithmetic and copies ran while one was open for 6% of the time, Pallas kernels for 0%

profile of v1, /device:TPU:1, one launch (start us, length us, event | category | flops | bytes accessed | tf_op | source)
XLA Modules:
  0.0 181.4 jit_solution(13185356866812417212)
XLA Ops:
  0.0 0.8 multiply_add_fusion
  2.7 1.1 dynamic-slice_bitcast_fusion.1
  3.8 1.3 copy.59
  5.1 18.4 %all-to-all-start = ((bf16[128,2,1,1024]{3,1,2,0:T(2,128)(2,1)}), bf16[128,2,1,1024]{3,1,2,0:T(2,128)(2,1)S(1)}, u32[]{:S(2)}, u32[]{:S(2)}) async-start(bf16[128,2,1,1024]{3,1,2,0:T(2,128)(2,1)} %copy.59), calls=%async_computation | async-start | bytes 1048576 | tf_op jit(solution)/shard_map/all_to_all | solution.py:86
  27.2 17.0 %all-to-all-done = bf16[128,2,1,1024]{3,1,2,0:T(2,128)(2,1)S(1)} async-done(((bf16[128,2,1,1024]{3,1,2,0:T(2,128)(2,1)}), bf16[128,2,1,1024]{3,1,2,0:T(2,128)(2,1)S(1)}, u32[]{:S(2)}, u32[]{:S(2)}) %all-to-all-start) | async-done | bytes 524320 | tf_op jit(solution)/shard_map/all_to_all | solution.py:86
  44.1 4.4 %all-to-all-start.1 = ((bf16[4,1024,128]{2,1,0:T(8,128)(2,1)}), bf16[4,1024,128]{2,1,0:T(8,128)(2,1)}, u32[]{:S(2)}, u32[]{:S(2)}) async-start(bf16[4,1024,128]{2,1,0:T(8,128)(2,1)} %bitcast.60), calls=%async_computation.1 | async-start | bytes 2097152 | tf_op jit(solution)/shard_map/all_to_all | solution.py:95
  48.5 0.7 fusion.66
  50.2 13.9 %all-to-all-done.1 = bf16[4,1024,128]{2,1,0:T(8,128)(2,1)} async-done(((bf16[4,1024,128]{2,1,0:T(8,128)(2,1)}), bf16[4,1024,128]{2,1,0:T(8,128)(2,1)}, u32[]{:S(2)}, u32[]{:S(2)}) %all-to-all-start.1) | async-done | bytes 1048608 | tf_op jit(solution)/shard_map/all_to_all | solution.py:95
  64.1 1.9 %fusion.9 = bf16[4,514,128]{2,1,0:T(8,128)(2,1)S(1)} fusion(bf16[4,1024,128]{2,1,0:T(8,128)(2,1)} %all-to-all-done.1, f32[1024]{0:T(1024)S(1)} %convert_element_type.69, bf16[1,1024]{1,0:T(2,128)(2,1)S(1)} %dynamic-slice_bitcast_fusion.2, bf16[1,1024]{1,0:T(2,128)(2,1)S(1)} %dynamic-slice_bitcast_fusion.3, bf16[512,1024]{1,0:T(8,128)(2,1)S(1)} %copy-done.1), kind=kOutput, calls=%fused_computation.17 | convolution fusion | flops 543441920 | bytes 2631680 | tf_op jit(solution)/shard_map/rd,hde->hre/dot_general | solution.py:114
  66.1 1.4 pad_maximum_fusion
  67.5 3.7 %all-to-all-start.2 = ((bf16[4,524,384]{2,1,0:T(8,128)(2,1)}), bf16[4,524,384]{2,1,0:T(8,128)(2,1)S(1)}, u32[]{:S(2)}, u32[]{:S(2)}) async-start(bf16[4,524,384]{2,1,0:T(8,128)(2,1)} %pad_maximum_fusion), calls=%async_computation.2 | async-start | bytes 3244032 | tf_op jit(solution)/shard_map/all_to_all | solution.py:127
  72.0 1.0 fusion.39
  73.0 18.9 %all-to-all-done.2 = bf16[4,524,384]{2,1,0:T(8,128)(2,1)S(1)} async-done(((bf16[4,524,384]{2,1,0:T(8,128)(2,1)}), bf16[4,524,384]{2,1,0:T(8,128)(2,1)S(1)}, u32[]{:S(2)}, u32[]{:S(2)}) %all-to-all-start.2) | async-done | bytes 1609760 | tf_op jit(solution)/shard_map/all_to_all | solution.py:127
  93.6 0.8 broadcast_in_dim.19
  94.4 6.5 %all-to-all-start.3 = ((bf16[128,2,384]{2,1,0:T(2,128)(2,1)}), bf16[128,2,384]{2,1,0:T(2,128)(2,1)S(1)}, u32[]{:S(2)}, u32[]{:S(2)}) async-start(bf16[128,2,384]{2,1,0:T(2,128)(2,1)} %broadcast_in_dim.19), calls=%async_computation.3 | async-start | bytes 393216 | tf_op jit(solution)/shard_map/all_to_all | solution.py:54
  101.0 3.5 %collective-permute-start = (bf16[256,256]{1,0:T(8,128)(2,1)S(1)}, bf16[256,256]{1,0:T(8,128)(2,1)S(1)}, u32[]{:S(2)}, u32[]{:S(2)}) collective-permute-start(bf16[256,256]{1,0:T(8,128)(2,1)S(1)} %get-tuple-element.22), channel_id=1, source_target_pairs={{0,1},{1,2},{2,3},{3,4},{4,5},{5,6},{6,7},{7,8},{8,9},{9,10},{10,1... | collective-permute-start | bytes 393224 | tf_op jit(solution)/shard_map/ppermute | solution.py:22
  104.6 1.9 %collective-permute-start.1 = (bf16[256,256]{1,0:T(8,128)(2,1)S(1)}, bf16[256,256]{1,0:T(8,128)(2,1)S(1)}, u32[]{:S(2)}, u32[]{:S(2)}) collective-permute-start(bf16[256,256]{1,0:T(8,128)(2,1)S(1)} %get-tuple-element.23), channel_id=1, source_target_pairs={{1,0},{2,1},{3,2},{4,3},{5,4},{6,5},{7,6},{8,7},{9,8},{10,9},{11,1... | collective-permute-start | bytes 393224 | tf_op jit(solution)/shard_map/ppermute | solution.py:24
  113.0 0.8 pad_maximum_fusion.2
  113.9 1.4 all-to-all-done.3
  116.5 0.8 reshape.135
  117.3 13.7 %all-to-all-start.4 = ((f32[128,2,256]{2,1,0:T(2,128)}), f32[128,2,256]{2,1,0:T(2,128)S(1)}, u32[]{:S(2)}, u32[]{:S(2)}) async-start(f32[128,2,256]{2,1,0:T(2,128)} %reshape.135), calls=%async_computation.4 | async-start | bytes 524288 | tf_op jit(solution)/shard_map/all_to_all | solution.py:168
  131.1 2.0 %fusion.72 = (f32[512]{0:T(512)S(1)}, f32[512,1024]{1,0:T(8,128)S(1)}) fusion(bf16[1024,256]{1,0:T(8,128)(2,1)} %pad_maximum_fusion.2, bf16[514,128]{1,0:T(8,128)(2,1)S(1)} %copy-done.7, pred[1024]{0:T(1024)(128)(4,1)} %not.7, s32[512]{0:T(512)S(1)} %broadcast_bitcast_fusion, s32[512]{0:T(512)S(1)} %fusion.54, s32[1024]{0:T(1024)S(1)} %fusion.49, ...), kind=kOutput, calls=%fused_computation.137 | convolution fusion | flops 138411520 | bytes 2502656 | tf_op jit(solution)/shard_map/qd,kd->qk/dot_general | solution.py:192
  134.2 0.8 copy-done.2
  135.5 10.8 %all-to-all-done.4 = f32[128,2,256]{2,1,0:T(2,128)S(1)} async-done(((f32[128,2,256]{2,1,0:T(2,128)}), f32[128,2,256]{2,1,0:T(2,128)S(1)}, u32[]{:S(2)}, u32[]{:S(2)}) %all-to-all-start.4) | async-done | bytes 262176 | tf_op jit(solution)/shard_map/all_to_all | solution.py:168
  146.3 1.0 fusion.67
  147.3 1.0 copy.75
  148.2 1.0 copy.76
  150.6 5.5 %all-to-all-start.5 = ((bf16[128,2,128]{2,1,0:T(2,128)(2,1)}), bf16[128,2,128]{2,1,0:T(2,128)(2,1)S(1)}, u32[]{:S(2)}, u32[]{:S(2)}) async-start(bf16[128,2,128]{2,1,0:T(2,128)(2,1)} %broadcast_in_dim.22), calls=%async_computation.5 | async-start | bytes 131072 | tf_op jit(solution)/shard_map/all_to_all | solution.py:54
  156.1 1.7 fusion.13
  157.8 9.9 %all-to-all-done.5 = bf16[128,2,128]{2,1,0:T(2,128)(2,1)S(1)} async-done(((bf16[128,2,128]{2,1,0:T(2,128)(2,1)}), bf16[128,2,128]{2,1,0:T(2,128)(2,1)S(1)}, u32[]{:S(2)}, u32[]{:S(2)}) %all-to-all-start.5) | async-done | bytes 65568 | tf_op jit(solution)/shard_map/all_to_all | solution.py:54
  167.8 12.0 %all_gather.3 = bf16[512,512]{1,0:T(8,128)(2,1)S(1)} all-gather(bf16[512,128]{1,0:T(8,128)(2,1)S(1)} %pad_maximum_fusion.7), channel_id=1, replica_groups=mesh['section'=4,'seq'=128] {'section'}, dimensions={1}, use_global_device_ids=true | all-gather | bytes 655360 | tf_op jit(solution)/shard_map/all_gather | solution.py:215
  179.7 1.7 convolution_convert_fusion
  (88 shorter events, 9.3 us)
Async XLA Ops:
  0.0 179.7 %copy-start = (bf16[512,1024]{1,0:T(8,128)(2,1)S(1)}, bf16[512,1024]{1,0:T(8,128)(2,1)}, u32[]{:S(2)}) copy-start(bf16[512,1024]{1,0:T(8,128)(2,1)} %param.13) | copy-start | bytes 3145732
  2.7 23.3 %copy-start.9 = (bf16[1024]{0:T(1024)(128)(2,1)S(1)}, bf16[1024]{0:T(1024)(128)(2,1)}, u32[]{:S(2)}) copy-start(bf16[1024]{0:T(1024)(128)(2,1)} %param.9) | copy-start | bytes 6148
  5.1 39.0 %all-to-all-start = ((bf16[128,2,1,1024]{3,1,2,0:T(2,128)(2,1)}), bf16[128,2,1,1024]{3,1,2,0:T(2,128)(2,1)S(1)}, u32[]{:S(2)}, u32[]{:S(2)}) async-start(bf16[128,2,1,1024]{3,1,2,0:T(2,128)(2,1)} %copy.59), calls=%async_computation | async-start | bytes 1048576 | tf_op jit(solution)/shard_map/all_to_all | solution.py:86
  44.1 5.2 %copy-start.1 = (bf16[512,1024]{1,0:T(8,128)(2,1)S(1)}, bf16[512,1024]{1,0:T(8,128)(2,1)}, u32[]{:S(2)}) copy-start(bf16[512,1024]{1,0:T(8,128)(2,1)} %param.8) | copy-start | bytes 3145732
  44.1 5.2 %copy-start.11 = (bf16[1024,128]{1,0:T(8,128)(2,1)S(1)}, bf16[1024,128]{1,0:T(8,128)(2,1)}, u32[]{:S(2)}) copy-start(bf16[1024,128]{1,0:T(8,128)(2,1)} %param.12) | copy-start | bytes 786436
  44.1 5.2 %copy-start.12 = (bf16[1024,128]{1,0:T(8,128)(2,1)S(1)}, bf16[1024,128]{1,0:T(8,128)(2,1)}, u32[]{:S(2)}) copy-start(bf16[1024,128]{1,0:T(8,128)(2,1)} %param.11) | copy-start | bytes 786436
  44.1 19.9 %all-to-all-start.1 = ((bf16[4,1024,128]{2,1,0:T(8,128)(2,1)}), bf16[4,1024,128]{2,1,0:T(8,128)(2,1)}, u32[]{:S(2)}, u32[]{:S(2)}) async-start(bf16[4,1024,128]{2,1,0:T(8,128)(2,1)} %bitcast.60), calls=%async_computation.1 | async-start | bytes 2097152 | tf_op jit(solution)/shard_map/all_to_all | solution.py:95
  67.5 3.8 %copy-start.8 = (s32[2]{0:T(128)S(1)}, s32[2]{0:T(128)}, u32[]{:S(2)}) copy-start(s32[2]{0:T(128)} %param.15) | copy-start | bytes 28
  67.5 4.5 %copy-start.10 = (s32[4]{0:T(128)S(1)}, s32[4]{0:T(128)}, u32[]{:S(2)}) copy-start(s32[4]{0:T(128)} %param.14) | copy-start | bytes 52
  67.5 24.5 %all-to-all-start.2 = ((bf16[4,524,384]{2,1,0:T(8,128)(2,1)}), bf16[4,524,384]{2,1,0:T(8,128)(2,1)S(1)}, u32[]{:S(2)}, u32[]{:S(2)}) async-start(bf16[4,524,384]{2,1,0:T(8,128)(2,1)} %pad_maximum_fusion), calls=%async_computation.2 | async-start | bytes 3244032 | tf_op jit(solution)/shard_map/all_to_all | solution.py:127
  93.0 0.7 copy-start.6
  94.4 20.9 %all-to-all-start.3 = ((bf16[128,2,384]{2,1,0:T(2,128)(2,1)}), bf16[128,2,384]{2,1,0:T(2,128)(2,1)S(1)}, u32[]{:S(2)}, u32[]{:S(2)}) async-start(bf16[128,2,384]{2,1,0:T(2,128)(2,1)} %broadcast_in_dim.19), calls=%async_computation.3 | async-start | bytes 393216 | tf_op jit(solution)/shard_map/all_to_all | solution.py:54
  101.0 12.0 %collective-permute-start = (bf16[256,256]{1,0:T(8,128)(2,1)S(1)}, bf16[256,256]{1,0:T(8,128)(2,1)S(1)}, u32[]{:S(2)}, u32[]{:S(2)}) collective-permute-start(bf16[256,256]{1,0:T(8,128)(2,1)S(1)} %get-tuple-element.22), channel_id=1, source_target_pairs={{0,1},{1,2},{2,3},{3,4},{4,5},{5,6},{6,7},{7,8},{8,9},{9,10},{10,1... | collective-permute-start | bytes 393224 | tf_op jit(solution)/shard_map/ppermute | solution.py:22
  104.6 8.5 %collective-permute-start.1 = (bf16[256,256]{1,0:T(8,128)(2,1)S(1)}, bf16[256,256]{1,0:T(8,128)(2,1)S(1)}, u32[]{:S(2)}, u32[]{:S(2)}) collective-permute-start(bf16[256,256]{1,0:T(8,128)(2,1)S(1)} %get-tuple-element.23), channel_id=1, source_target_pairs={{1,0},{2,1},{3,2},{4,3},{5,4},{6,5},{7,6},{8,7},{9,8},{10,9},{11,1... | collective-permute-start | bytes 393224 | tf_op jit(solution)/shard_map/ppermute | solution.py:24
  115.4 0.9 copy-start.4
  115.4 15.6 %copy-start.7 = (bf16[514,128]{1,0:T(8,128)(2,1)S(1)}, bf16[514,128]{1,0:T(8,128)(2,1)}, u32[]{:S(2)}) copy-start(bf16[514,128]{1,0:T(8,128)(2,1)} %copy-done.6) | copy-start | bytes 394756
  117.3 29.0 %all-to-all-start.4 = ((f32[128,2,256]{2,1,0:T(2,128)}), f32[128,2,256]{2,1,0:T(2,128)S(1)}, u32[]{:S(2)}, u32[]{:S(2)}) async-start(f32[128,2,256]{2,1,0:T(2,128)} %reshape.135), calls=%async_computation.4 | async-start | bytes 524288 | tf_op jit(solution)/shard_map/all_to_all | solution.py:168
  131.1 2.1 %copy-start.3 = (bf16[1024,256]{1,0:T(8,128)(2,1)S(1)}, bf16[1024,256]{1,0:T(8,128)(2,1)}, u32[]{:S(2)}) copy-start(bf16[1024,256]{1,0:T(8,128)(2,1)} %pad_maximum_fusion.2) | copy-start | bytes 1572868
  131.1 2.8 %copy-start.5 = (bf16[256,384]{1,0:T(8,128)(2,1)S(1)}, bf16[256,384]{1,0:T(8,128)(2,1)}, u32[]{:S(2)}) copy-start(bf16[256,384]{1,0:T(8,128)(2,1)} %copy-done.4) | copy-start | bytes 589828
  134.2 0.8 copy-start.2
  134.2 21.9 %slice-start = ((bf16[256,384]{1,0:T(8,128)(2,1)}), bf16[256,128]{1,0:T(8,128)(2,1)S(1)}, s32[]{:S(2)}) async-start(bf16[256,384]{1,0:T(8,128)(2,1)} %copy-done.4), calls=%async_computation.6 | async-start | bytes 131072 | tf_op jit(solution)/shard_map/slice | solution.py:149
  150.6 17.0 %all-to-all-start.5 = ((bf16[128,2,128]{2,1,0:T(2,128)(2,1)}), bf16[128,2,128]{2,1,0:T(2,128)(2,1)S(1)}, u32[]{:S(2)}, u32[]{:S(2)}) async-start(bf16[128,2,128]{2,1,0:T(2,128)(2,1)} %broadcast_in_dim.22), calls=%async_computation.5 | async-start | bytes 131072 | tf_op jit(solution)/shard_map/all_to_all | solution.py:54

commit v2 on v1

v2 whole, which is shorter than its diff:
```python
import math

import jax
import jax.numpy as jnp
from jax import lax
from jax.sharding import PartitionSpec as P

BLOCK = 128
REACH = 2

EPSILON = 1e-05
THETA = 500000.0


def shift(value, axis, by):
    count = lax.axis_size(axis)
    return lax.ppermute(value, axis, [(i, (i + by) % count) for i in range(count)])


def tables(positions, head_width):
    middle = head_width // 2
    frequency = jnp.exp(
        -(2.0 / head_width) * math.log(THETA) * jnp.arange(middle, dtype=jnp.float32)
    )
    angles = positions.astype(jnp.float32)[:, None] * frequency[None, :]
    cosine, sine = jnp.cos(angles), jnp.sin(angles)
    return jnp.concatenate([cosine, cosine], axis=1), jnp.concatenate([-sine, sine], axis=1)


def rotate(values, cosine, signed_sine):
    middle = values.shape[-1] // 2
    turned = jnp.concatenate([values[..., middle:], values[..., :middle]], axis=-1)
    return values * cosine + turned * signed_sine


def project(total, cosine, sine, head_width):
    bf16 = jnp.bfloat16
    queries = rotate(total[:, :head_width], cosine, sine).astype(bf16)
    keys = rotate(total[:, head_width : 2 * head_width], cosine, sine).astype(bf16)
    return queries, keys, total[:, 2 * head_width :].astype(bf16)


def on_device(
    hidden,
    norm_gain,
    query_weight,
    key_weight,
    value_weight,
    output_weight,
    block_reach,
    header_ids,
):
    bf16, f32 = jnp.bfloat16, jnp.float32
    rows, part = hidden.shape
    head_width = key_weight.shape[1]
    sections = lax.axis_size("section")
    shards = lax.axis_size("seq")
    local_blocks = rows // BLOCK
    total_blocks = local_blocks * shards
    section_place = lax.axis_index("section")
    seq_place = lax.axis_index("seq")
    headers = header_ids.shape[0]
    lines = BLOCK // shards
    mine = headers * lines
    owners = header_ids // local_blocks
    slots = header_ids % local_blocks
    width = part * sections
    gain = norm_gain.astype(f32)[None, :]

    candidates = jnp.concatenate(
        [
            lax.dynamic_slice_in_dim(hidden, slots[h] * BLOCK, BLOCK, axis=0).reshape(
                shards, lines, part
            )
            for h in range(headers)
        ],
        axis=1,
    )
    spread = lax.all_to_all(candidates, "seq", 0, 0)

    head_weights = []
    for k in range(sections):
        target = (section_place + k) % sections
        piece = lax.dynamic_slice_in_dim(query_weight, target * part, part, axis=0)
        head_weights.append(shift(piece, "section", k) if k else piece)

    floats = hidden.astype(f32)
    squares = lax.psum(jnp.sum(floats * floats, axis=1), "section")
    scaling = lax.rsqrt(squares / width + EPSILON)
    normed = (floats * scaling[:, None] * gain).astype(bf16)
    keyval_weight = jnp.concatenate([key_weight, value_weight], axis=1)

    header_rows = jnp.concatenate(
        [
            lax.dynamic_slice_in_dim(spread, owners[h], 1, axis=0)[
                0, h * lines : (h + 1) * lines
            ]
            for h in range(headers)
        ]
    ).astype(f32)
    gained = header_rows * gain
    gained_high = gained.astype(bf16)
    gained_low = (gained - gained_high.astype(f32)).astype(bf16)
    gained = jnp.concatenate([gained_high, gained_low])
    both = [
        jnp.dot(gained, weight, preferred_element_type=f32)
        for weight in head_weights + [keyval_weight]
    ]
    both = [value[:mine] + value[mine:] for value in both]
    header_squares = jnp.broadcast_to(
        jnp.sum(header_rows * header_rows, axis=1, keepdims=True), (mine, head_width)
    )
    chunks = []
    for target in range(sections):
        which = (section_place - target) % sections
        query_part = sum(jnp.where(which == k, both[k], 0.0) for k in range(sections))
        chunks.append(jnp.concatenate([query_part, both[sections], header_squares], axis=1))
    header_arrived = jnp.sum(lax.all_to_all(jnp.stack(chunks), "section", 0, 0), axis=0)
    header_scaling = lax.rsqrt(header_arrived[:, 3 * head_width :] / width + EPSILON)
    header_total = header_arrived[:, : 3 * head_width] * jnp.concatenate(
        [header_scaling] * 3, axis=1
    )
    header_positions = (
        header_ids[:, None] * BLOCK + seq_place * lines + jnp.arange(lines, dtype=jnp.int32)[None]
    ).reshape(-1)
    header_tables = tables(header_positions, head_width)
    header_chunk = jnp.concatenate(
        project(header_total, *header_tables, head_width), axis=1
    )
    keyval = jnp.dot(normed, keyval_weight, preferred_element_type=f32)
    total = jnp.concatenate(
        [jnp.dot(normed, head_weights[0], preferred_element_type=f32), keyval], axis=1
    )
    sends = [
        jnp.concatenate(
            [jnp.dot(normed, head_weights[k], preferred_element_type=f32), keyval], axis=1
        ).astype(bf16)
        for k in range(1, sections)
    ]
    header_chunk, *sends = lax.optimization_barrier((header_chunk, *sends))
    header_pack = lax.all_to_all(
        jnp.broadcast_to(header_chunk[None], (shards,) + header_chunk.shape), "seq", 0, 0
    ).reshape(-1, 3 * head_width)
    arrivals = [shift(sends[k - 1], "section", -k) for k in range(1, sections)]
    header_pack, *arrivals = lax.optimization_barrier((header_pack, *arrivals))
    for arrival in arrivals:
        total = total + arrival.astype(f32)
    own_positions = seq_place * rows + jnp.arange(rows, dtype=jnp.int32)
    queries, keys, values = project(total, *tables(own_positions, head_width), head_width)

    head_queries = header_pack[:, :head_width]
    head_keys = header_pack[:, head_width : 2 * head_width]
    head_values = header_pack[:, 2 * head_width :]

    inverse_root = 1.0 / math.sqrt(head_width)
    far_scores = (
        jnp.einsum("qd,kd->qk", head_queries, keys, preferred_element_type=f32) * inverse_root
    )
    far_max = jnp.max(far_scores, axis=1, keepdims=True)
    far_weights = jnp.exp(far_scores - far_max)
    far_total = jnp.sum(far_weights, axis=1, keepdims=True)
    far_out = jnp.dot(far_weights.astype(bf16), values, preferred_element_type=f32) / far_total
    far_level = far_max + jnp.log(far_total)
    first = far_level.astype(bf16).astype(f32)
    second = (far_level - first).astype(bf16).astype(f32)
    third = far_level - first - second
    lane = lax.broadcasted_iota(jnp.int32, far_out.shape, 1)
    level = jnp.where(lane < 32, first, jnp.where(lane < 64, second, third))
    partial = jnp.concatenate(
        [
            far_out.astype(bf16).reshape(shards, mine, head_width),
            level.astype(bf16).reshape(shards, mine, head_width),
        ],
        axis=1,
    )
    stacked = jnp.concatenate([keys, values], axis=1)
    partial, queries, stacked = lax.optimization_barrier((partial, queries, stacked))
    parts = lax.all_to_all(partial, "seq", 0, 0).astype(f32)
    levels = parts[:, mine:, 0:1] + parts[:, mine:, 32:33] + parts[:, mine:, 64:65]
    factor = jnp.exp(levels - jnp.max(levels, axis=0, keepdims=True))
    header_result = jnp.sum(parts[:, :mine] * factor, axis=0) / jnp.sum(factor, axis=0)
    everywhere = sections * shards
    header_all = lax.all_to_all(
        jnp.broadcast_to(
            header_result.astype(bf16)[None], (everywhere, mine, head_width)
        ),
        ("section", "seq"),
        0,
        0,
    ).reshape(sections, shards, headers, lines, head_width)

    margin_rows = REACH * BLOCK
    extended = jnp.concatenate(
        [
            shift(stacked[rows - margin_rows :], "seq", 1),
            stacked,
            shift(stacked[:margin_rows], "seq", -1),
        ]
    )
    near_keys = extended[:, :head_width]
    near_values = extended[:, head_width:]
    extent = rows + 2 * margin_rows
    key_blocks = seq_place * local_blocks - REACH + jnp.arange(extent, dtype=jnp.int32) // BLOCK
    query_blocks = seq_place * local_blocks + jnp.arange(rows, dtype=jnp.int32) // BLOCK
    limits = jnp.repeat(block_reach, BLOCK)
    key_header = jnp.any(header_ids[:, None] == key_blocks[None, :], axis=0)
    allowed = (key_blocks >= 0)[None, :] & (key_blocks < total_blocks)[None, :]
    allowed = allowed & (jnp.abs(key_blocks[None, :] - query_blocks[:, None]) <= limits[:, None])
    allowed = allowed & jnp.logical_not(key_header)[None, :]
    near_scores = (
        jnp.einsum("qd,kd->qk", queries, near_keys, preferred_element_type=f32) * inverse_root
    )
    near_scores = jnp.where(allowed, near_scores, -jnp.inf)
    head_scores = (
        jnp.einsum("qd,kd->qk", queries, head_keys, preferred_element_type=f32) * inverse_root
    )
    scores = jnp.concatenate([near_scores, head_scores], axis=1)
    row_top = jnp.max(scores, axis=1)
    weights = jnp.exp(scores - row_top[:, None])
    row_sums = jnp.sum(weights, axis=1)
    joined = jnp.concatenate([near_values, head_values], axis=0)
    mixed = (
        jnp.dot(weights.astype(bf16), joined, preferred_element_type=f32) / row_sums[:, None]
    ).astype(bf16)
    result = None
    for k in range(sections):
        piece = shift(mixed, "section", k) if k else mixed
        source = (section_place - k) % sections
        matrix = lax.dynamic_slice_in_dim(output_weight, source * head_width, head_width, axis=0)
        product = jnp.dot(piece, matrix, preferred_element_type=f32)
        result = product if result is None else result + product
    result = result.astype(bf16)

    for h in range(headers):
        attended = jnp.concatenate(
            [header_all[s, :, h].reshape(BLOCK, head_width) for s in range(sections)], axis=1
        )
        block = jnp.dot(attended, output_weight, preferred_element_type=f32).astype(bf16)
        place = slots[h] * BLOCK
        present = lax.dynamic_slice_in_dim(result, place, BLOCK, axis=0)
        block = jnp.where(owners[h] == seq_place, block, present)
        result = lax.dynamic_update_slice_in_dim(result, block, place, axis=0)
    return result


def solution(mesh):
    return jax.shard_map(
        on_device,
        mesh=mesh,
        in_specs=(
            P("seq", "section"),
            P("section"),
            P(None, "section"),
            P("section", None),
            P("section", None),
            P(None, "section"),
            P("seq"),
            P(),
        ),
        out_specs=P("seq", "section"),
        check_vma=False,
    )
```

time: 183 us -> 202 us (1.10)
  starting transfers between devices: 57.7 us -> 104 us
  waiting for transfers between devices: 71.9 us -> 27.8 us
  matrix products: 8.76 us -> 28.3 us
  between operations: 10.7 us -> 6.85 us
  other arithmetic: 8.73 us -> 12.3 us
    all_to_all x6 -> x5, waiting for transfers between devices: 71.9 us -> 15.9 us  [the longest x1 11.8 us: on_device(): lax.all_to_all(jnp.broadcast_to(header_result.astype(bf16)[None], (everyw...]
    ppermute x2 -> x11, starting transfers between devices: 5.47 us -> 33.5 us  [shift(): lax.ppermute(value, axis, [(i, (i + by) % count) for i in range(count)])]
    dot_general x3 -> x16, matrix products: 4.09 us -> 25 us  [the longest x3 6.53 us: on_device(): jnp.dot(normed, head_weights[k], preferred_element_type=f32)]
    all_to_all x6 -> x5, starting transfers between devices: 52.2 us -> 70.3 us  [the longest x1 19 us: on_device(): spread = lax.all_to_all(candidates, 'seq', 0, 0)]
    all_gather x1 -> x0, blocking collectives: 12 us -> none  [on_device(): gathered = lax.all_gather(attended, 'section', axis=1, tiled=True)]
    ppermute x2 -> x11, waiting for transfers between devices: 0.01 us -> 11.9 us  [shift(): lax.ppermute(value, axis, [(i, (i + by) % count) for i in range(count)])]
    psum x0 -> x1, blocking collectives: none -> 11.4 us  [on_device(): squares = lax.psum(jnp.sum(floats * floats, axis=1), 'section')]
    unnamed x29 -> x39, local copies, waits for them, and re-layouts: 3.48 us -> 0.16 us
  transfers between devices with their start and end apart: 8 -> 16, of which waited for: 6 -> 5; matrix products, arithmetic and copies ran while one was open for 6% -> 16% of each run, Pallas kernels for 0% -> 0%
where the time goes in v2:
time: 202 us; the launch traced here: 201 us
  starting transfers between devices  104 us (51%)
  matrix products  28.3 us (14%)
  waiting for transfers between devices  27.8 us (14%)
  other arithmetic  12.3 us (6%)
  blocking collectives  11.4 us (6%)
  local copies, waits for them, and re-layouts  10.2 us (5%)
  between operations  6.85 us (3%)
    ppermute x11, starting transfers between devices, shift(): lax.ppermute(value, axis, [(i, (i + by) % count) for i in range(count)])  33.5 us
    all_to_all x1, starting transfers between devices, on_device(): spread = lax.all_to_all(candidates, 'seq', 0, 0)  19 us
    all_to_all x1, starting transfers between devices, on_device(): lax.all_to_all(jnp.broadcast_to(header_chunk[None], (shards,) + header_ch...  16.2 us
    all_to_all x1, starting transfers between devices, on_device(): lax.all_to_all(jnp.broadcast_to(header_result.astype(bf16)[None], (everyw...  16.1 us
    all_to_all x1, starting transfers between devices, on_device(): parts = lax.all_to_all(partial, 'seq', 0, 0).astype(f32)  15.2 us
    ppermute x11, waiting for transfers between devices, shift(): lax.ppermute(value, axis, [(i, (i + by) % count) for i in range(count)])  11.9 us
    all_to_all x1, waiting for transfers between devices, on_device(): lax.all_to_all(jnp.broadcast_to(header_result.astype(bf16)[None], (everyw...  11.8 us
    psum x1, blocking collectives, on_device(): squares = lax.psum(jnp.sum(floats * floats, axis=1), 'section')  11.4 us
  transfers between devices with their start and end apart: 16, of which 5 were waited for; matrix products, arithmetic and copies ran while one was open for 16% of the time, Pallas kernels for 0%

profile of v2, /device:TPU:1, one launch (start us, length us, event | category | flops | bytes accessed | tf_op | source)
XLA Modules:
  0.0 200.6 jit_solution(3881626402151819669)
XLA Ops:
  5.2 19.0 %all-to-all-start = ((bf16[128,2,1024]{2,1,0:T(2,128)(2,1)}), bf16[128,2,1024]{2,1,0:T(2,128)(2,1)}, u32[]{:S(2)}, u32[]{:S(2)}) async-start(bf16[128,2,1024]{2,1,0:T(2,128)(2,1)} %copy.93), calls=%async_computation | async-start | bytes 1048576 | tf_op jit(solution)/shard_map/all_to_all | solution.py:79
  25.2 3.1 %collective-permute-start = (bf16[1024,128]{1,0:T(8,128)(2,1)}, bf16[1024,128]{1,0:T(8,128)(2,1)}, u32[]{:S(2)}, u32[]{:S(2)}) collective-permute-start(bf16[1024,128]{1,0:T(8,128)(2,1)} %get-tuple-element.41), channel_id=1, source_target_pairs={{0,128},{128,256},{256,384},{384,0},{1,129},{129,257},{257,385},{3... | collective-permute-start | bytes 786440 | tf_op jit(solution)/shard_map/ppermute | solution.py:17
  28.4 4.4 %collective-permute-start.1 = (bf16[1024,128]{1,0:T(8,128)(2,1)}, bf16[1024,128]{1,0:T(8,128)(2,1)}, u32[]{:S(2)}, u32[]{:S(2)}) collective-permute-start(bf16[1024,128]{1,0:T(8,128)(2,1)} %get-tuple-element.42), channel_id=1, source_target_pairs={{0,256},{128,384},{256,0},{384,128},{1,257},{129,385},{257,1},{385... | collective-permute-start | bytes 786440 | tf_op jit(solution)/shard_map/ppermute | solution.py:17
  32.7 3.1 %collective-permute-start.2 = (bf16[1024,128]{1,0:T(8,128)(2,1)}, bf16[1024,128]{1,0:T(8,128)(2,1)}, u32[]{:S(2)}, u32[]{:S(2)}) collective-permute-start(bf16[1024,128]{1,0:T(8,128)(2,1)} %get-tuple-element.40), channel_id=1, source_target_pairs={{0,384},{128,0},{256,128},{384,256},{1,385},{129,1},{257,129},{385... | collective-permute-start | bytes 786440 | tf_op jit(solution)/shard_map/ppermute | solution.py:17
  36.2 11.4 %psum.7 = f32[512]{0:T(512)S(1)} all-reduce(f32[512]{0:T(512)S(1)} %fusion.1), channel_id=1, replica_groups=mesh['section'=4,'seq'=128] {'section'}, use_global_device_ids=true, to_apply=%region_4.5 | all-reduce | flops 512 | bytes 4096 | tf_op jit(solution)/shard_map/psum | solution.py:88
  57.3 2.2 %convolution_convert_fusion.2 = bf16[512,128]{0,1:T(8,128)(2,1)} fusion(bf16[1024,128]{1,0:T(8,128)(2,1)} %collective-permute-done.2, bf16[512,1024]{1,0:T(8,128)(2,1)S(1)} %copy-done.1, f32[1024]{0:T(1024)S(1)} %convert_element_type.145, f32[512]{0:T(512)} %copy-done.10), kind=kOutput, calls=%fused_computation.20 | convolution fusion | flops 136380416 | bytes 1447936 | tf_op jit(solution)/shard_map/dot_general | solution.py:136
  59.4 2.2 %convolution_convert_fusion.3 = bf16[512,128]{0,1:T(8,128)(2,1)} fusion(bf16[1024,128]{1,0:T(8,128)(2,1)} %collective-permute-done.1, bf16[512,1024]{1,0:T(8,128)(2,1)S(1)} %copy-done.1, f32[1024]{0:T(1024)S(1)} %convert_element_type.145, f32[512]{0:T(512)S(1)} %copy-done.11), kind=kOutput, calls=%fused_computation.21 | convolution fusion | flops 136380416 | bytes 1447936 | tf_op jit(solution)/shard_map/dot_general | solution.py:136
  61.6 2.2 %convolution_convert_fusion.4 = bf16[512,128]{0,1:T(8,128)(2,1)} fusion(bf16[1024,128]{1,0:T(8,128)(2,1)} %collective-permute-done, bf16[512,1024]{1,0:T(8,128)(2,1)S(1)} %copy-done.1, f32[1024]{0:T(1024)S(1)} %convert_element_type.145, f32[512]{0:T(512)S(1)} %copy-done.11), kind=kOutput, calls=%fused_computation.22 | convolution fusion | flops 136380416 | bytes 1447936 | tf_op jit(solution)/shard_map/dot_general | solution.py:136
  70.0 3.7 %all-to-all-start.1 = ((f32[4,2,512]{2,1,0:T(2,128)}), f32[4,2,512]{2,1,0:T(2,128)S(1)}, u32[]{:S(2)}, u32[]{:S(2)}) async-start(f32[4,2,512]{2,1,0:T(2,128)} %pad_maximum_fusion.8), calls=%async_computation.1 | async-start | bytes 32768 | tf_op jit(solution)/shard_map/all_to_all | solution.py:118
  73.8 2.2 %pad_maximum_fusion.1 = (bf16[512,384]{0,1:T(8,128)(2,1)}, bf16[512,384]{0,1:T(8,128)(2,1)}, bf16[512,384]{0,1:T(8,128)(2,1)}) fusion(bf16[512,256]{0,1:T(8,128)(2,1)} %get-tuple-element.94, bf16[512,128]{0,1:T(8,128)(2,1)} %convolution_convert_fusion.2, bf16[512,128]{0,1:T(8,128)(2,1)} %convolution_convert_fusion.3, ...), kind=kLoop, calls=%fused_computation.33 | loop fusion | flops 1966080 | bytes 1835008 | tf_op jit(solution)/shard_map/concatenate | solution.py:135
  76.0 2.0 %all-to-all-done.1 = f32[4,2,512]{2,1,0:T(2,128)S(1)} async-done(((f32[4,2,512]{2,1,0:T(2,128)}), f32[4,2,512]{2,1,0:T(2,128)S(1)}, u32[]{:S(2)}, u32[]{:S(2)}) %all-to-all-start.1) | async-done | bytes 16416 | tf_op jit(solution)/shard_map/all_to_all | solution.py:118
  79.7 16.2 %all-to-all-start.2 = ((bf16[128,2,384]{2,1,0:T(2,128)(2,1)}), bf16[128,2,384]{2,1,0:T(2,128)(2,1)S(1)}, u32[]{:S(2)}, u32[]{:S(2)}) async-start(bf16[128,2,384]{2,1,0:T(2,128)(2,1)} %broadcast_in_dim.90), calls=%async_computation.2 | async-start | bytes 393216 | tf_op jit(solution)/shard_map/all_to_all | solution.py:141
  95.9 2.8 %collective-permute-start.3 = (bf16[512,384]{0,1:T(8,128)(2,1)}, bf16[512,384]{0,1:T(8,128)(2,1)}, u32[]{:S(2)}, u32[]{:S(2)}) collective-permute-start(bf16[512,384]{0,1:T(8,128)(2,1)} %get-tuple-element.17), channel_id=1, source_target_pairs={{0,384},{128,0},{256,128},{384,256},{1,385},{129,1},{257,129},{385... | collective-permute-start | bytes 1179656 | tf_op jit(solution)/shard_map/ppermute | solution.py:17
  98.7 3.1 %collective-permute-start.4 = (bf16[512,384]{0,1:T(8,128)(2,1)}, bf16[512,384]{0,1:T(8,128)(2,1)}, u32[]{:S(2)}, u32[]{:S(2)}) collective-permute-start(bf16[512,384]{0,1:T(8,128)(2,1)} %get-tuple-element.18), channel_id=1, source_target_pairs={{0,256},{128,384},{256,0},{384,128},{1,257},{129,385},{257,1},{385... | collective-permute-start | bytes 1179656 | tf_op jit(solution)/shard_map/ppermute | solution.py:17
  101.8 1.9 collective-permute-start.5
  105.5 2.2 %fusion.41 = f32[512,128]{0,1:T(8,128)} fusion(bf16[4096,128]{1,0:T(8,128)(2,1)} %param.10, s32[]{:T(128)S(6)} %select_n.249, bf16[512,1024]{1,0:T(8,128)(2,1)S(1)} %copy-done.1, f32[1024]{0:T(1024)S(1)} %convert_element_type.145, f32[512]{0:T(512)S(1)} %copy-done.12), kind=kOutput, calls=%fused_computation.65 | convolution fusion | flops 136314880 | bytes 1579012 | tf_op jit(solution)/shard_map/dot_general | solution.py:132
  107.8 2.1 %all-to-all-done.2 = bf16[128,2,384]{2,1,0:T(2,128)(2,1)S(1)} async-done(((bf16[128,2,384]{2,1,0:T(2,128)(2,1)}), bf16[128,2,384]{2,1,0:T(2,128)(2,1)S(1)}, u32[]{:S(2)}, u32[]{:S(2)}) %all-to-all-start.2) | async-done | bytes 196640 | tf_op jit(solution)/shard_map/all_to_all | solution.py:141
  110.0 1.9 collective-permute-done.4
  111.9 10.0 %collective-permute-done.5 = bf16[512,384]{0,1:T(8,128)(2,1)} collective-permute-done((bf16[512,384]{0,1:T(8,128)(2,1)}, bf16[512,384]{0,1:T(8,128)(2,1)}, u32[]{:S(2)}, u32[]{:S(2)}) %collective-permute-start.5) | collective-permute-done | bytes 393248 | tf_op jit(solution)/shard_map/ppermute | solution.py:17
  121.9 1.5 fusion.18
  125.2 3.7 %collective-permute-start.6 = (bf16[256,256]{0,1:T(8,128)(2,1)S(1)}, bf16[256,256]{0,1:T(8,128)(2,1)S(1)}, u32[]{:S(2)}, u32[]{:S(2)}) collective-permute-start(bf16[256,256]{0,1:T(8,128)(2,1)S(1)} %get-tuple-element.60), channel_id=1, source_target_pairs={{0,1},{1,2},{2,3},{3,4},{4,5},{5,6},{6,7},{7,8},{8,9},{9,10},{10,1... | collective-permute-start | bytes 393224 | tf_op jit(solution)/shard_map/ppermute | solution.py:17
  128.9 1.9 collective-permute-start.7
  131.6 15.2 %all-to-all-start.3 = ((bf16[128,4,128]{2,1,0:T(4,128)(2,1)}), bf16[128,4,128]{2,1,0:T(4,128)(2,1)S(1)}, u32[]{:S(2)}, u32[]{:S(2)}) async-start(bf16[128,4,128]{2,1,0:T(4,128)(2,1)} %copy.99), calls=%async_computation.3 | async-start | bytes 262144 | tf_op jit(solution)/shard_map/all_to_all | solution.py:178
  150.5 3.1 %collective-permute-start.9 = (bf16[512,128]{1,0:T(8,128)(2,1)}, bf16[512,128]{1,0:T(8,128)(2,1)}, u32[]{:S(2)}, u32[]{:S(2)}) collective-permute-start(bf16[512,128]{1,0:T(8,128)(2,1)} %fusion.13), channel_id=1, source_target_pairs={{0,256},{128,384},{256,0},{384,128},{1,257},{129,385},{257,1},{385... | collective-permute-start | bytes 393224 | tf_op jit(solution)/shard_map/ppermute | solution.py:17
  153.5 1.9 collective-permute-start.8
  155.5 4.6 %collective-permute-start.10 = (bf16[512,128]{1,0:T(8,128)(2,1)}, bf16[512,128]{1,0:T(8,128)(2,1)}, u32[]{:S(2)}, u32[]{:S(2)}) collective-permute-start(bf16[512,128]{1,0:T(8,128)(2,1)} %fusion.13), channel_id=1, source_target_pairs={{0,384},{128,0},{256,128},{384,256},{1,385},{129,1},{257,129},{385... | collective-permute-start | bytes 393224 | tf_op jit(solution)/shard_map/ppermute | solution.py:17
  160.1 1.4 fusion.38
  163.6 16.1 %all-to-all-start.4 = ((bf16[512,2,128]{2,1,0:T(2,128)(2,1)}), bf16[512,2,128]{2,1,0:T(2,128)(2,1)S(1)}, u32[]{:S(2)}, u32[]{:S(2)}) async-start(bf16[512,2,128]{2,1,0:T(2,128)(2,1)} %broadcast_in_dim.95), calls=%async_computation.4 | async-start | bytes 524288 | tf_op jit(solution)/shard_map/all_to_all | solution.py:183
  182.4 2.4 %add_convert_fusion = bf16[512,1024]{1,0:T(8,128)(2,1)} fusion(f32[512,1024]{1,0:T(8,128)S(1)} %fusion.34, f32[512,1024]{1,0:T(8,128)S(1)} %fusion.38, f32[512,1024]{1,0:T(8,128)S(1)} %fusion.36, bf16[512,128]{1,0:T(8,128)(2,1)} %collective-permute-done.10, bf16[512,1024]{1,0:T(8,128)(2,1)S(1)} %copy-done, s32[]{:T(128)S(6)} %select_n.296), kind=kOutput, calls=%fused_computation.7 | convolution fusion | flops 136314880 | bytes 7733252 | tf_op jit(solution)/shard_map/dot_general | solution.py:230
  184.8 11.8 %all-to-all-done.4 = bf16[512,2,128]{2,1,0:T(2,128)(2,1)S(1)} async-done(((bf16[512,2,128]{2,1,0:T(2,128)(2,1)}), bf16[512,2,128]{2,1,0:T(2,128)(2,1)S(1)}, u32[]{:S(2)}, u32[]{:S(2)}) %all-to-all-start.4) | async-done | bytes 262176 | tf_op jit(solution)/shard_map/all_to_all | solution.py:183
  196.7 2.0 select_dynamic-update-slice_fusion.1
  198.7 2.0 select_dynamic-update-slice_fusion
  (134 shorter events, 30.6 us)
Async XLA Ops:
  0.0 160.1 %copy-start = (bf16[512,1024]{1,0:T(8,128)(2,1)S(1)}, bf16[512,1024]{1,0:T(8,128)(2,1)}, u32[]{:S(2)}) copy-start(bf16[512,1024]{1,0:T(8,128)(2,1)} %param.13) | copy-start | bytes 3145732
  2.6 21.7 %copy-start.2 = (bf16[4096,128]{1,0:T(8,128)(2,1)S(1)}, bf16[4096,128]{1,0:T(8,128)(2,1)}, u32[]{:S(2)}) copy-start(bf16[4096,128]{1,0:T(8,128)(2,1)} %param.10) | copy-start | bytes 3145732
  3.9 31.9 %copy-start.1 = (bf16[512,1024]{1,0:T(8,128)(2,1)S(1)}, bf16[512,1024]{1,0:T(8,128)(2,1)}, u32[]{:S(2)}) copy-start(bf16[512,1024]{1,0:T(8,128)(2,1)} %param.8) | copy-start | bytes 3145732
  5.2 30.9 %copy-start.4 = (bf16[1024,128]{1,0:T(8,128)(2,1)S(1)}, bf16[1024,128]{1,0:T(8,128)(2,1)}, u32[]{:S(2)}) copy-start(bf16[1024,128]{1,0:T(8,128)(2,1)} %param.11) | copy-start | bytes 786436
  5.2 30.9 %copy-start.8 = (bf16[1024]{0:T(1024)(128)(2,1)S(1)}, bf16[1024]{0:T(1024)(128)(2,1)}, u32[]{:S(2)}) copy-start(bf16[1024]{0:T(1024)(128)(2,1)} %param.9) | copy-start | bytes 6148
  5.2 42.4 %copy-start.13 = (s32[2]{0:T(128)S(1)}, s32[2]{0:T(128)}, u32[]{:S(2)}) copy-start(s32[2]{0:T(128)} %param.15) | copy-start | bytes 28
  5.2 43.0 %copy-start.16 = (s32[4]{0:T(128)S(1)}, s32[4]{0:T(128)}, u32[]{:S(2)}) copy-start(s32[4]{0:T(128)} %param.14) | copy-start | bytes 52
  5.2 58.6 %all-to-all-start = ((bf16[128,2,1024]{2,1,0:T(2,128)(2,1)}), bf16[128,2,1024]{2,1,0:T(2,128)(2,1)}, u32[]{:S(2)}, u32[]{:S(2)}) async-start(bf16[128,2,1024]{2,1,0:T(2,128)(2,1)} %copy.93), calls=%async_computation | async-start | bytes 1048576 | tf_op jit(solution)/shard_map/all_to_all | solution.py:79
  25.2 36.4 %collective-permute-start = (bf16[1024,128]{1,0:T(8,128)(2,1)}, bf16[1024,128]{1,0:T(8,128)(2,1)}, u32[]{:S(2)}, u32[]{:S(2)}) collective-permute-start(bf16[1024,128]{1,0:T(8,128)(2,1)} %get-tuple-element.41), channel_id=1, source_target_pairs={{0,128},{128,256},{256,384},{384,0},{1,129},{129,257},{257,385},{3... | collective-permute-start | bytes 786440 | tf_op jit(solution)/shard_map/ppermute | solution.py:17
  28.4 31.1 %collective-permute-start.1 = (bf16[1024,128]{1,0:T(8,128)(2,1)}, bf16[1024,128]{1,0:T(8,128)(2,1)}, u32[]{:S(2)}, u32[]{:S(2)}) collective-permute-start(bf16[1024,128]{1,0:T(8,128)(2,1)} %get-tuple-element.42), channel_id=1, source_target_pairs={{0,256},{128,384},{256,0},{384,128},{1,257},{129,385},{257,1},{385... | collective-permute-start | bytes 786440 | tf_op jit(solution)/shard_map/ppermute | solution.py:17
  32.7 24.5 %collective-permute-start.2 = (bf16[1024,128]{1,0:T(8,128)(2,1)}, bf16[1024,128]{1,0:T(8,128)(2,1)}, u32[]{:S(2)}, u32[]{:S(2)}) collective-permute-start(bf16[1024,128]{1,0:T(8,128)(2,1)} %get-tuple-element.40), channel_id=1, source_target_pairs={{0,384},{128,0},{256,128},{384,256},{1,385},{129,1},{257,129},{385... | collective-permute-start | bytes 786440 | tf_op jit(solution)/shard_map/ppermute | solution.py:17
  36.1 18.7 %copy-start.7 = (f32[64]{0:T(128)}, f32[64]{0:T(128)S(1)}, u32[]{:S(2)}) copy-start(f32[64]{0:T(128)S(1)} %multiply_exponential_fusion) | copy-start | bytes 772
  47.6 7.3 %copy-start.10 = (f32[512]{0:T(512)}, f32[512]{0:T(512)S(1)}, u32[]{:S(2)}) copy-start(f32[512]{0:T(512)S(1)} %add_rsqrt_fusion) | copy-start | bytes 6148
  56.0 3.4 %copy-start.11 = (f32[512]{0:T(512)S(1)}, f32[512]{0:T(512)}, u32[]{:S(2)}) copy-start(f32[512]{0:T(512)} %copy-done.10) | copy-start | bytes 6148
  63.8 14.3 %copy-start.5 = (f32[2,64]{1,0:T(2,128)S(1)}, f32[2,64]{1,0:T(2,128)}, u32[]{:S(2)}) copy-start(f32[2,64]{1,0:T(2,128)} %get-tuple-element.85) | copy-start | bytes 1540
  64.9 40.6 %copy-start.6 = (pred[1024]{0:T(1024)(128)(4,1)S(1)}, pred[1024]{0:T(1024)(128)(4,1)}, u32[]{:S(2)}) copy-start(pred[1024]{0:T(1024)(128)(4,1)} %compare_reduce_fusion) | copy-start | bytes 3076
  64.9 40.7 %copy-start.12 = (f32[512]{0:T(512)S(1)}, f32[512]{0:T(512)}, u32[]{:S(2)}) copy-start(f32[512]{0:T(512)} %copy-done.10) | copy-start | bytes 6148
  70.0 7.9 %all-to-all-start.1 = ((f32[4,2,512]{2,1,0:T(2,128)}), f32[4,2,512]{2,1,0:T(2,128)S(1)}, u32[]{:S(2)}, u32[]{:S(2)}) async-start(f32[4,2,512]{2,1,0:T(2,128)} %pad_maximum_fusion.8), calls=%async_computation.1 | async-start | bytes 32768 | tf_op jit(solution)/shard_map/all_to_all | solution.py:118
  79.7 30.2 %all-to-all-start.2 = ((bf16[128,2,384]{2,1,0:T(2,128)(2,1)}), bf16[128,2,384]{2,1,0:T(2,128)(2,1)S(1)}, u32[]{:S(2)}, u32[]{:S(2)}) async-start(bf16[128,2,384]{2,1,0:T(2,128)(2,1)} %broadcast_in_dim.90), calls=%async_computation.2 | async-start | bytes 393216 | tf_op jit(solution)/shard_map/all_to_all | solution.py:141
  95.9 14.1 %collective-permute-start.3 = (bf16[512,384]{0,1:T(8,128)(2,1)}, bf16[512,384]{0,1:T(8,128)(2,1)}, u32[]{:S(2)}, u32[]{:S(2)}) collective-permute-start(bf16[512,384]{0,1:T(8,128)(2,1)} %get-tuple-element.17), channel_id=1, source_target_pairs={{0,384},{128,0},{256,128},{384,256},{1,385},{129,1},{257,129},{385... | collective-permute-start | bytes 1179656 | tf_op jit(solution)/shard_map/ppermute | solution.py:17
  98.7 13.2 %collective-permute-start.4 = (bf16[512,384]{0,1:T(8,128)(2,1)}, bf16[512,384]{0,1:T(8,128)(2,1)}, u32[]{:S(2)}, u32[]{:S(2)}) collective-permute-start(bf16[512,384]{0,1:T(8,128)(2,1)} %get-tuple-element.18), channel_id=1, source_target_pairs={{0,256},{128,384},{256,0},{384,128},{1,257},{129,385},{257,1},{385... | collective-permute-start | bytes 1179656 | tf_op jit(solution)/shard_map/ppermute | solution.py:17
  101.8 20.1 %collective-permute-start.5 = (bf16[512,384]{0,1:T(8,128)(2,1)}, bf16[512,384]{0,1:T(8,128)(2,1)}, u32[]{:S(2)}, u32[]{:S(2)}) collective-permute-start(bf16[512,384]{0,1:T(8,128)(2,1)} %get-tuple-element.19), channel_id=1, source_target_pairs={{0,128},{128,256},{256,384},{384,0},{1,129},{129,257},{257,385},{3... | collective-permute-start | bytes 1179656 | tf_op jit(solution)/shard_map/ppermute | solution.py:17
  124.9 22.4 %copy-start.3 = (bf16[256,384]{0,1:T(8,128)(2,1)}, bf16[256,384]{0,1:T(8,128)(2,1)S(1)}, u32[]{:S(2)}) copy-start(bf16[256,384]{0,1:T(8,128)(2,1)S(1)} %copy.98) | copy-start | bytes 589828
  124.9 22.4 %copy-start.9 = (s32[512]{0:T(512)S(1)}, s32[512]{0:T(512)}, u32[]{:S(2)}) copy-start(s32[512]{0:T(512)} %broadcast_bitcast_fusion) | copy-start | bytes 6148
  124.9 22.4 %copy-start.17 = (pred[1024]{0:T(1024)(128)(4,1)S(1)}, pred[1024]{0:T(1024)(128)(4,1)}, u32[]{:S(2)}) copy-start(pred[1024]{0:T(1024)(128)(4,1)} %compare_and_fusion) | copy-start | bytes 3076
  125.2 21.9 %collective-permute-start.6 = (bf16[256,256]{0,1:T(8,128)(2,1)S(1)}, bf16[256,256]{0,1:T(8,128)(2,1)S(1)}, u32[]{:S(2)}, u32[]{:S(2)}) collective-permute-start(bf16[256,256]{0,1:T(8,128)(2,1)S(1)} %get-tuple-element.60), channel_id=1, source_target_pairs={{0,1},{1,2},{2,3},{3,4},{4,5},{5,6},{6,7},{7,8},{8,9},{9,10},{10,1... | collective-permute-start | bytes 393224 | tf_op jit(solution)/shard_map/ppermute | solution.py:17
  128.9 18.3 %collective-permute-start.7 = (bf16[256,256]{0,1:T(8,128)(2,1)S(1)}, bf16[256,256]{0,1:T(8,128)(2,1)S(1)}, u32[]{:S(2)}, u32[]{:S(2)}) collective-permute-start(bf16[256,256]{0,1:T(8,128)(2,1)S(1)} %get-tuple-element.59), channel_id=1, source_target_pairs={{0,127},{1,0},{2,1},{3,2},{4,3},{5,4},{6,5},{7,6},{8,7},{9,8},{10,... | collective-permute-start | bytes 393224 | tf_op jit(solution)/shard_map/ppermute | solution.py:17
  131.6 29.8 %all-to-all-start.3 = ((bf16[128,4,128]{2,1,0:T(4,128)(2,1)}), bf16[128,4,128]{2,1,0:T(4,128)(2,1)S(1)}, u32[]{:S(2)}, u32[]{:S(2)}) async-start(bf16[128,4,128]{2,1,0:T(4,128)(2,1)} %copy.99), calls=%async_computation.3 | async-start | bytes 262144 | tf_op jit(solution)/shard_map/all_to_all | solution.py:178
  150.5 29.3 %collective-permute-start.9 = (bf16[512,128]{1,0:T(8,128)(2,1)}, bf16[512,128]{1,0:T(8,128)(2,1)}, u32[]{:S(2)}, u32[]{:S(2)}) collective-permute-start(bf16[512,128]{1,0:T(8,128)(2,1)} %fusion.13), channel_id=1, source_target_pairs={{0,256},{128,384},{256,0},{384,128},{1,257},{129,385},{257,1},{385... | collective-permute-start | bytes 393224 | tf_op jit(solution)/shard_map/ppermute | solution.py:17
  153.5 27.6 %collective-permute-start.8 = (bf16[512,128]{1,0:T(8,128)(2,1)}, bf16[512,128]{1,0:T(8,128)(2,1)}, u32[]{:S(2)}, u32[]{:S(2)}) collective-permute-start(bf16[512,128]{1,0:T(8,128)(2,1)} %fusion.13), channel_id=1, source_target_pairs={{0,128},{128,256},{256,384},{384,0},{1,129},{129,257},{257,385},{3... | collective-permute-start | bytes 393224 | tf_op jit(solution)/shard_map/ppermute | solution.py:17
  155.5 27.0 %collective-permute-start.10 = (bf16[512,128]{1,0:T(8,128)(2,1)}, bf16[512,128]{1,0:T(8,128)(2,1)}, u32[]{:S(2)}, u32[]{:S(2)}) collective-permute-start(bf16[512,128]{1,0:T(8,128)(2,1)} %fusion.13), channel_id=1, source_target_pairs={{0,384},{128,0},{256,128},{384,256},{1,385},{129,1},{257,129},{385... | collective-permute-start | bytes 393224 | tf_op jit(solution)/shard_map/ppermute | solution.py:17
  163.6 33.0 %all-to-all-start.4 = ((bf16[512,2,128]{2,1,0:T(2,128)(2,1)}), bf16[512,2,128]{2,1,0:T(2,128)(2,1)S(1)}, u32[]{:S(2)}, u32[]{:S(2)}) async-start(bf16[512,2,128]{2,1,0:T(2,128)(2,1)} %broadcast_in_dim.95), calls=%async_computation.4 | async-start | bytes 524288 | tf_op jit(solution)/shard_map/all_to_all | solution.py:183
  (3 other events, 3.6 us)

commit v3 on v2

--- a/solution.py
+++ b/solution.py
@@ -78,17 +78,24 @@
     )
     spread = lax.all_to_all(candidates, "seq", 0, 0)
 
+    floats = hidden.astype(f32)
+    squares = jnp.sum(floats * floats, axis=1).reshape(-1, head_width)
+    squares_high = squares.astype(bf16)
+    squares_low = (squares - squares_high.astype(f32)).astype(bf16)
+    square_rows = squares.shape[0]
     head_weights = []
     for k in range(sections):
         target = (section_place + k) % sections
         piece = lax.dynamic_slice_in_dim(query_weight, target * part, part, axis=0)
-        head_weights.append(shift(piece, "section", k) if k else piece)
-
-    floats = hidden.astype(f32)
-    squares = lax.psum(jnp.sum(floats * floats, axis=1), "section")
-    scaling = lax.rsqrt(squares / width + EPSILON)
+        if k:
+            piece = jnp.concatenate([piece, squares_high, squares_low])
+            piece = shift(piece, "section", k)
+            tail = piece[part:].astype(f32)
+            squares = squares + tail[:square_rows] + tail[square_rows:]
+            piece = piece[:part]
+        head_weights.append(piece)
+    scaling = lax.rsqrt(squares.reshape(-1) / width + EPSILON)
     normed = (floats * scaling[:, None] * gain).astype(bf16)
-    keyval_weight = jnp.concatenate([key_weight, value_weight], axis=1)
 
     header_rows = jnp.concatenate(
         [
@@ -101,53 +108,63 @@
     gained = header_rows * gain
     gained_high = gained.astype(bf16)
     gained_low = (gained - gained_high.astype(f32)).astype(bf16)
-    gained = jnp.concatenate([gained_high, gained_low])
-    both = [
-        jnp.dot(gained, weight, preferred_element_type=f32)
-        for weight in head_weights + [keyval_weight]
-    ]
-    both = [value[:mine] + value[mine:] for value in both]
+    left = jnp.concatenate([normed, gained_high, gained_low])
     header_squares = jnp.broadcast_to(
         jnp.sum(header_rows * header_rows, axis=1, keepdims=True), (mine, head_width)
     )
+    products = [
+        jnp.dot(left, weight, preferred_element_type=f32)
+        for weight in head_weights + [key_weight, value_weight]
+    ]
+    mains = [value[:rows].astype(bf16) for value in products]
+    smalls = [value[rows : rows + mine] + value[rows + mine :] for value in products]
+    highs = [value.astype(bf16) for value in smalls + [header_squares]]
+    lows = [
+        (value - high.astype(f32)).astype(bf16)
+        for value, high in zip(smalls + [header_squares], highs)
+    ]
+    used = 3 * rows + 8 * mine
+    filler = jnp.zeros((-used % BLOCK, head_width), bf16)
     chunks = []
     for target in range(sections):
         which = (section_place - target) % sections
-        query_part = sum(jnp.where(which == k, both[k], 0.0) for k in range(sections))
-        chunks.append(jnp.concatenate([query_part, both[sections], header_squares], axis=1))
-    header_arrived = jnp.sum(lax.all_to_all(jnp.stack(chunks), "section", 0, 0), axis=0)
-    header_scaling = lax.rsqrt(header_arrived[:, 3 * head_width :] / width + EPSILON)
-    header_total = header_arrived[:, : 3 * head_width] * jnp.concatenate(
-        [header_scaling] * 3, axis=1
-    )
+
+        def chosen(options):
+            value = options[0]
+            for k in range(1, sections):
+                value = jnp.where(which == k, options[k], value)
+            return value
+
+        chunks.append(
+            jnp.concatenate(
+                [chosen(mains), mains[sections], mains[sections + 1]]
+                + [chosen(highs)]
+                + highs[sections:]
+                + [chosen(lows)]
+                + lows[sections:]
+                + [filler]
+            )
+        )
+    arrived = lax.all_to_all(jnp.stack(chunks), "section", 0, 0)
+    total = jnp.sum(arrived[:, :used].astype(f32), axis=0)
+    small = total[3 * rows :]
+    small = (small[: 4 * mine] + small[4 * mine :]).reshape(4, mine, head_width)
+    small = small[:3] * lax.rsqrt(small[3] / width + EPSILON)
+    total = jnp.concatenate([total[k * rows : (k + 1) * rows] for k in range(3)], axis=1)
+    header_total = jnp.concatenate([small[0], small[1], small[2]], axis=1)
+
     header_positions = (
         header_ids[:, None] * BLOCK + seq_place * lines + jnp.arange(lines, dtype=jnp.int32)[None]
     ).reshape(-1)
-    header_tables = tables(header_positions, head_width)
     header_chunk = jnp.concatenate(
-        project(header_total, *header_tables, head_width), axis=1
-    )
-    keyval = jnp.dot(normed, keyval_weight, preferred_element_type=f32)
-    total = jnp.concatenate(
-        [jnp.dot(normed, head_weights[0], preferred_element_type=f32), keyval], axis=1
-    )
-    sends = [
-        jnp.concatenate(
-            [jnp.dot(normed, head_weights[k], preferred_element_type=f32), keyval], axis=1
-        ).astype(bf16)
-        for k in range(1, sections)
-    ]
-    header_chunk, *sends = lax.optimization_barrier((header_chunk, *sends))
+        project(header_total, *tables(header_positions, head_width), head_width), axis=1
+    )
     header_pack = lax.all_to_all(
         jnp.broadcast_to(header_chunk[None], (shards,) + header_chunk.shape), "seq", 0, 0
     ).reshape(-1, 3 * head_width)
-    arrivals = [shift(sends[k - 1], "section", -k) for k in range(1, sections)]
-    header_pack, *arrivals = lax.optimization_barrier((header_pack, *arrivals))
-    for arrival in arrivals:
-        total = total + arrival.astype(f32)
     own_positions = seq_place * rows + jnp.arange(rows, dtype=jnp.int32)
     queries, keys, values = project(total, *tables(own_positions, head_width), head_width)
-
+    stacked = jnp.concatenate([keys, values], axis=1)
     head_queries = header_pack[:, :head_width]
     head_keys = header_pack[:, head_width : 2 * head_width]
     head_values = header_pack[:, 2 * head_width :]
@@ -166,28 +183,19 @@
     third = far_level - first - second
     lane = lax.broadcasted_iota(jnp.int32, far_out.shape, 1)
     level = jnp.where(lane < 32, first, jnp.where(lane < 64, second, third))
-    partial = jnp.concatenate(
-        [
-            far_out.astype(bf16).reshape(shards, mine, head_width),
-            level.astype(bf16).reshape(shards, mine, head_width),
-        ],
-        axis=1,
-    )
-    stacked = jnp.concatenate([keys, values], axis=1)
-    partial, queries, stacked = lax.optimization_barrier((partial, queries, stacked))
-    parts = lax.all_to_all(partial, "seq", 0, 0).astype(f32)
-    levels = parts[:, mine:, 0:1] + parts[:, mine:, 32:33] + parts[:, mine:, 64:65]
+    partial = jnp.concatenate([far_out, level], axis=1).astype(bf16)
+    partial, queries = lax.optimization_barrier((partial, queries))
+    parts = lax.all_to_all(partial.reshape(shards, mine, 2 * head_width), "seq", 0, 0)
+    parts = parts.astype(f32)
+    levels = sum(parts[..., head_width + lane : head_width + lane + 1] for lane in (0, 32, 64))
     factor = jnp.exp(levels - jnp.max(levels, axis=0, keepdims=True))
-    header_result = jnp.sum(parts[:, :mine] * factor, axis=0) / jnp.sum(factor, axis=0)
-    everywhere = sections * shards
+    header_result = jnp.sum(parts[..., :head_width] * factor, axis=0) / jnp.sum(factor, axis=0)
     header_all = lax.all_to_all(
-        jnp.broadcast_to(
-            header_result.astype(bf16)[None], (everywhere, mine, head_width)
-        ),
-        ("section", "seq"),
+        jnp.broadcast_to(header_result.astype(bf16)[None], (shards, mine, head_width)),
+        "seq",
         0,
         0,
-    ).reshape(sections, shards, headers, lines, head_width)
+    ).reshape(shards, headers, lines, head_width)
 
     margin_rows = REACH * BLOCK
     extended = jnp.concatenate(
@@ -222,25 +230,17 @@
     mixed = (
         jnp.dot(weights.astype(bf16), joined, preferred_element_type=f32) / row_sums[:, None]
     ).astype(bf16)
-    result = None
-    for k in range(sections):
-        piece = shift(mixed, "section", k) if k else mixed
-        source = (section_place - k) % sections
-        matrix = lax.dynamic_slice_in_dim(output_weight, source * head_width, head_width, axis=0)
-        product = jnp.dot(piece, matrix, preferred_element_type=f32)
-        result = product if result is None else result + product
-    result = result.astype(bf16)
-
-    for h in range(headers):
-        attended = jnp.concatenate(
-            [header_all[s, :, h].reshape(BLOCK, head_width) for s in range(sections)], axis=1
-        )
-        block = jnp.dot(attended, output_weight, preferred_element_type=f32).astype(bf16)
-        place = slots[h] * BLOCK
-        present = lax.dynamic_slice_in_dim(result, place, BLOCK, axis=0)
-        block = jnp.where(owners[h] == seq_place, block, present)
-        result = lax.dynamic_update_slice_in_dim(result, block, place, axis=0)
-    return result
+
+    blocks = []
+    for b in range(local_blocks):
+        block = mixed[b * BLOCK : (b + 1) * BLOCK]
+        for h in range(headers):
+            here = header_ids[h] == seq_place * local_blocks + b
+            block = jnp.where(here, header_all[:, h].reshape(BLOCK, head_width), block)
+        blocks.append(block)
+    attended = jnp.concatenate(blocks, axis=0)
+    gathered = lax.all_gather(attended, "section", axis=1, tiled=True)
+    return jnp.dot(gathered, output_weight, preferred_element_type=f32).astype(bf16)
 
 
 def solution(mesh):

time: 202 us -> 180 us (0.89)
  starting transfers between devices: 104 us -> 64.7 us
  waiting for transfers between devices: 27.8 us -> 47.5 us
  matrix products: 28.3 us -> 12.9 us
  other arithmetic: 12.3 us -> 17.1 us
  local copies, waits for them, and re-layouts: 10.2 us -> 14.5 us
  between operations: 6.85 us -> 10.1 us
    all_to_all x3, waiting for transfers between devices: 13.8 us -> 35.8 us  [the longest x1 17.3 us: on_device(): arrived = lax.all_to_all(jnp.stack(chunks), 'section', 0, 0)]
    ppermute x11 -> x5, starting transfers between devices: 33.5 us -> 15.9 us  [shift(): lax.ppermute(value, axis, [(i, (i + by) % count) for i in range(count)])]
    dot_general x16 -> x7, matrix products: 25 us -> 8.27 us  [the longest x6 6.59 us: on_device(): jnp.dot(left, weight, preferred_element_type=f32)]
    all_gather x0 -> x1, blocking collectives: none -> 12 us  [on_device(): gathered = lax.all_gather(attended, 'section', axis=1, tiled=True)]
    all_to_all x3, starting transfers between devices: 35.1 us -> 23.4 us  [the longest x1 14.1 us: on_device(): lax.all_to_all(partial.reshape(shards, mine, 2 * head_width), 'seq', 0, 0)]
    psum x1 -> x0, blocking collectives: 11.4 us -> none  [on_device(): squares = lax.psum(jnp.sum(floats * floats, axis=1), 'section')]
    all_to_all x1, starting transfers between devices: 16.2 us -> 6.82 us  [on_device(): lax.all_to_all(jnp.broadcast_to(header_chunk[None], (shards,) + header_ch...]
    ppermute x11 -> x5, waiting for transfers between devices: 11.9 us -> 2.63 us  [shift(): lax.ppermute(value, axis, [(i, (i + by) % count) for i in range(count)])]
  transfers between devices with their start and end apart: 16 -> 10, of which waited for: 5 -> 5; matrix products, arithmetic and copies ran while one was open for 16% -> 10% of each run, Pallas kernels for 0% -> 0%
where the time goes in v3:
time: 180 us; the launch traced here: 179 us
  starting transfers between devices  64.7 us (36%)
  waiting for transfers between devices  47.5 us (26%)
  other arithmetic  17.1 us (10%)
  local copies, waits for them, and re-layouts  14.5 us (8%)
  matrix products  12.9 us (7%)
  blocking collectives  12 us (7%)
  between operations  10.1 us (6%)
    all_to_all x1, starting transfers between devices, on_device(): spread = lax.all_to_all(candidates, 'seq', 0, 0)  18.6 us
    all_to_all x1, waiting for transfers between devices, on_device(): arrived = lax.all_to_all(jnp.stack(chunks), 'section', 0, 0)  17.3 us
    ppermute x5, starting transfers between devices, shift(): lax.ppermute(value, axis, [(i, (i + by) % count) for i in range(count)])  15.9 us
    all_to_all x1, starting transfers between devices, on_device(): lax.all_to_all(partial.reshape(shards, mine, 2 * head_width), 'seq', 0, 0)  14.1 us
    all_gather x1, blocking collectives, on_device(): gathered = lax.all_gather(attended, 'section', axis=1, tiled=True)  12 us
    all_to_all x1, waiting for transfers between devices, on_device(): lax.all_to_all(jnp.broadcast_to(header_result.astype(bf16)[None], (shards...  9.86 us
    all_to_all x1, waiting for transfers between devices, on_device(): spread = lax.all_to_all(candidates, 'seq', 0, 0)  8.98 us
    all_to_all x1, waiting for transfers between devices, on_device(): lax.all_to_all(partial.reshape(shards, mine, 2 * head_width), 'seq', 0, 0)  8.68 us
  transfers between devices with their start and end apart: 10, of which 5 were waited for; matrix products, arithmetic and copies ran while one was open for 10% of the time, Pallas kernels for 0%

profile of v3, /device:TPU:1, one launch (start us, length us, event | category | flops | bytes accessed | tf_op | source)
XLA Modules:
  0.0 178.7 jit_solution(14884136693440306708)
XLA Ops:
  0.1 1.6 fusion.1
  1.7 1.2 constant_dynamic-slice_fusion.2
  3.0 5.2 %collective-permute-start.2 = (bf16[1032,128]{1,0:T(8,128)(2,1)S(1)}, bf16[1032,128]{1,0:T(8,128)(2,1)}, u32[]{:S(2)}, u32[]{:S(2)}) collective-permute-start(bf16[1032,128]{1,0:T(8,128)(2,1)S(1)} %concatenate.78), channel_id=1, source_target_pairs={{0,384},{128,0},{256,128},{384,256},{1,385},{129,1},{257,129},{385... | collective-permute-start | bytes 792584 | tf_op jit(solution)/shard_map/ppermute | solution.py:17
  8.4 2.4 %collective-permute-start.1 = (bf16[1032,128]{1,0:T(8,128)(2,1)S(1)}, bf16[1032,128]{1,0:T(8,128)(2,1)}, u32[]{:S(2)}, u32[]{:S(2)}) collective-permute-start(bf16[1032,128]{1,0:T(8,128)(2,1)S(1)} %concatenate.77), channel_id=1, source_target_pairs={{0,256},{128,384},{256,0},{384,128},{1,257},{129,385},{257,1},{385... | collective-permute-start | bytes 792584 | tf_op jit(solution)/shard_map/ppermute | solution.py:17
  13.3 1.3 copy.27
  14.6 18.6 %all-to-all-start = ((bf16[128,2,1024]{2,1,0:T(2,128)(2,1)}), bf16[128,2,1024]{2,1,0:T(2,128)(2,1)}, u32[]{:S(2)}, u32[]{:S(2)}) async-start(bf16[128,2,1024]{2,1,0:T(2,128)(2,1)} %copy.27), calls=%async_computation | async-start | bytes 1048576 | tf_op jit(solution)/shard_map/all_to_all | solution.py:79
  33.4 2.5 %collective-permute-start = (bf16[1032,128]{1,0:T(8,128)(2,1)S(1)}, bf16[1032,128]{1,0:T(8,128)(2,1)}, u32[]{:S(2)}, u32[]{:S(2)}) collective-permute-start(bf16[1032,128]{1,0:T(8,128)(2,1)S(1)} %concatenate.76), channel_id=1, source_target_pairs={{0,128},{128,256},{256,384},{384,0},{1,129},{129,257},{257,385},{3... | collective-permute-start | bytes 792584 | tf_op jit(solution)/shard_map/ppermute | solution.py:17
  40.8 2.6 %collective-permute-done = bf16[1032,128]{1,0:T(8,128)(2,1)} collective-permute-done((bf16[1032,128]{1,0:T(8,128)(2,1)S(1)}, bf16[1032,128]{1,0:T(8,128)(2,1)}, u32[]{:S(2)}, u32[]{:S(2)}) %collective-permute-start) | collective-permute-done | bytes 264224 | tf_op jit(solution)/shard_map/ppermute | solution.py:17
  44.5 9.0 %all-to-all-done = bf16[128,2,1024]{2,1,0:T(2,128)(2,1)} async-done(((bf16[128,2,1024]{2,1,0:T(2,128)(2,1)}), bf16[128,2,1024]{2,1,0:T(2,128)(2,1)}, u32[]{:S(2)}, u32[]{:S(2)}) %all-to-all-start) | async-done | bytes 524320 | tf_op jit(solution)/shard_map/all_to_all | solution.py:79
  54.3 1.4 fusion.35
  55.7 1.4 fusion.28
  57.1 1.4 fusion.30
  58.6 1.4 fusion.32
  62.4 1.4 pad_maximum_fusion
  63.9 3.9 %all-to-all-start.1 = ((bf16[4,1664,128]{2,1,0:T(8,128)(2,1)}), bf16[4,1664,128]{2,1,0:T(8,128)(2,1)S(1)}, u32[]{:S(2)}, u32[]{:S(2)}) async-start(bf16[4,1664,128]{2,1,0:T(8,128)(2,1)} %pad_maximum_fusion), calls=%async_computation.1 | async-start | bytes 3407872 | tf_op jit(solution)/shard_map/all_to_all | solution.py:148
  70.9 1.9 %fusion.39 = (f32[512,64]{1,0:T(8,128)}, f32[512,64]{1,0:T(8,128)}, f32[512,64]{1,0:T(8,128)}) fusion(f32[64]{0:T(128)S(1)} %multiply_exponential_fusion, f32[512]{0:T(512)S(1)} %add_convert_fusion), kind=kLoop, calls=%fused_computation.79 | loop fusion | flops 65536 | bytes 395520 | tf_op jit(solution)/shard_map/neg | solution.py:27
  72.8 17.3 %all-to-all-done.1 = bf16[4,1664,128]{2,1,0:T(8,128)(2,1)S(1)} async-done(((bf16[4,1664,128]{2,1,0:T(8,128)(2,1)}), bf16[4,1664,128]{2,1,0:T(8,128)(2,1)S(1)}, u32[]{:S(2)}, u32[]{:S(2)}) %all-to-all-start.1) | async-done | bytes 1703968 | tf_op jit(solution)/shard_map/all_to_all | solution.py:148
  93.2 6.8 %all-to-all-start.2 = ((bf16[128,2,384]{2,1,0:T(2,128)(2,1)}), bf16[128,2,384]{2,1,0:T(2,128)(2,1)}, u32[]{:S(2)}, u32[]{:S(2)}) async-start(bf16[128,2,384]{2,1,0:T(2,128)(2,1)} %broadcast_in_dim.42), calls=%async_computation.2 | async-start | bytes 393216 | tf_op jit(solution)/shard_map/all_to_all | solution.py:162
  100.0 1.4 fusion.25
  101.5 3.0 %collective-permute-start.4 = (bf16[256,256]{1,0:T(8,128)(2,1)S(1)}, bf16[256,256]{1,0:T(8,128)(2,1)S(1)}, u32[]{:S(2)}, u32[]{:S(2)}) collective-permute-start(bf16[256,256]{1,0:T(8,128)(2,1)S(1)} %get-tuple-element.52), channel_id=1, source_target_pairs={{0,127},{1,0},{2,1},{3,2},{4,3},{5,4},{6,5},{7,6},{8,7},{9,8},{10,... | collective-permute-start | bytes 393224 | tf_op jit(solution)/shard_map/ppermute | solution.py:17
  104.5 2.8 %collective-permute-start.3 = (bf16[256,256]{1,0:T(8,128)(2,1)S(1)}, bf16[256,256]{1,0:T(8,128)(2,1)S(1)}, u32[]{:S(2)}, u32[]{:S(2)}) collective-permute-start(bf16[256,256]{1,0:T(8,128)(2,1)S(1)} %get-tuple-element.51), channel_id=1, source_target_pairs={{0,1},{1,2},{2,3},{3,4},{4,5},{5,6},{6,7},{7,8},{8,9},{9,10},{10,1... | collective-permute-start | bytes 393224 | tf_op jit(solution)/shard_map/ppermute | solution.py:17
  114.2 1.0 reshape.162
  117.0 14.1 %all-to-all-start.3 = ((bf16[128,2,256]{2,1,0:T(2,128)(2,1)}), bf16[128,2,256]{2,1,0:T(2,128)(2,1)}, u32[]{:S(2)}, u32[]{:S(2)}) async-start(bf16[128,2,256]{2,1,0:T(2,128)(2,1)} %reshape.163), calls=%async_computation.3 | async-start | bytes 262144 | tf_op jit(solution)/shard_map/all_to_all | solution.py:188
  131.1 2.0 %fusion.102 = (f32[512]{0:T(512)S(1)}, f32[512,1024]{1,0:T(8,128)S(1)}) fusion(bf16[512,128]{1,0:T(8,128)(2,1)S(1)} %get-tuple-element.8, bf16[1024,256]{1,0:T(8,128)(2,1)} %copy-done.3, pred[1024]{0:T(1024)(128)(4,1)S(1)} %not.7, s32[512]{0:T(512)S(1)} %copy-done.11, s32[512]{0:T(512)S(1)} %fusion.54, s32[1024]{0:T(1024)S(1)} %fusion.50, ...), kind=kOutput, calls=%fused_computation.232 | convolution fusion | flops 138411520 | bytes 2502656 | tf_op jit(solution)/shard_map/qd,kd->qk/dot_general | solution.py:219
  134.8 8.7 %all-to-all-done.3 = bf16[128,2,256]{2,1,0:T(2,128)(2,1)} async-done(((bf16[128,2,256]{2,1,0:T(2,128)(2,1)}), bf16[128,2,256]{2,1,0:T(2,128)(2,1)}, u32[]{:S(2)}, u32[]{:S(2)}) %all-to-all-start.3) | async-done | bytes 131104 | tf_op jit(solution)/shard_map/all_to_all | solution.py:188
  143.5 1.0 convert_element_type.263
  145.9 1.0 copy.29
  147.9 5.5 %all-to-all-start.4 = ((bf16[128,2,128]{2,1,0:T(2,128)(2,1)}), bf16[128,2,128]{2,1,0:T(2,128)(2,1)S(1)}, u32[]{:S(2)}, u32[]{:S(2)}) async-start(bf16[128,2,128]{2,1,0:T(2,128)(2,1)} %broadcast_in_dim.46), calls=%async_computation.4 | async-start | bytes 131072 | tf_op jit(solution)/shard_map/all_to_all | solution.py:193
  153.4 1.7 fusion.13
  155.1 9.9 %all-to-all-done.4 = bf16[128,2,128]{2,1,0:T(2,128)(2,1)S(1)} async-done(((bf16[128,2,128]{2,1,0:T(2,128)(2,1)}), bf16[128,2,128]{2,1,0:T(2,128)(2,1)S(1)}, u32[]{:S(2)}, u32[]{:S(2)}) %all-to-all-start.4) | async-done | bytes 65568 | tf_op jit(solution)/shard_map/all_to_all | solution.py:193
  165.1 12.0 %all_gather.3 = bf16[512,512]{1,0:T(8,128)(2,1)S(1)} all-gather(bf16[512,128]{1,0:T(8,128)(2,1)S(1)} %pad_maximum_fusion.8), channel_id=1, replica_groups=mesh['section'=4,'seq'=128] {'section'}, dimensions={1}, use_global_device_ids=true | all-gather | bytes 655360 | tf_op jit(solution)/shard_map/all_gather | solution.py:242
  177.0 1.7 convolution_convert_fusion
  (129 shorter events, 21.6 us)
Async XLA Ops:
  0.0 177.0 %copy-start = (bf16[512,1024]{1,0:T(8,128)(2,1)S(1)}, bf16[512,1024]{1,0:T(8,128)(2,1)}, u32[]{:S(2)}) copy-start(bf16[512,1024]{1,0:T(8,128)(2,1)} %param.13) | copy-start | bytes 3145732
  0.0 13.1 %copy-start.1 = (bf16[512,1024]{1,0:T(8,128)(2,1)S(1)}, bf16[512,1024]{1,0:T(8,128)(2,1)}, u32[]{:S(2)}) copy-start(bf16[512,1024]{1,0:T(8,128)(2,1)} %param.8) | copy-start | bytes 3145732
  0.0 10.8 %copy-start.9 = (s32[2]{0:T(128)S(1)}, s32[2]{0:T(128)}, u32[]{:S(2)}) copy-start(s32[2]{0:T(128)} %param.15) | copy-start | bytes 28
  3.0 36.4 %collective-permute-start.2 = (bf16[1032,128]{1,0:T(8,128)(2,1)S(1)}, bf16[1032,128]{1,0:T(8,128)(2,1)}, u32[]{:S(2)}, u32[]{:S(2)}) collective-permute-start(bf16[1032,128]{1,0:T(8,128)(2,1)S(1)} %concatenate.78), channel_id=1, source_target_pairs={{0,384},{128,0},{256,128},{384,256},{1,385},{129,1},{257,129},{385... | collective-permute-start | bytes 792584 | tf_op jit(solution)/shard_map/ppermute | solution.py:17
  8.4 31.8 %collective-permute-start.1 = (bf16[1032,128]{1,0:T(8,128)(2,1)S(1)}, bf16[1032,128]{1,0:T(8,128)(2,1)}, u32[]{:S(2)}, u32[]{:S(2)}) collective-permute-start(bf16[1032,128]{1,0:T(8,128)(2,1)S(1)} %concatenate.77), channel_id=1, source_target_pairs={{0,256},{128,384},{256,0},{384,128},{1,257},{129,385},{257,1},{385... | collective-permute-start | bytes 792584 | tf_op jit(solution)/shard_map/ppermute | solution.py:17
  13.2 25.1 %copy-start.10 = (bf16[1024]{0:T(1024)(128)(2,1)S(1)}, bf16[1024]{0:T(1024)(128)(2,1)}, u32[]{:S(2)}) copy-start(bf16[1024]{0:T(1024)(128)(2,1)} %param.9) | copy-start | bytes 6148
  14.6 38.8 %all-to-all-start = ((bf16[128,2,1024]{2,1,0:T(2,128)(2,1)}), bf16[128,2,1024]{2,1,0:T(2,128)(2,1)}, u32[]{:S(2)}, u32[]{:S(2)}) async-start(bf16[128,2,1024]{2,1,0:T(2,128)(2,1)} %copy.27), calls=%async_computation | async-start | bytes 1048576 | tf_op jit(solution)/shard_map/all_to_all | solution.py:79
  33.4 10.1 %collective-permute-start = (bf16[1032,128]{1,0:T(8,128)(2,1)S(1)}, bf16[1032,128]{1,0:T(8,128)(2,1)}, u32[]{:S(2)}, u32[]{:S(2)}) collective-permute-start(bf16[1032,128]{1,0:T(8,128)(2,1)S(1)} %concatenate.76), channel_id=1, source_target_pairs={{0,128},{128,256},{256,384},{384,0},{1,129},{129,257},{257,385},{3... | collective-permute-start | bytes 792584 | tf_op jit(solution)/shard_map/ppermute | solution.py:17
  58.5 1.6 copy-start.16
  60.1 1.0 copy-start.17
  63.9 5.7 %copy-start.15 = (s32[4]{0:T(128)S(1)}, s32[4]{0:T(128)}, u32[]{:S(2)}) copy-start(s32[4]{0:T(128)} %param.14) | copy-start | bytes 52
  63.9 6.4 %copy-start.12 = (f32[2]{0:T(128)S(1)}, f32[2]{0:T(128)}, u32[]{:S(2)}) copy-start(f32[2]{0:T(128)} %get-tuple-element.83) | copy-start | bytes 28
  63.9 26.2 %all-to-all-start.1 = ((bf16[4,1664,128]{2,1,0:T(8,128)(2,1)}), bf16[4,1664,128]{2,1,0:T(8,128)(2,1)S(1)}, u32[]{:S(2)}, u32[]{:S(2)}) async-start(bf16[4,1664,128]{2,1,0:T(8,128)(2,1)} %pad_maximum_fusion), calls=%async_computation.1 | async-start | bytes 3407872 | tf_op jit(solution)/shard_map/all_to_all | solution.py:148
  90.4 9.6 %copy-start.4 = (f32[512,64]{1,0:T(8,128)S(1)}, f32[512,64]{1,0:T(8,128)}, u32[]{:S(2)}) copy-start(f32[512,64]{1,0:T(8,128)} %get-tuple-element.62) | copy-start | bytes 393220
  90.4 9.6 %copy-start.5 = (f32[512,64]{1,0:T(8,128)S(1)}, f32[512,64]{1,0:T(8,128)}, u32[]{:S(2)}) copy-start(f32[512,64]{1,0:T(8,128)} %get-tuple-element.63) | copy-start | bytes 393220
  90.4 9.6 %copy-start.6 = (f32[512,64]{1,0:T(8,128)S(1)}, f32[512,64]{1,0:T(8,128)}, u32[]{:S(2)}) copy-start(f32[512,64]{1,0:T(8,128)} %get-tuple-element.64) | copy-start | bytes 393220
  93.2 21.0 %all-to-all-start.2 = ((bf16[128,2,384]{2,1,0:T(2,128)(2,1)}), bf16[128,2,384]{2,1,0:T(2,128)(2,1)}, u32[]{:S(2)}, u32[]{:S(2)}) async-start(bf16[128,2,384]{2,1,0:T(2,128)(2,1)} %broadcast_in_dim.42), calls=%async_computation.2 | async-start | bytes 393216 | tf_op jit(solution)/shard_map/all_to_all | solution.py:162
  101.5 14.6 %copy-start.13 = (pred[128]{0:T(512)(128)(4,1)S(1)}, pred[128]{0:T(512)(128)(4,1)}, u32[]{:S(2)}) copy-start(pred[128]{0:T(512)(128)(4,1)} %get-tuple-element.100) | copy-start | bytes 388
  101.5 14.6 %copy-start.14 = (pred[128]{0:T(512)(128)(4,1)S(1)}, pred[128]{0:T(512)(128)(4,1)}, u32[]{:S(2)}) copy-start(pred[128]{0:T(512)(128)(4,1)} %get-tuple-element.101) | copy-start | bytes 388
  101.5 11.1 %collective-permute-start.4 = (bf16[256,256]{1,0:T(8,128)(2,1)S(1)}, bf16[256,256]{1,0:T(8,128)(2,1)S(1)}, u32[]{:S(2)}, u32[]{:S(2)}) collective-permute-start(bf16[256,256]{1,0:T(8,128)(2,1)S(1)} %get-tuple-element.52), channel_id=1, source_target_pairs={{0,127},{1,0},{2,1},{3,2},{4,3},{5,4},{6,5},{7,6},{8,7},{9,8},{10,... | collective-permute-start | bytes 393224 | tf_op jit(solution)/shard_map/ppermute | solution.py:17
  104.5 8.1 %collective-permute-start.3 = (bf16[256,256]{1,0:T(8,128)(2,1)S(1)}, bf16[256,256]{1,0:T(8,128)(2,1)S(1)}, u32[]{:S(2)}, u32[]{:S(2)}) collective-permute-start(bf16[256,256]{1,0:T(8,128)(2,1)S(1)} %get-tuple-element.51), channel_id=1, source_target_pairs={{0,1},{1,2},{2,3},{3,4},{4,5},{5,6},{6,7},{7,8},{8,9},{9,10},{10,1... | collective-permute-start | bytes 393224 | tf_op jit(solution)/shard_map/ppermute | solution.py:17
  112.7 0.8 copy-start.3
  113.5 17.6 %copy-start.11 = (s32[512]{0:T(512)S(1)}, s32[512]{0:T(512)}, u32[]{:S(2)}) copy-start(s32[512]{0:T(512)} %broadcast_bitcast_fusion) | copy-start | bytes 6148
  115.2 1.9 %copy-start.7 = (bf16[256,384]{1,0:T(8,128)(2,1)}, bf16[256,384]{1,0:T(8,128)(2,1)S(1)}, u32[]{:S(2)}) copy-start(bf16[256,384]{1,0:T(8,128)(2,1)S(1)} %reshape.162) | copy-start | bytes 589828
  117.0 26.4 %all-to-all-start.3 = ((bf16[128,2,256]{2,1,0:T(2,128)(2,1)}), bf16[128,2,256]{2,1,0:T(2,128)(2,1)}, u32[]{:S(2)}, u32[]{:S(2)}) async-start(bf16[128,2,256]{2,1,0:T(2,128)(2,1)} %reshape.163), calls=%async_computation.3 | async-start | bytes 262144 | tf_op jit(solution)/shard_map/all_to_all | solution.py:188
  131.1 2.0 %copy-start.8 = (bf16[256,384]{1,0:T(8,128)(2,1)S(1)}, bf16[256,384]{1,0:T(8,128)(2,1)}, u32[]{:S(2)}) copy-start(bf16[256,384]{1,0:T(8,128)(2,1)} %copy-done.7) | copy-start | bytes 589828
  133.5 0.8 copy-start.2
  134.3 19.1 %slice-start = ((bf16[256,384]{1,0:T(8,128)(2,1)}), bf16[256,128]{1,0:T(8,128)(2,1)S(1)}, s32[]{:S(2)}) async-start(bf16[256,384]{1,0:T(8,128)(2,1)} %copy-done.7), calls=%async_computation.5 | async-start | bytes 131072 | tf_op jit(solution)/shard_map/slice | solution.py:170
  147.9 17.0 %all-to-all-start.4 = ((bf16[128,2,128]{2,1,0:T(2,128)(2,1)}), bf16[128,2,128]{2,1,0:T(2,128)(2,1)S(1)}, u32[]{:S(2)}, u32[]{:S(2)}) async-start(bf16[128,2,128]{2,1,0:T(2,128)(2,1)} %broadcast_in_dim.46), calls=%async_computation.4 | async-start | bytes 131072 | tf_op jit(solution)/shard_map/all_to_all | solution.py:193

commit v4 on v3

v4 whole, which is shorter than its diff:
```python
import functools
import math

import jax
import jax.numpy as jnp
from jax import lax
from jax.experimental import pallas as pl
from jax.experimental.pallas import tpu as pltpu
from jax.sharding import PartitionSpec as P

BLOCK = 128
REACH = 2

EPSILON = 1e-05
THETA = 500000.0


def shift(value, axis, by):
    count = lax.axis_size(axis)
    return lax.ppermute(value, axis, [(i, (i + by) % count) for i in range(count)])


def tables(positions, head_width):
    middle = head_width // 2
    frequency = jnp.exp(
        -(2.0 / head_width) * math.log(THETA) * jnp.arange(middle, dtype=jnp.float32)
    )
    angles = positions.astype(jnp.float32)[:, None] * frequency[None, :]
    cosine, sine = jnp.cos(angles), jnp.sin(angles)
    return jnp.concatenate([cosine, cosine], axis=1), jnp.concatenate([-sine, sine], axis=1)

BF16, F32 = jnp.bfloat16, jnp.float32
VMEM_LIMIT = 48 * 1024 * 1024


def call(kernel, outs, scalars, arrays, scratch=(), blocks=None, aliases=None, anywhere=()):
    whole = pl.BlockSpec(memory_space=pltpu.VMEM)
    specs = [pl.BlockSpec(memory_space=pltpu.SMEM)] * len(scalars)
    specs += [
        pl.BlockSpec(memory_space=pl.ANY) if i in anywhere else whole for i in range(len(arrays))
    ]
    out_specs = [pl.BlockSpec(memory_space=pl.ANY) if aliases else whole for _ in outs]
    return pl.pallas_call(
        kernel,
        out_shape=[jax.ShapeDtypeStruct(shape, dtype) for shape, dtype in outs],
        in_specs=specs,
        out_specs=out_specs,
        scratch_shapes=list(scratch),
        input_output_aliases=aliases or {},
        compiler_params=pltpu.CompilerParams(vmem_limit_bytes=VMEM_LIMIT),
    )(*scalars, *arrays)


def turn(values, cosine, signed_sine):
    return values * cosine + pltpu.roll(values, values.shape[1] // 2, axis=1) * signed_sine


def spread_down(row, size):
    return jnp.transpose(jnp.broadcast_to(row, (size, size)))


def outgoing_kernel(sections, place, x, gain, query_weight, keyval_weight, *refs):
    outs, (keyval_own, squares_own, keyval, rows16) = refs[: sections - 1], refs[sections - 1 :]
    rows, part = x.shape
    size = BLOCK
    count = rows // size
    rows16[...] = jnp.zeros_like(rows16)
    squares_own[...] = jnp.zeros_like(squares_own)
    for b in range(count):
        block = x[b * size : (b + 1) * size, :].astype(F32)
        total = jnp.sum(block * block, axis=1, keepdims=True)
        line = jnp.transpose(jnp.broadcast_to(total, (size, size)))[0:1, :]
        high = line.astype(BF16).astype(F32)
        squares_own[b : b + 1, :] = line
        rows16[b : b + 1, :] = high
        rows16[count + b : count + b + 1, :] = line - high
        block = block * gain[...]
        high = block.astype(BF16)
        low = (block - high.astype(F32)).astype(BF16)
        both = jnp.dot(
            jnp.concatenate([high, low], axis=0), keyval_weight[...], preferred_element_type=F32
        )
        keyval[b * size : (b + 1) * size, :] = both[:size] + both[size:]
    here = place[0]
    keyval_own[...] = keyval[pl.ds(pl.multiple_of(here * size, size), size), :]
    width = keyval.shape[1] // 2
    for k in range(1, sections):
        target = lax.rem(here + k, sections)
        out = outs[k - 1]
        out[0:part, :] = query_weight[pl.ds(pl.multiple_of(target * part, part), part), :]
        block = keyval[pl.ds(pl.multiple_of(target * size, size), size), :].astype(BF16)
        out[part : part + size, :] = block[:, :width]
        out[part + size : part + 2 * size, :] = block[:, width:]
        out[part + 2 * size : part + 2 * size + 16, :] = rows16[...].astype(BF16)


def partial_kernel(
    sections, place, x, gain, query_weight, keyval_own, squares_own, cosine, sine, *refs
):
    arrived, (out, squares, normed) = refs[: sections - 1], refs[sections - 1 :]
    rows, part = x.shape
    size = BLOCK
    count = rows // size
    here = place[0]
    total = squares_own[0:count, :]
    keyval = keyval_own[...]
    for piece in arrived:
        tail = piece[part + 2 * size : part + 2 * size + 16, :].astype(F32)
        total = total + tail[0:count, :] + tail[count : 2 * count, :]
        keyval = keyval + jnp.concatenate(
            [
                piece[part : part + size, :].astype(F32),
                piece[part + size : part + 2 * size, :].astype(F32),
            ],
            axis=1,
        )
    squares[0:count, :] = lax.rsqrt(total / (part * sections) + EPSILON)
    for b in range(count):
        scale = spread_down(squares[b : b + 1, :], size)
        scale = jnp.concatenate([scale] * (part // size), axis=1)
        block = x[b * size : (b + 1) * size, :].astype(F32) * scale * gain[...]
        normed[b * size : (b + 1) * size, :] = block.astype(BF16)
    weights = [query_weight[pl.ds(pl.multiple_of(here * part, part), part), :]]
    weights += [piece[0:part, :] for piece in arrived]
    head_width = query_weight.shape[1]
    for k in range(0, sections, 2):
        pair = jnp.concatenate(weights[k : k + 2], axis=1)
        value = jnp.dot(normed[...], pair, preferred_element_type=F32).astype(BF16)
        for j in range(2):
            target = lax.rem(here - k - j + sections, sections)
            out[target, 0:rows, :] = value[:, j * head_width : (j + 1) * head_width]
    scale = spread_down(squares[pl.ds(here, 1), :], size)
    keys = turn(keyval[:, :head_width] * scale, cosine[...], sine[...]).astype(BF16)
    values = (keyval[:, head_width:] * scale).astype(BF16)
    for target in range(sections):
        out[target, rows : rows + size, :] = keys
        out[target, rows + size : rows + 2 * size, :] = values
        out[target, rows + 2 * size : rows + 2 * size + 16, :] = jnp.zeros(
            (16, head_width), BF16
        )


def header_kernel(
    sections, offset, place, owners, spread, gain, query_weight, keyval_weight, *refs
):
    arrived, (_, out, small, semaphore) = refs[: sections - 1], refs[sections - 1 :]
    part = gain.shape[1]
    head_width = query_weight.shape[1]
    here = place[0]
    row = lax.broadcasted_iota(jnp.int32, (16, part), 0)
    pair = [spread[owners[h]].astype(F32) for h in range(2)]
    line = jnp.where(lax.rem(row, 2) == 0, pair[0][0:1, :], pair[1][1:2, :])
    gained = line * gain[...]
    high = gained.astype(BF16)
    low = (gained - high.astype(F32)).astype(BF16)
    left = jnp.concatenate([high, low], axis=0)
    squares = jnp.broadcast_to(jnp.sum(line * line, axis=1, keepdims=True), (16, head_width))
    row = lax.broadcasted_iota(jnp.int32, (16, head_width), 0)

    def product(weight):
        both = jnp.dot(left, weight, preferred_element_type=F32)
        return both[:16] + both[16:]

    keyval = product(keyval_weight[...])
    weights = [query_weight[pl.ds(pl.multiple_of(here * part, part), part), :]]
    weights += [piece[0:part, :] for piece in arrived]
    for k in range(0, sections, 2):
        queries = product(jnp.concatenate(weights[k : k + 2], axis=1))
        for j in range(2):
            target = lax.rem(here - k - j + sections, sections)
            value = jnp.where(
                row < 4,
                queries[:, j * head_width : (j + 1) * head_width],
                jnp.where(
                    row < 8,
                    keyval[:, :head_width],
                    jnp.where(row < 12, keyval[:, head_width:], squares),
                ),
            )
            high = value.astype(BF16).astype(F32)
            value = jnp.where(lax.rem(row, 4) < 2, high, value - high)
            small[target] = value.astype(BF16)
    copy = pltpu.make_async_copy(small, out.at[:, pl.ds(offset, 16), :], semaphore)
    copy.start()
    copy.wait()


def header_finish_kernel(width, arrived, cosine, sine, out):
    total = jnp.sum(arrived[...].astype(F32), axis=0)
    total = total + pltpu.roll(total, 14, axis=0)
    scale = lax.rsqrt(pltpu.roll(total, 4, axis=0) / width + EPSILON)
    queries = turn(total * scale, cosine[...], sine[...])
    keys = turn(pltpu.roll(total, 12, axis=0) * scale, cosine[...], sine[...])
    values = pltpu.roll(total, 8, axis=0) * scale
    chunk = jnp.concatenate([queries, keys, values], axis=1)[0:2, :].astype(BF16)
    out[...] = jnp.broadcast_to(chunk[None], out.shape)


def main_finish_kernel(arrived, cosine, sine, queries, keyval):
    rows, head_width = queries.shape
    size = BLOCK
    for b in range(rows // size):
        part = slice(b * size, (b + 1) * size)
        total = jnp.sum(arrived[:, part, :].astype(F32), axis=0)
        queries[part, :] = turn(total, cosine[part, :], sine[part, :]).astype(BF16)
        keyval[part, 0:head_width] = arrived[b, rows : rows + size, :]
        keyval[part, head_width:] = arrived[b, rows + size : rows + 2 * size, :]


def merge_kernel(parts, out):
    head_width = out.shape[2]
    everything = parts[...].astype(F32)
    level = everything[:, :, head_width:]
    level = level[:, :, 0:1] + level[:, :, 32:33] + level[:, :, 64:65]
    factor = jnp.exp(level - jnp.max(level, axis=0, keepdims=True))
    total = jnp.sum(everything[:, :, :head_width] * factor, axis=0)
    result = (total / jnp.sum(factor, axis=0)).astype(BF16)
    out[...] = jnp.broadcast_to(result[None], out.shape)


def on_device(
    hidden,
    norm_gain,
    query_weight,
    key_weight,
    value_weight,
    output_weight,
    block_reach,
    header_ids,
):
    bf16, f32 = jnp.bfloat16, jnp.float32
    rows, part = hidden.shape
    head_width = key_weight.shape[1]
    sections = lax.axis_size("section")
    shards = lax.axis_size("seq")
    local_blocks = rows // BLOCK
    total_blocks = local_blocks * shards
    section_place = lax.axis_index("section")
    seq_place = lax.axis_index("seq")
    headers = header_ids.shape[0]
    lines = BLOCK // shards
    mine = headers * lines
    owners = header_ids // local_blocks
    slots = header_ids % local_blocks
    width = part * sections
    gain = norm_gain.astype(f32)[None, :]

    candidates = jnp.concatenate(
        [
            lax.dynamic_slice_in_dim(hidden, slots[h] * BLOCK, BLOCK, axis=0).reshape(
                shards, lines, part
            )
            for h in range(headers)
        ],
        axis=1,
    )
    spread = lax.all_to_all(candidates, "seq", 0, 0)

    place = section_place.astype(jnp.int32).reshape(1)
    keyval_weight = jnp.concatenate([key_weight, value_weight], axis=1)
    tall = part + 2 * BLOCK + 16
    *outgoing, keyval_own, squares_own = call(
        functools.partial(outgoing_kernel, sections),
        [((tall, head_width), bf16)] * (sections - 1)
        + [((BLOCK, 2 * head_width), f32), ((8, head_width), f32)],
        [place],
        [hidden, gain, query_weight, keyval_weight],
        [pltpu.VMEM((rows, 2 * head_width), f32), pltpu.VMEM((16, head_width), f32)],
    )
    incoming = [shift(outgoing[k - 1], "section", k) for k in range(1, sections)]
    own_positions = seq_place * rows + jnp.arange(rows, dtype=jnp.int32)
    own_tables = tables(own_positions, head_width)
    block_tables = [
        lax.dynamic_slice_in_dim(table, section_place * BLOCK, BLOCK, axis=0)
        for table in own_tables
    ]
    length = rows + 2 * BLOCK + 16
    (payload,) = call(
        functools.partial(partial_kernel, sections),
        [((sections, length, head_width), bf16)],
        [place],
        [hidden, gain, query_weight, keyval_own, squares_own, *block_tables, *incoming],
        [pltpu.VMEM((8, head_width), f32), pltpu.VMEM((rows, part), bf16)],
    )
    (payload,) = call(
        functools.partial(header_kernel, sections, length - 16),
        [((sections, length, head_width), bf16)],
        [place, owners],
        [spread, gain, query_weight, keyval_weight, *incoming, payload],
        [pltpu.VMEM((sections, 16, head_width), bf16), pltpu.SemaphoreType.DMA],
        aliases={5 + sections: 0},
        anywhere=(3 + sections,),
    )
    arrived = lax.all_to_all(payload, "section", 0, 0)

    index = jnp.arange(16, dtype=jnp.int32) % 2
    header_positions = jnp.where(index == 0, header_ids[0], header_ids[1]) * BLOCK + seq_place
    (header_copies,) = call(
        functools.partial(header_finish_kernel, width),
        [((shards, mine, 3 * head_width), bf16)],
        [],
        [arrived[:, length - 16 :], *tables(header_positions, head_width)],
    )
    header_pack = lax.all_to_all(header_copies, "seq", 0, 0).reshape(-1, 3 * head_width)
    queries, stacked = call(
        main_finish_kernel,
        [((rows, head_width), bf16), ((rows, 2 * head_width), bf16)],
        [],
        [arrived, *own_tables],
    )
    keys, values = stacked[:, :head_width], stacked[:, head_width:]
    head_queries = header_pack[:, :head_width]
    head_keys = header_pack[:, head_width : 2 * head_width]
    head_values = header_pack[:, 2 * head_width :]

    inverse_root = 1.0 / math.sqrt(head_width)
    far_scores = (
        jnp.einsum("qd,kd->qk", head_queries, keys, preferred_element_type=f32) * inverse_root
    )
    far_max = jnp.max(far_scores, axis=1, keepdims=True)
    far_weights = jnp.exp(far_scores - far_max)
    far_total = jnp.sum(far_weights, axis=1, keepdims=True)
    far_out = jnp.dot(far_weights.astype(bf16), values, preferred_element_type=f32) / far_total
    far_level = far_max + jnp.log(far_total)
    first = far_level.astype(bf16).astype(f32)
    second = (far_level - first).astype(bf16).astype(f32)
    third = far_level - first - second
    lane = lax.broadcasted_iota(jnp.int32, far_out.shape, 1)
    level = jnp.where(lane < 32, first, jnp.where(lane < 64, second, third))
    partial = jnp.concatenate([far_out, level], axis=1).astype(bf16)
    partial, queries, stacked = lax.optimization_barrier((partial, queries, stacked))
    parts = lax.all_to_all(partial.reshape(shards, mine, 2 * head_width), "seq", 0, 0)
    (result_copies,) = call(merge_kernel, [((shards, mine, head_width), bf16)], [], [parts])
    header_all = lax.all_to_all(result_copies, "seq", 0, 0).reshape(
        shards, headers, lines, head_width
    )

    margin_rows = REACH * BLOCK
    extended = jnp.concatenate(
        [
            shift(stacked[rows - margin_rows :], "seq", 1),
            stacked,
            shift(stacked[:margin_rows], "seq", -1),
        ]
    )
    near_keys = extended[:, :head_width]
    near_values = extended[:, head_width:]
    extent = rows + 2 * margin_rows
    key_blocks = seq_place * local_blocks - REACH + jnp.arange(extent, dtype=jnp.int32) // BLOCK
    query_blocks = seq_place * local_blocks + jnp.arange(rows, dtype=jnp.int32) // BLOCK
    limits = jnp.repeat(block_reach, BLOCK)
    key_header = jnp.any(header_ids[:, None] == key_blocks[None, :], axis=0)
    allowed = (key_blocks >= 0)[None, :] & (key_blocks < total_blocks)[None, :]
    allowed = allowed & (jnp.abs(key_blocks[None, :] - query_blocks[:, None]) <= limits[:, None])
    allowed = allowed & jnp.logical_not(key_header)[None, :]
    near_scores = (
        jnp.einsum("qd,kd->qk", queries, near_keys, preferred_element_type=f32) * inverse_root
    )
    near_scores = jnp.where(allowed, near_scores, -jnp.inf)
    head_scores = (
        jnp.einsum("qd,kd->qk", queries, head_keys, preferred_element_type=f32) * inverse_root
    )
    scores = jnp.concatenate([near_scores, head_scores], axis=1)
    row_top = jnp.max(scores, axis=1)
    weights = jnp.exp(scores - row_top[:, None])
    row_sums = jnp.sum(weights, axis=1)
    joined = jnp.concatenate([near_values, head_values], axis=0)
    mixed = (
        jnp.dot(weights.astype(bf16), joined, preferred_element_type=f32) / row_sums[:, None]
    ).astype(bf16)

    blocks = []
    for b in range(local_blocks):
        block = mixed[b * BLOCK : (b + 1) * BLOCK]
        for h in range(headers):
            here = header_ids[h] == seq_place * local_blocks + b
            block = jnp.where(here, header_all[:, h].reshape(BLOCK, head_width), block)
        blocks.append(block)
    attended = jnp.concatenate(blocks, axis=0)
    gathered = lax.all_gather(attended, "section", axis=1, tiled=True)
    return jnp.dot(gathered, output_weight, preferred_element_type=f32).astype(bf16)


def solution(mesh):
    return jax.shard_map(
        on_device,
        mesh=mesh,
        in_specs=(
            P("seq", "section"),
            P("section"),
            P(None, "section"),
            P("section", None),
            P("section", None),
            P(None, "section"),
            P("seq"),
            P(),
        ),
        out_specs=P("seq", "section"),
        check_vma=False,
    )
```

time: 180 us -> 169 us (0.939)
  other arithmetic: 17.1 us -> 6.61 us
  starting transfers between devices: 64.7 us -> 74.2 us
  Pallas kernels: 0 us -> 8.96 us
  matrix products: 12.9 us -> 5.81 us
  waiting for transfers between devices: 47.5 us -> 41.1 us
  between operations: 10.1 us -> 6.84 us
  local copies, waits for them, and re-layouts: 14.5 us -> 11.7 us
    all_to_all x3, starting transfers between devices: 16.2 us -> 33.5 us  [the longest x1 15.7 us: on_device(): lax.all_to_all(header_copies, 'seq', 0, 0).reshape(-1, 3 * head_width)]
    ppermute x5, waiting for transfers between devices: 2.63 us -> 13.9 us  [shift(): lax.ppermute(value, axis, [(i, (i + by) % count) for i in range(count)])]
    all_to_all x1, waiting for transfers between devices: 8.98 us -> 0.01 us  [on_device(): spread = lax.all_to_all(candidates, 'seq', 0, 0)]
    pallas_call x0 -> x6, Pallas kernels: none -> 8.96 us  [call(): pl.pallas_call(kernel, out_shape=[jax.ShapeDtypeStruct(shape, dtype) for...]
    all_to_all x1, waiting for transfers between devices: 8.68 us -> 0.01 us  [on_device(): lax.all_to_all(partial.reshape(shards, mine, 2 * head_width), 'seq', 0, 0)]
    all_to_all x1, starting transfers between devices: 14.1 us -> 5.73 us  [on_device(): lax.all_to_all(partial.reshape(shards, mine, 2 * head_width), 'seq', 0, 0)]
    dot_general x6 -> x0, matrix products: 6.59 us -> none  [on_device(): jnp.dot(left, weight, preferred_element_type=f32)]
    convert_element_type x14 -> x0, other arithmetic: 5.67 us -> none  [the longest x2 2.21 us: project(): queries = rotate(total[:, :head_width], cosine, sine).astype(bf16)]
  transfers between devices with their start and end apart: 10 -> 10, of which waited for: 5 -> 6; matrix products, arithmetic and copies ran while one was open for 10% -> 6% of each run, Pallas kernels for 0% -> 3%
where the time goes in v4:
time: 169 us; the launch traced here: 167 us
  starting transfers between devices  74.2 us (44%)
  waiting for transfers between devices  41.1 us (24%)
  blocking collectives  11.9 us (7%)
  local copies, waits for them, and re-layouts  11.7 us (7%)
  Pallas kernels  8.96 us (5%)
  between operations  6.84 us (4%)
  other arithmetic  6.61 us (4%)
  matrix products  5.81 us (3%)
    all_to_all x1, starting transfers between devices, on_device(): spread = lax.all_to_all(candidates, 'seq', 0, 0)  18.9 us
    ppermute x5, starting transfers between devices, shift(): lax.ppermute(value, axis, [(i, (i + by) % count) for i in range(count)])  16.1 us
    all_to_all x1, starting transfers between devices, on_device(): lax.all_to_all(header_copies, 'seq', 0, 0).reshape(-1, 3 * head_width)  15.7 us
    ppermute x5, waiting for transfers between devices, shift(): lax.ppermute(value, axis, [(i, (i + by) % count) for i in range(count)])  13.9 us
    all_to_all x1, starting transfers between devices, on_device(): lax.all_to_all(result_copies, 'seq', 0, 0)  13 us
    all_gather x1, blocking collectives, on_device(): gathered = lax.all_gather(attended, 'section', axis=1, tiled=True)  11.9 us
    all_to_all x1, waiting for transfers between devices, on_device(): arrived = lax.all_to_all(payload, 'section', 0, 0)  9.62 us
    all_to_all x1, waiting for transfers between devices, on_device(): lax.all_to_all(result_copies, 'seq', 0, 0)  9.25 us
  transfers between devices with their start and end apart: 10, of which 6 were waited for; matrix products, arithmetic and copies ran while one was open for 6% of the time, Pallas kernels for 3%

profile of v4, /device:TPU:1, one launch (start us, length us, event | category | flops | bytes accessed | tf_op | source)
XLA Modules:
  0.0 167.2 jit_solution(4500462226739365176)
XLA Ops:
  2.6 1.1 dynamic-slice_bitcast_fusion.1
  4.5 2.0 %pad_maximum_fusion = bf16[128,2,1024]{2,1,0:T(2,128)(2,1)} fusion(bf16[128,1,1024]{2,1,0:T(2,128)(2,1)S(1)} %copy.22, bf16[128,1,1024]{2,1,0:T(2,128)(2,1)S(1)} %copy.21), kind=kLoop, calls=%fused_computation.16 | loop fusion | flops 1048576 | bytes 1048576 | tf_op jit(solution)/shard_map/concatenate | solution.py:248
  6.5 18.9 %all-to-all-start = ((bf16[128,2,1024]{2,1,0:T(2,128)(2,1)}), bf16[128,2,1024]{2,1,0:T(2,128)(2,1)}, u32[]{:S(2)}, u32[]{:S(2)}) async-start(bf16[128,2,1024]{2,1,0:T(2,128)(2,1)} %pad_maximum_fusion), calls=%async_computation | async-start | bytes 1048576 | tf_op jit(solution)/shard_map/all_to_all | solution.py:257
  26.2 1.7 %constant_dynamic-update-slice_fusion.keyval_weight = bf16[1024,256]{1,0:T(8,128)(2,1)} fusion(bf16[1024,256]{1,0:T(8,128)(2,1)} %constant_dynamic-update-slice_fusion.1, bf16[1024,128]{1,0:T(8,128)(2,1)} %param.12), kind=kLoop, calls=%fused_computation.54 | loop fusion | bytes 524288 | tf_op jit(solution)/shard_map/concatenate | solution.py:260
  27.9 1.0 copy-done.3
  28.9 1.8 %shard_map.82 = (bf16[1296,128]{1,0:T(8,128)(2,1)}, bf16[1296,128]{1,0:T(8,128)(2,1)}, bf16[1296,128]{1,0:T(8,128)(2,1)}, f32[128,256]{1,0:T(8,128)S(1)}, f32[8,128]{1,0:T(8,128)S(1)}) custom-call(s32[1]{0:T(128)} %bitcast.1.place, bf16[512,1024]{1,0:T(8,128)(2,1)S(1)} %copy-done.2, f32[1,1024]{1,0:T(1,128)S(1)} %bitcast.27, ...), custom_call_target="tpu_custom_call" | custom-call | tf_op jit(solution)/shard_map/pallas_call | solution.py:43
  31.4 3.1 %collective-permute-start = (bf16[1296,128]{1,0:T(8,128)(2,1)}, bf16[1296,128]{1,0:T(8,128)(2,1)S(1)}, u32[]{:S(2)}, u32[]{:S(2)}) collective-permute-start(bf16[1296,128]{1,0:T(8,128)(2,1)} %get-tuple-element.15), channel_id=1, source_target_pairs={{0,128},{128,256},{256,384},{384,0},{1,129},{129,257},{257,385},{3... | collective-permute-start | bytes 995336 | tf_op jit(solution)/shard_map/ppermute | solution.py:20
  34.5 4.4 %collective-permute-start.1 = (bf16[1296,128]{1,0:T(8,128)(2,1)}, bf16[1296,128]{1,0:T(8,128)(2,1)}, u32[]{:S(2)}, u32[]{:S(2)}) collective-permute-start(bf16[1296,128]{1,0:T(8,128)(2,1)} %get-tuple-element.16), channel_id=1, source_target_pairs={{0,256},{128,384},{256,0},{384,128},{1,257},{129,385},{257,1},{385... | collective-permute-start | bytes 995336 | tf_op jit(solution)/shard_map/ppermute | solution.py:20
  38.8 3.1 %collective-permute-start.2 = (bf16[1296,128]{1,0:T(8,128)(2,1)}, bf16[1296,128]{1,0:T(8,128)(2,1)}, u32[]{:S(2)}, u32[]{:S(2)}) collective-permute-start(bf16[1296,128]{1,0:T(8,128)(2,1)} %get-tuple-element.17), channel_id=1, source_target_pairs={{0,384},{128,0},{256,128},{384,256},{1,385},{129,1},{257,129},{385... | collective-permute-start | bytes 995336 | tf_op jit(solution)/shard_map/ppermute | solution.py:20
  42.6 1.0 multiply_sine_fusion
  43.8 7.4 %collective-permute-done.1.refs_1_ = bf16[1296,128]{1,0:T(8,128)(2,1)} collective-permute-done((bf16[1296,128]{1,0:T(8,128)(2,1)}, bf16[1296,128]{1,0:T(8,128)(2,1)}, u32[]{:S(2)}, u32[]{:S(2)}) %collective-permute-start.1) | collective-permute-done | bytes 331808 | tf_op jit(solution)/shard_map/ppermute | solution.py:20
  51.2 1.8 %collective-permute-done.2.refs_2_ = bf16[1296,128]{1,0:T(8,128)(2,1)} collective-permute-done((bf16[1296,128]{1,0:T(8,128)(2,1)}, bf16[1296,128]{1,0:T(8,128)(2,1)}, u32[]{:S(2)}, u32[]{:S(2)}) %collective-permute-start.2) | collective-permute-done | bytes 331808 | tf_op jit(solution)/shard_map/ppermute | solution.py:20
  53.9 2.8 %shard_map.83.refs_3_ = bf16[4,784,128]{2,1,0:T(8,128)(2,1)} custom-call(s32[1]{0:T(128)} %bitcast.1.place, bf16[512,1024]{1,0:T(8,128)(2,1)S(1)} %copy-done.2, f32[1,1024]{1,0:T(1,128)S(1)} %bitcast.28, bf16[4096,128]{1,0:T(8,128)(2,1)S(1)} %copy-done.1, f32[128,256]{1,0:T(8,128)S(1)} %copy-done.6, f32[8,128]{1,0:T(8,128)S(1)} %get-tuple-element.19.squares_own, ...), custom_call_target="tpu_custom_call" | custom-call | tf_op jit(solution)/shard_map/pallas_call | solution.py:43
  56.6 1.0 copy-done.4
  57.7 2.2 %shard_map.84 = bf16[4,784,128]{2,1,0:T(8,128)(2,1)} custom-call(s32[1]{0:T(128)} %bitcast.1.place, s32[2]{0:T(128)S(1)} %get-tuple-element.50.owners, bf16[128,2,1024]{2,1,0:T(2,128)(2,1)} %all-to-all-done.spread, f32[1,1024]{1,0:T(1,128)S(1)} %bitcast.29, bf16[4096,128]{1,0:T(8,128)(2,1)S(1)} %copy-done.1, ...), custom_call_target="tpu_custom_call", output_to_operand_aliasing={{}: (9, {})} | custom-call | tf_op jit(solution)/shard_map/pallas_call | solution.py:43
  60.0 4.8 %all-to-all-start.1 = ((bf16[4,784,128]{2,1,0:T(8,128)(2,1)}), bf16[4,784,128]{2,1,0:T(8,128)(2,1)S(1)}, u32[]{:S(2)}, u32[]{:S(2)}) async-start(bf16[4,784,128]{2,1,0:T(8,128)(2,1)} %shard_map.84), calls=%async_computation.1 | async-start | bytes 1605632 | tf_op jit(solution)/shard_map/all_to_all | solution.py:294
  64.8 1.3 fusion.44
  66.4 9.6 %all-to-all-done.1.arrived = bf16[4,784,128]{2,1,0:T(8,128)(2,1)S(1)} async-done(((bf16[4,784,128]{2,1,0:T(8,128)(2,1)}), bf16[4,784,128]{2,1,0:T(8,128)(2,1)S(1)}, u32[]{:S(2)}, u32[]{:S(2)}) %all-to-all-start.1) | async-done | bytes 802848 | tf_op jit(solution)/shard_map/all_to_all | solution.py:294
  76.8 15.7 %all-to-all-start.2 = ((bf16[128,2,384]{2,1,0:T(2,128)(2,1)}), bf16[128,2,384]{2,1,0:T(2,128)(2,1)S(1)}, u32[]{:S(2)}, u32[]{:S(2)}) async-start(bf16[128,2,384]{2,1,0:T(2,128)(2,1)} %shard_map.85), calls=%async_computation.2 | async-start | bytes 393216 | tf_op jit(solution)/shard_map/all_to_all | solution.py:304
  98.1 8.4 %all-to-all-done.2 = bf16[128,2,384]{2,1,0:T(2,128)(2,1)S(1)} async-done(((bf16[128,2,384]{2,1,0:T(2,128)(2,1)}), bf16[128,2,384]{2,1,0:T(2,128)(2,1)S(1)}, u32[]{:S(2)}, u32[]{:S(2)}) %all-to-all-start.2) | async-done | bytes 196640 | tf_op jit(solution)/shard_map/all_to_all | solution.py:304
  108.5 5.7 %all-to-all-start.3 = ((bf16[128,2,256]{2,1,0:T(2,128)(2,1)}), bf16[128,2,256]{2,1,0:T(2,128)(2,1)S(1)}, u32[]{:S(2)}, u32[]{:S(2)}) async-start(bf16[128,2,256]{2,1,0:T(2,128)(2,1)} %reshape.125), calls=%async_computation.3 | async-start | bytes 262144 | tf_op jit(solution)/shard_map/all_to_all | solution.py:332
  114.2 2.9 %collective-permute-start.4 = (bf16[256,256]{1,0:T(8,128)(2,1)S(1)}, bf16[256,256]{1,0:T(8,128)(2,1)S(1)}, u32[]{:S(2)}, u32[]{:S(2)}) collective-permute-start(bf16[256,256]{1,0:T(8,128)(2,1)S(1)} %get-tuple-element.30), channel_id=1, source_target_pairs={{0,127},{1,0},{2,1},{3,2},{4,3},{5,4},{6,5},{7,6},{8,7},{9,8},{10,... | collective-permute-start | bytes 393224 | tf_op jit(solution)/shard_map/ppermute | solution.py:20
  117.2 2.6 %collective-permute-start.3 = (bf16[256,256]{1,0:T(8,128)(2,1)S(1)}, bf16[256,256]{1,0:T(8,128)(2,1)S(1)}, u32[]{:S(2)}, u32[]{:S(2)}) collective-permute-start(bf16[256,256]{1,0:T(8,128)(2,1)S(1)} %get-tuple-element.31), channel_id=1, source_target_pairs={{0,1},{1,2},{2,3},{3,4},{4,5},{5,6},{6,7},{7,8},{8,9},{9,10},{10,1... | collective-permute-start | bytes 393224 | tf_op jit(solution)/shard_map/ppermute | solution.py:20
  120.2 4.7 %collective-permute-done.3 = bf16[256,256]{1,0:T(8,128)(2,1)S(1)} collective-permute-done((bf16[256,256]{1,0:T(8,128)(2,1)S(1)}, bf16[256,256]{1,0:T(8,128)(2,1)S(1)}, u32[]{:S(2)}, u32[]{:S(2)}) %collective-permute-start.3) | collective-permute-done | bytes 131104 | tf_op jit(solution)/shard_map/ppermute | solution.py:20
  124.9 1.0 fusion.54
  126.0 1.3 copy-done.13
  127.8 1.1 shard_map.87
  129.0 13.0 %all-to-all-start.4 = ((bf16[128,2,128]{2,1,0:T(2,128)(2,1)}), bf16[128,2,128]{2,1,0:T(2,128)(2,1)S(1)}, u32[]{:S(2)}, u32[]{:S(2)}) async-start(bf16[128,2,128]{2,1,0:T(2,128)(2,1)} %shard_map.87), calls=%async_computation.4 | async-start | bytes 131072 | tf_op jit(solution)/shard_map/all_to_all | solution.py:334
  142.0 2.2 %fusion.10 = bf16[512,128]{1,0:T(8,128)(2,1)S(1)} fusion(f32[512,256]{1,0:T(8,128)S(1)} %get-tuple-element.56, f32[512,1024]{1,0:T(8,128)} %copy-done.13, f32[512]{0:T(512)S(1)} %reduce_max.32, bf16[256,128]{1,0:T(8,128)(2,1)S(1)} %slice-done, bf16[1024,128]{1,0:T(8,128)(2,1)S(1)} %slice.100, f32[512]{0:T(512)S(1)} %fusion.3), kind=kOutput, calls=%fused_computation.13 | convolution fusion | flops 170524672 | bytes 3084288 | tf_op jit(solution)/shard_map/dot_general | solution.py:369
  144.1 9.3 %all-to-all-done.4 = bf16[128,2,128]{2,1,0:T(2,128)(2,1)S(1)} async-done(((bf16[128,2,128]{2,1,0:T(2,128)(2,1)}), bf16[128,2,128]{2,1,0:T(2,128)(2,1)S(1)}, u32[]{:S(2)}, u32[]{:S(2)}) %all-to-all-start.4) | async-done | bytes 65568 | tf_op jit(solution)/shard_map/all_to_all | solution.py:334
  153.6 11.9 %all_gather.3 = bf16[512,512]{1,0:T(8,128)(2,1)S(1)} all-gather(bf16[512,128]{1,0:T(8,128)(2,1)S(1)} %pad_maximum_fusion.4), channel_id=1, replica_groups=mesh['section'=4,'seq'=128] {'section'}, dimensions={1}, use_global_device_ids=true | all-gather | bytes 655360 | tf_op jit(solution)/shard_map/all_gather | solution.py:380
  165.5 1.7 %convolution_convert_fusion = bf16[512,1024]{1,0:T(8,128)(2,1)} fusion(bf16[512,512]{1,0:T(8,128)(2,1)S(1)} %all_gather.3, bf16[512,1024]{1,0:T(8,128)(2,1)S(1)} %copy-done), kind=kOutput, calls=%fused_computation.8 | convolution fusion | flops 537395200 | bytes 2621440 | tf_op jit(solution)/shard_map/dot_general | solution.py:381
  (86 shorter events, 9.9 us)
Async XLA Ops:
  0.0 165.5 %copy-start = (bf16[512,1024]{1,0:T(8,128)(2,1)S(1)}, bf16[512,1024]{1,0:T(8,128)(2,1)}, u32[]{:S(2)}) copy-start(bf16[512,1024]{1,0:T(8,128)(2,1)} %param.13) | copy-start | bytes 3145732
  3.6 21.8 %copy-start.15 = (bf16[1024,128]{1,0:T(8,128)(2,1)S(1)}, bf16[1024,128]{1,0:T(8,128)(2,1)}, u32[]{:S(2)}) copy-start(bf16[1024,128]{1,0:T(8,128)(2,1)} %param.11) | copy-start | bytes 786436
  4.1 22.1 %copy-start.17 = (bf16[1024]{0:T(1024)(128)(2,1)S(1)}, bf16[1024]{0:T(1024)(128)(2,1)}, u32[]{:S(2)}) copy-start(bf16[1024]{0:T(1024)(128)(2,1)} %param.9) | copy-start | bytes 6148
  4.1 23.8 %copy-start.1 = (bf16[4096,128]{1,0:T(8,128)(2,1)S(1)}, bf16[4096,128]{1,0:T(8,128)(2,1)}, u32[]{:S(2)}) copy-start(bf16[4096,128]{1,0:T(8,128)(2,1)} %query_weight.5) | copy-start | bytes 3145732
  4.1 23.8 %copy-start.2 = (bf16[512,1024]{1,0:T(8,128)(2,1)S(1)}, bf16[512,1024]{1,0:T(8,128)(2,1)}, u32[]{:S(2)}) copy-start(bf16[512,1024]{1,0:T(8,128)(2,1)} %x.3) | copy-start | bytes 3145732
  6.5 50.1 %all-to-all-start = ((bf16[128,2,1024]{2,1,0:T(2,128)(2,1)}), bf16[128,2,1024]{2,1,0:T(2,128)(2,1)}, u32[]{:S(2)}, u32[]{:S(2)}) async-start(bf16[128,2,1024]{2,1,0:T(2,128)(2,1)} %pad_maximum_fusion), calls=%async_computation | async-start | bytes 1048576 | tf_op jit(solution)/shard_map/all_to_all | solution.py:257
  25.4 16.6 %copy-start.16 = (s32[2]{0:T(128)S(1)}, s32[2]{0:T(128)}, u32[]{:S(2)}) copy-start(s32[2]{0:T(128)} %param.15) | copy-start | bytes 28
  27.9 1.0 copy-start.3
  30.7 0.6 copy-start.5
  31.4 12.4 %collective-permute-start = (bf16[1296,128]{1,0:T(8,128)(2,1)}, bf16[1296,128]{1,0:T(8,128)(2,1)S(1)}, u32[]{:S(2)}, u32[]{:S(2)}) collective-permute-start(bf16[1296,128]{1,0:T(8,128)(2,1)} %get-tuple-element.15), channel_id=1, source_target_pairs={{0,128},{128,256},{256,384},{384,0},{1,129},{129,257},{257,385},{3... | collective-permute-start | bytes 995336 | tf_op jit(solution)/shard_map/ppermute | solution.py:20
  34.5 16.7 %collective-permute-start.1 = (bf16[1296,128]{1,0:T(8,128)(2,1)}, bf16[1296,128]{1,0:T(8,128)(2,1)}, u32[]{:S(2)}, u32[]{:S(2)}) collective-permute-start(bf16[1296,128]{1,0:T(8,128)(2,1)} %get-tuple-element.16), channel_id=1, source_target_pairs={{0,256},{128,384},{256,0},{384,128},{1,257},{129,385},{257,1},{385... | collective-permute-start | bytes 995336 | tf_op jit(solution)/shard_map/ppermute | solution.py:20
  38.8 14.1 %collective-permute-start.2 = (bf16[1296,128]{1,0:T(8,128)(2,1)}, bf16[1296,128]{1,0:T(8,128)(2,1)}, u32[]{:S(2)}, u32[]{:S(2)}) collective-permute-start(bf16[1296,128]{1,0:T(8,128)(2,1)} %get-tuple-element.17), channel_id=1, source_target_pairs={{0,384},{128,0},{256,128},{384,256},{1,385},{129,1},{257,129},{385... | collective-permute-start | bytes 995336 | tf_op jit(solution)/shard_map/ppermute | solution.py:20
  43.6 9.3 %copy-start.7 = (f32[512,64]{1,0:T(8,128)}, f32[512,64]{1,0:T(8,128)S(1)}, u32[]{:S(2)}) copy-start(f32[512,64]{1,0:T(8,128)S(1)} %get-tuple-element.37) | copy-start | bytes 393220
  43.7 9.3 %copy-start.9 = (f32[512,64]{1,0:T(8,128)}, f32[512,64]{1,0:T(8,128)S(1)}, u32[]{:S(2)}) copy-start(f32[512,64]{1,0:T(8,128)S(1)} %get-tuple-element.38) | copy-start | bytes 393220
  43.7 9.3 %copy-start.11 = (f32[512,64]{1,0:T(8,128)}, f32[512,64]{1,0:T(8,128)S(1)}, u32[]{:S(2)}) copy-start(f32[512,64]{1,0:T(8,128)S(1)} %get-tuple-element.39) | copy-start | bytes 393220
  53.0 0.9 copy-start.6
  56.6 1.0 copy-start.4
  59.9 37.7 %copy-start.8 = (f32[512,64]{1,0:T(8,128)S(1)}, f32[512,64]{1,0:T(8,128)}, u32[]{:S(2)}) copy-start(f32[512,64]{1,0:T(8,128)} %copy-done.7) | copy-start | bytes 393220
  59.9 37.7 %copy-start.10 = (f32[512,64]{1,0:T(8,128)S(1)}, f32[512,64]{1,0:T(8,128)}, u32[]{:S(2)}) copy-start(f32[512,64]{1,0:T(8,128)} %copy-done.9) | copy-start | bytes 393220
  59.9 37.7 %copy-start.12 = (f32[512,64]{1,0:T(8,128)S(1)}, f32[512,64]{1,0:T(8,128)}, u32[]{:S(2)}) copy-start(f32[512,64]{1,0:T(8,128)} %copy-done.11) | copy-start | bytes 393220
  60.0 37.9 %copy-start.18 = (s32[4]{0:T(128)S(1)}, s32[4]{0:T(128)}, u32[]{:S(2)}) copy-start(s32[4]{0:T(128)} %param.14) | copy-start | bytes 52
  60.0 16.0 %all-to-all-start.1 = ((bf16[4,784,128]{2,1,0:T(8,128)(2,1)}), bf16[4,784,128]{2,1,0:T(8,128)(2,1)S(1)}, u32[]{:S(2)}, u32[]{:S(2)}) async-start(bf16[4,784,128]{2,1,0:T(8,128)(2,1)} %shard_map.84), calls=%async_computation.1 | async-start | bytes 1605632 | tf_op jit(solution)/shard_map/all_to_all | solution.py:294
  76.8 29.7 %all-to-all-start.2 = ((bf16[128,2,384]{2,1,0:T(2,128)(2,1)}), bf16[128,2,384]{2,1,0:T(2,128)(2,1)S(1)}, u32[]{:S(2)}, u32[]{:S(2)}) async-start(bf16[128,2,384]{2,1,0:T(2,128)(2,1)} %shard_map.85), calls=%async_computation.2 | async-start | bytes 393216 | tf_op jit(solution)/shard_map/all_to_all | solution.py:304
  106.6 13.5 %copy-start.14 = (bf16[256,384]{1,0:T(8,128)(2,1)}, bf16[256,384]{1,0:T(8,128)(2,1)S(1)}, u32[]{:S(2)}) copy-start(bf16[256,384]{1,0:T(8,128)(2,1)S(1)} %reshape.124) | copy-start | bytes 589828
  108.5 19.4 %all-to-all-start.3 = ((bf16[128,2,256]{2,1,0:T(2,128)(2,1)}), bf16[128,2,256]{2,1,0:T(2,128)(2,1)S(1)}, u32[]{:S(2)}, u32[]{:S(2)}) async-start(bf16[128,2,256]{2,1,0:T(2,128)(2,1)} %reshape.125), calls=%async_computation.3 | async-start | bytes 262144 | tf_op jit(solution)/shard_map/all_to_all | solution.py:332
  114.2 10.7 %collective-permute-start.4 = (bf16[256,256]{1,0:T(8,128)(2,1)S(1)}, bf16[256,256]{1,0:T(8,128)(2,1)S(1)}, u32[]{:S(2)}, u32[]{:S(2)}) collective-permute-start(bf16[256,256]{1,0:T(8,128)(2,1)S(1)} %get-tuple-element.30), channel_id=1, source_target_pairs={{0,127},{1,0},{2,1},{3,2},{4,3},{5,4},{6,5},{7,6},{8,7},{9,8},{10,... | collective-permute-start | bytes 393224 | tf_op jit(solution)/shard_map/ppermute | solution.py:20
  117.2 7.7 %collective-permute-start.3 = (bf16[256,256]{1,0:T(8,128)(2,1)S(1)}, bf16[256,256]{1,0:T(8,128)(2,1)S(1)}, u32[]{:S(2)}, u32[]{:S(2)}) collective-permute-start(bf16[256,256]{1,0:T(8,128)(2,1)S(1)} %get-tuple-element.31), channel_id=1, source_target_pairs={{0,1},{1,2},{2,3},{3,4},{4,5},{5,6},{6,7},{7,8},{8,9},{9,10},{10,1... | collective-permute-start | bytes 393224 | tf_op jit(solution)/shard_map/ppermute | solution.py:20
  125.9 1.4 copy-start.13
  125.9 16.0 %slice-start = ((bf16[256,384]{1,0:T(8,128)(2,1)}), bf16[256,128]{1,0:T(8,128)(2,1)S(1)}, s32[]{:S(2)}) async-start(bf16[256,384]{1,0:T(8,128)(2,1)} %copy-done.14), calls=%async_computation.5 | async-start | bytes 131072 | tf_op jit(solution)/shard_map/slice | solution.py:314
  129.0 24.4 %all-to-all-start.4 = ((bf16[128,2,128]{2,1,0:T(2,128)(2,1)}), bf16[128,2,128]{2,1,0:T(2,128)(2,1)S(1)}, u32[]{:S(2)}, u32[]{:S(2)}) async-start(bf16[128,2,128]{2,1,0:T(2,128)(2,1)} %shard_map.87), calls=%async_computation.4 | async-start | bytes 131072 | tf_op jit(solution)/shard_map/all_to_all | solution.py:334

commit v5 on v4

--- a/solution.py
+++ b/solution.py
@@ -33,7 +33,7 @@
 VMEM_LIMIT = 48 * 1024 * 1024
 
 
-def call(kernel, outs, scalars, arrays, scratch=(), blocks=None, aliases=None, anywhere=()):
+def call(kernel, outs, scalars, arrays, scratch=(), blocks=None, aliases=None, anywhere=(), flops=None):
     whole = pl.BlockSpec(memory_space=pltpu.VMEM)
     specs = [pl.BlockSpec(memory_space=pltpu.SMEM)] * len(scalars)
     specs += [
@@ -48,6 +48,8 @@
         scratch_shapes=list(scratch),
         input_output_aliases=aliases or {},
         compiler_params=pltpu.CompilerParams(vmem_limit_bytes=VMEM_LIMIT),
+        cost_estimate=flops
+        and pl.CostEstimate(flops=flops, bytes_accessed=0, transcendentals=0),
     )(*scalars, *arrays)
 
 
@@ -59,11 +61,20 @@
     return jnp.transpose(jnp.broadcast_to(row, (size, size)))
 
 
-def outgoing_kernel(sections, place, x, gain, query_weight, keyval_weight, *refs):
-    outs, (keyval_own, squares_own, keyval, rows16) = refs[: sections - 1], refs[sections - 1 :]
+def outgoing_kernel(
+    sections, place, header_ids, x, gain, query_weight, key_weight, value_weight, *refs
+):
+    outs, (picked, keyval_own, squares_own, keyval, rows16) = (
+        refs[: sections - 1],
+        refs[sections - 1 :],
+    )
     rows, part = x.shape
     size = BLOCK
     count = rows // size
+    for h in range(picked.shape[0]):
+        slot = lax.rem(header_ids[h], count)
+        picked[h] = x[pl.ds(pl.multiple_of(slot * size, size), size), :]
+    keyval_weight = jnp.concatenate([key_weight[...], value_weight[...]], axis=1)
     rows16[...] = jnp.zeros_like(rows16)
     squares_own[...] = jnp.zeros_like(squares_own)
     for b in range(count):
@@ -78,7 +89,7 @@
         high = block.astype(BF16)
         low = (block - high.astype(F32)).astype(BF16)
         both = jnp.dot(
-            jnp.concatenate([high, low], axis=0), keyval_weight[...], preferred_element_type=F32
+            jnp.concatenate([high, low], axis=0), keyval_weight, preferred_element_type=F32
         )
         keyval[b * size : (b + 1) * size, :] = both[:size] + both[size:]
     here = place[0]
@@ -141,14 +152,24 @@
 
 
 def header_kernel(
-    sections, offset, place, owners, spread, gain, query_weight, keyval_weight, *refs
+    sections,
+    offset,
+    local_blocks,
+    place,
+    header_ids,
+    spread,
+    gain,
+    query_weight,
+    key_weight,
+    value_weight,
+    *refs,
 ):
     arrived, (_, out, small, semaphore) = refs[: sections - 1], refs[sections - 1 :]
     part = gain.shape[1]
     head_width = query_weight.shape[1]
     here = place[0]
     row = lax.broadcasted_iota(jnp.int32, (16, part), 0)
-    pair = [spread[owners[h]].astype(F32) for h in range(2)]
+    pair = [spread[lax.div(header_ids[h], local_blocks)].astype(F32) for h in range(2)]
     line = jnp.where(lax.rem(row, 2) == 0, pair[0][0:1, :], pair[1][1:2, :])
     gained = line * gain[...]
     high = gained.astype(BF16)
@@ -161,7 +182,7 @@
         both = jnp.dot(left, weight, preferred_element_type=F32)
         return both[:16] + both[16:]
 
-    keyval = product(keyval_weight[...])
+    keyval = product(jnp.concatenate([key_weight[...], value_weight[...]], axis=1))
     weights = [query_weight[pl.ds(pl.multiple_of(here * part, part), part), :]]
     weights += [piece[0:part, :] for piece in arrived]
     for k in range(0, sections, 2):
@@ -205,6 +226,44 @@
         queries[part, :] = turn(total, cosine[part, :], sine[part, :]).astype(BF16)
         keyval[part, 0:head_width] = arrived[b, rows : rows + size, :]
         keyval[part, head_width:] = arrived[b, rows + size : rows + 2 * size, :]
+
+
+def window_kernel(
+    total_blocks, seq_place, reach, header_ids, queries, before, here, after, header, out
+):
+    rows, head_width = queries.shape
+    size = BLOCK
+    count = rows // size
+    parts = [before[j * size : (j + 1) * size, :] for j in range(REACH)]
+    parts += [here[j * size : (j + 1) * size, :] for j in range(count)]
+    parts += [after[j * size : (j + 1) * size, :] for j in range(REACH)]
+    head_keys = header[:, head_width : 2 * head_width]
+    head_values = header[:, 2 * head_width :]
+    for b in range(count):
+        near = parts[b : b + 2 * REACH + 1]
+        keys = jnp.concatenate([part[:, :head_width] for part in near] + [head_keys], axis=0)
+        values = jnp.concatenate([part[:, head_width:] for part in near] + [head_values], axis=0)
+        scores = lax.dot_general(
+            queries[b * size : (b + 1) * size, :],
+            keys,
+            (((1,), (1,)), ((), ())),
+            preferred_element_type=F32,
+        ) * (1.0 / math.sqrt(head_width))
+        pieces = []
+        for j in range(2 * REACH + 1):
+            block = seq_place[0] * count + b + j - REACH
+            allowed = (block >= 0) & (block < total_blocks) & (abs(j - REACH) <= reach[b])
+            for h in range(2):
+                allowed = allowed & (block != header_ids[h])
+            pieces.append(
+                jnp.where(allowed, scores[:, j * size : (j + 1) * size], -jnp.inf)
+            )
+        pieces.append(scores[:, (2 * REACH + 1) * size :])
+        scores = jnp.concatenate(pieces, axis=1)
+        weights = jnp.exp(scores - jnp.max(scores, axis=1, keepdims=True))
+        total = jnp.sum(weights, axis=1, keepdims=True)
+        mixed = jnp.dot(weights.astype(BF16), values, preferred_element_type=F32)
+        out[b * size : (b + 1) * size, :] = (mixed / total).astype(BF16)
 
 
 def merge_kernel(parts, out):
@@ -240,33 +299,24 @@
     headers = header_ids.shape[0]
     lines = BLOCK // shards
     mine = headers * lines
-    owners = header_ids // local_blocks
-    slots = header_ids % local_blocks
     width = part * sections
     gain = norm_gain.astype(f32)[None, :]
 
-    candidates = jnp.concatenate(
-        [
-            lax.dynamic_slice_in_dim(hidden, slots[h] * BLOCK, BLOCK, axis=0).reshape(
-                shards, lines, part
-            )
-            for h in range(headers)
-        ],
-        axis=1,
-    )
-    spread = lax.all_to_all(candidates, "seq", 0, 0)
-
     place = section_place.astype(jnp.int32).reshape(1)
-    keyval_weight = jnp.concatenate([key_weight, value_weight], axis=1)
     tall = part + 2 * BLOCK + 16
-    *outgoing, keyval_own, squares_own = call(
+    *outgoing, picked, keyval_own, squares_own = call(
         functools.partial(outgoing_kernel, sections),
         [((tall, head_width), bf16)] * (sections - 1)
-        + [((BLOCK, 2 * head_width), f32), ((8, head_width), f32)],
-        [place],
-        [hidden, gain, query_weight, keyval_weight],
+        + [
+            ((headers, BLOCK, part), bf16),
+            ((BLOCK, 2 * head_width), f32),
+            ((8, head_width), f32),
+        ],
+        [place, header_ids],
+        [hidden, gain, query_weight, key_weight, value_weight],
         [pltpu.VMEM((rows, 2 * head_width), f32), pltpu.VMEM((16, head_width), f32)],
     )
+    spread = lax.all_to_all(picked.transpose(1, 0, 2), "seq", 0, 0)
     incoming = [shift(outgoing[k - 1], "section", k) for k in range(1, sections)]
     own_positions = seq_place * rows + jnp.arange(rows, dtype=jnp.int32)
     own_tables = tables(own_positions, head_width)
@@ -281,15 +331,16 @@
         [place],
         [hidden, gain, query_weight, keyval_own, squares_own, *block_tables, *incoming],
         [pltpu.VMEM((8, head_width), f32), pltpu.VMEM((rows, part), bf16)],
+        flops=10**11,
     )
     (payload,) = call(
-        functools.partial(header_kernel, sections, length - 16),
+        functools.partial(header_kernel, sections, length - 16, local_blocks),
         [((sections, length, head_width), bf16)],
-        [place, owners],
-        [spread, gain, query_weight, keyval_weight, *incoming, payload],
+        [place, header_ids],
+        [spread, gain, query_weight, key_weight, value_weight, *incoming, payload],
         [pltpu.VMEM((sections, 16, head_width), bf16), pltpu.SemaphoreType.DMA],
-        aliases={5 + sections: 0},
-        anywhere=(3 + sections,),
+        aliases={6 + sections: 0},
+        anywhere=(4 + sections,),
     )
     arrived = lax.all_to_all(payload, "section", 0, 0)
 
@@ -329,45 +380,23 @@
     level = jnp.where(lane < 32, first, jnp.where(lane < 64, second, third))
     partial = jnp.concatenate([far_out, level], axis=1).astype(bf16)
     partial, queries, stacked = lax.optimization_barrier((partial, queries, stacked))
+    margin_rows = REACH * BLOCK
     parts = lax.all_to_all(partial.reshape(shards, mine, 2 * head_width), "seq", 0, 0)
     (result_copies,) = call(merge_kernel, [((shards, mine, head_width), bf16)], [], [parts])
+    before, after = shift(stacked[rows - margin_rows :], "seq", 1), shift(
+        stacked[:margin_rows], "seq", -1
+    )
+    result_copies, queries = lax.optimization_barrier((result_copies, queries))
     header_all = lax.all_to_all(result_copies, "seq", 0, 0).reshape(
         shards, headers, lines, head_width
     )
 
-    margin_rows = REACH * BLOCK
-    extended = jnp.concatenate(
-        [
-            shift(stacked[rows - margin_rows :], "seq", 1),
-            stacked,
-            shift(stacked[:margin_rows], "seq", -1),
-        ]
-    )
-    near_keys = extended[:, :head_width]
-    near_values = extended[:, head_width:]
-    extent = rows + 2 * margin_rows
-    key_blocks = seq_place * local_blocks - REACH + jnp.arange(extent, dtype=jnp.int32) // BLOCK
-    query_blocks = seq_place * local_blocks + jnp.arange(rows, dtype=jnp.int32) // BLOCK
-    limits = jnp.repeat(block_reach, BLOCK)
-    key_header = jnp.any(header_ids[:, None] == key_blocks[None, :], axis=0)
-    allowed = (key_blocks >= 0)[None, :] & (key_blocks < total_blocks)[None, :]
-    allowed = allowed & (jnp.abs(key_blocks[None, :] - query_blocks[:, None]) <= limits[:, None])
-    allowed = allowed & jnp.logical_not(key_header)[None, :]
-    near_scores = (
-        jnp.einsum("qd,kd->qk", queries, near_keys, preferred_element_type=f32) * inverse_root
-    )
-    near_scores = jnp.where(allowed, near_scores, -jnp.inf)
-    head_scores = (
-        jnp.einsum("qd,kd->qk", queries, head_keys, preferred_element_type=f32) * inverse_root
-    )
-    scores = jnp.concatenate([near_scores, head_scores], axis=1)
-    row_top = jnp.max(scores, axis=1)
-    weights = jnp.exp(scores - row_top[:, None])
-    row_sums = jnp.sum(weights, axis=1)
-    joined = jnp.concatenate([near_values, head_values], axis=0)
-    mixed = (
-        jnp.dot(weights.astype(bf16), joined, preferred_element_type=f32) / row_sums[:, None]
-    ).astype(bf16)
+    (mixed,) = call(
+        functools.partial(window_kernel, total_blocks),
+        [((rows, head_width), bf16)],
+        [seq_place.astype(jnp.int32).reshape(1), block_reach, header_ids],
+        [queries, before, stacked, after, header_pack],
+    )
 
     blocks = []
     for b in range(local_blocks):

time: 169 us -> 160 us (0.947)
  starting transfers between devices: 74.2 us -> 67.1 us
  matrix products: 5.81 us -> 2.31 us
  other arithmetic: 6.61 us -> 3.95 us
  waiting for transfers between devices: 41.1 us -> 43.5 us
  Pallas kernels: 8.96 us -> 11.1 us
    all_to_all x1, waiting for transfers between devices: 0.01 us -> 7.24 us  [on_device(): lax.all_to_all(partial.reshape(shards, mine, 2 * head_width), 'seq', 0, 0)]
    all_to_all x1, starting transfers between devices: 13 us -> 6.55 us  [on_device(): lax.all_to_all(result_copies, 'seq', 0, 0)]
    all_to_all x1, waiting for transfers between devices: 8.4 us -> 13.6 us  [on_device(): lax.all_to_all(header_copies, 'seq', 0, 0).reshape(-1, 3 * head_width)]
    all_to_all x1, waiting for transfers between devices: 9.25 us -> 4.28 us  [on_device(): lax.all_to_all(result_copies, 'seq', 0, 0)]
    ppermute x5, waiting for transfers between devices: 13.9 us -> 9.19 us  [shift(): lax.ppermute(value, axis, [(i, (i + by) % count) for i in range(count)])]
    unnamed x41 -> x50, local copies, waits for them, and re-layouts: 5.78 us -> 9.87 us
    dot_general x3 -> x0, matrix products: 3.5 us -> none  [the longest x1 2.16 us: on_device(): jnp.dot(weights.astype(bf16), joined, preferred_element_type=f32)]
    pallas_call x6 -> x7, Pallas kernels: 8.96 us -> 11.1 us  [call(): pl.pallas_call(kernel, out_shape=[jax.ShapeDtypeStruct(shape, dtype) for...]
  transfers between devices with their start and end apart: 10 -> 10, of which waited for: 6 -> 6; matrix products, arithmetic and copies ran while one was open for 6% -> 2% of each run, Pallas kernels for 3% -> 4%
where the time goes in v5:
time: 160 us; the launch traced here: 158 us
  starting transfers between devices  67.1 us (42%)
  waiting for transfers between devices  43.5 us (27%)
  local copies, waits for them, and re-layouts  12.7 us (8%)
  blocking collectives  11.9 us (7%)
  Pallas kernels  11.1 us (7%)
  between operations  5.34 us (3%)
  other arithmetic  3.95 us (2%)
  matrix products  2.31 us (1%)
    all_to_all x1, starting transfers between devices, on_device(): spread = lax.all_to_all(picked.transpose(1, 0, 2), 'seq', 0, 0)  18.4 us
    ppermute x5, starting transfers between devices, shift(): lax.ppermute(value, axis, [(i, (i + by) % count) for i in range(count)])  16.2 us
    all_to_all x1, starting transfers between devices, on_device(): lax.all_to_all(header_copies, 'seq', 0, 0).reshape(-1, 3 * head_width)  15.5 us
    all_to_all x1, waiting for transfers between devices, on_device(): lax.all_to_all(header_copies, 'seq', 0, 0).reshape(-1, 3 * head_width)  13.6 us
    all_gather x1, blocking collectives, on_device(): gathered = lax.all_gather(attended, 'section', axis=1, tiled=True)  11.9 us
    pallas_call x7, Pallas kernels, call(): pl.pallas_call(kernel, out_shape=[jax.ShapeDtypeStruct(shape, dtype) for...  11.1 us
    unnamed x50, local copies, waits for them, and re-layouts  9.87 us
    all_to_all x1, waiting for transfers between devices, on_device(): arrived = lax.all_to_all(payload, 'section', 0, 0)  9.24 us
  transfers between devices with their start and end apart: 10, of which 6 were waited for; matrix products, arithmetic and copies ran while one was open for 2% of the time, Pallas kernels for 4%

profile of v5, /device:TPU:1, one launch (start us, length us, event | category | flops | bytes accessed | tf_op | source)
XLA Modules:
  0.0 158.1 jit_solution(9679527546199490353)
XLA Ops:
  0.8 1.2 copy-done.1
  2.0 0.9 copy-done.3
  3.9 1.2 copy-done.7
  5.8 2.2 %shard_map.82 = (bf16[1296,128]{1,0:T(8,128)(2,1)}, bf16[1296,128]{1,0:T(8,128)(2,1)S(1)}, bf16[1296,128]{1,0:T(8,128)(2,1)S(1)}, bf16[2,128,1024]{2,1,0:T(8,128...) custom-call(s32[1]{0:T(128)} %bitcast.1.place, s32[2]{0:T(128)S(1)} %copy-done.12, ...), custom_call_target="tpu_custom_call" | custom-call | tf_op jit(solution)/shard_map/pallas_call | solution.py:43
  8.0 1.3 copy.18
  9.3 18.4 %all-to-all-start = ((bf16[128,2,1024]{2,1,0:T(2,128)(2,1)}), bf16[128,2,1024]{2,1,0:T(2,128)(2,1)S(1)}, u32[]{:S(2)}, u32[]{:S(2)}) async-start(bf16[128,2,1024]{2,1,0:T(2,128)(2,1)} %bitcast.31), calls=%async_computation | async-start | bytes 1048576 | tf_op jit(solution)/shard_map/all_to_all | solution.py:319
  27.8 3.3 %collective-permute-start = (bf16[1296,128]{1,0:T(8,128)(2,1)}, bf16[1296,128]{1,0:T(8,128)(2,1)S(1)}, u32[]{:S(2)}, u32[]{:S(2)}) collective-permute-start(bf16[1296,128]{1,0:T(8,128)(2,1)} %get-tuple-element.19), channel_id=1, source_target_pairs={{0,128},{128,256},{256,384},{384,0},{1,129},{129,257},{257,385},{3... | collective-permute-start | bytes 995336 | tf_op jit(solution)/shard_map/ppermute | solution.py:20
  31.0 4.3 %collective-permute-start.1 = (bf16[1296,128]{1,0:T(8,128)(2,1)}, bf16[1296,128]{1,0:T(8,128)(2,1)S(1)}, u32[]{:S(2)}, u32[]{:S(2)}) collective-permute-start(bf16[1296,128]{1,0:T(8,128)(2,1)} %copy-done.16), channel_id=1, source_target_pairs={{0,256},{128,384},{256,0},{384,128},{1,257},{129,385},{257,1},{385... | collective-permute-start | bytes 995336 | tf_op jit(solution)/shard_map/ppermute | solution.py:20
  35.4 3.1 %collective-permute-start.2 = (bf16[1296,128]{1,0:T(8,128)(2,1)}, bf16[1296,128]{1,0:T(8,128)(2,1)}, u32[]{:S(2)}, u32[]{:S(2)}) collective-permute-start(bf16[1296,128]{1,0:T(8,128)(2,1)} %copy-done.15), channel_id=1, source_target_pairs={{0,384},{128,0},{256,128},{384,256},{1,385},{129,1},{257,129},{385... | collective-permute-start | bytes 995336 | tf_op jit(solution)/shard_map/ppermute | solution.py:20
  38.5 1.0 multiply_sine_fusion
  39.6 8.1 %collective-permute-done.1.refs_1_ = bf16[1296,128]{1,0:T(8,128)(2,1)S(1)} collective-permute-done((bf16[1296,128]{1,0:T(8,128)(2,1)}, bf16[1296,128]{1,0:T(8,128)(2,1)S(1)}, u32[]{:S(2)}, u32[]{:S(2)}) %collective-permute-start.1) | collective-permute-done | bytes 331808 | tf_op jit(solution)/shard_map/ppermute | solution.py:20
  48.4 1.1 collective-permute-done.2.refs_2_
  49.6 1.2 copy-done.8
  50.8 1.0 copy-done.10
  52.7 2.7 %shard_map.83.refs_3_ = bf16[4,784,128]{2,1,0:T(8,128)(2,1)} custom-call(s32[1]{0:T(128)} %bitcast.1.place, bf16[512,1024]{1,0:T(8,128)(2,1)S(1)} %copy-done.8, f32[1,1024]{1,0:T(1,128)S(1)} %bitcast.34, bf16[4096,128]{1,0:T(8,128)(2,1)S(1)} %copy-done.2, f32[128,256]{1,0:T(8,128)S(1)} %copy-done.18, f32[8,128]{1,0:T(8,128)S(1)} %get-tuple-element.23.squares_own, ...), custom_call_target="tpu_custom_call" | custom-call | flops 99999997952 | tf_op jit(solution)/shard_map/pallas_call | solution.py:43
  55.4 1.0 copy-done.11
  56.4 2.0 %shard_map.84 = bf16[4,784,128]{2,1,0:T(8,128)(2,1)} custom-call(s32[1]{0:T(128)} %bitcast.1.place, s32[2]{0:T(128)S(1)} %copy-done.13, bf16[128,2,1024]{2,1,0:T(2,128)(2,1)S(1)} %all-to-all-done.spread, f32[1,1024]{1,0:T(1,128)S(1)} %bitcast.35, bf16[4096,128]{1,0:T(8,128)(2,1)S(1)} %copy-done.2, ...), custom_call_target="tpu_custom_call", output_to_operand_aliasing={{}: (10, {})} | custom-call | tf_op jit(solution)/shard_map/pallas_call | solution.py:43
  58.4 4.8 %all-to-all-start.1 = ((bf16[4,784,128]{2,1,0:T(8,128)(2,1)}), bf16[4,784,128]{2,1,0:T(8,128)(2,1)S(1)}, u32[]{:S(2)}, u32[]{:S(2)}) async-start(bf16[4,784,128]{2,1,0:T(8,128)(2,1)} %shard_map.84), calls=%async_computation.1 | async-start | bytes 1605632 | tf_op jit(solution)/shard_map/all_to_all | solution.py:345
  63.8 1.2 fusion.18
  65.3 9.2 %all-to-all-done.1.arrived = bf16[4,784,128]{2,1,0:T(8,128)(2,1)S(1)} async-done(((bf16[4,784,128]{2,1,0:T(8,128)(2,1)}), bf16[4,784,128]{2,1,0:T(8,128)(2,1)S(1)}, u32[]{:S(2)}, u32[]{:S(2)}) %all-to-all-start.1) | async-done | bytes 802848 | tf_op jit(solution)/shard_map/all_to_all | solution.py:345
  75.4 15.5 %all-to-all-start.2 = ((bf16[128,2,384]{2,1,0:T(2,128)(2,1)}), bf16[128,2,384]{2,1,0:T(2,128)(2,1)S(1)}, u32[]{:S(2)}, u32[]{:S(2)}) async-start(bf16[128,2,384]{2,1,0:T(2,128)(2,1)} %shard_map.85), calls=%async_computation.2 | async-start | bytes 393216 | tf_op jit(solution)/shard_map/all_to_all | solution.py:355
  91.3 13.6 %all-to-all-done.2 = bf16[128,2,384]{2,1,0:T(2,128)(2,1)S(1)} async-done(((bf16[128,2,384]{2,1,0:T(2,128)(2,1)}), bf16[128,2,384]{2,1,0:T(2,128)(2,1)S(1)}, u32[]{:S(2)}, u32[]{:S(2)}) %all-to-all-start.2) | async-done | bytes 196640 | tf_op jit(solution)/shard_map/all_to_all | solution.py:355
  106.8 5.6 %all-to-all-start.3 = ((bf16[128,2,256]{2,1,0:T(2,128)(2,1)}), bf16[128,2,256]{2,1,0:T(2,128)(2,1)S(1)}, u32[]{:S(2)}, u32[]{:S(2)}) async-start(bf16[128,2,256]{2,1,0:T(2,128)(2,1)} %reshape.71), calls=%async_computation.3 | async-start | bytes 262144 | tf_op jit(solution)/shard_map/all_to_all | solution.py:384
  112.4 2.9 %collective-permute-start.4 = (bf16[256,256]{1,0:T(8,128)(2,1)S(1)}, bf16[256,256]{1,0:T(8,128)(2,1)S(1)}, u32[]{:S(2)}, u32[]{:S(2)}) collective-permute-start(bf16[256,256]{1,0:T(8,128)(2,1)S(1)} %get-tuple-element.31), channel_id=1, source_target_pairs={{0,127},{1,0},{2,1},{3,2},{4,3},{5,4},{6,5},{7,6},{8,7},{9,8},{10,... | collective-permute-start | bytes 393224 | tf_op jit(solution)/shard_map/ppermute | solution.py:20
  115.3 2.6 %collective-permute-start.3 = (bf16[256,256]{1,0:T(8,128)(2,1)S(1)}, bf16[256,256]{1,0:T(8,128)(2,1)S(1)}, u32[]{:S(2)}, u32[]{:S(2)}) collective-permute-start(bf16[256,256]{1,0:T(8,128)(2,1)S(1)} %get-tuple-element.32), channel_id=1, source_target_pairs={{0,1},{1,2},{2,3},{3,4},{4,5},{5,6},{6,7},{7,8},{8,9},{9,10},{10,1... | collective-permute-start | bytes 393224 | tf_op jit(solution)/shard_map/ppermute | solution.py:20
  118.0 7.2 %all-to-all-done.3.parts = bf16[128,2,256]{2,1,0:T(2,128)(2,1)S(1)} async-done(((bf16[128,2,256]{2,1,0:T(2,128)(2,1)}), bf16[128,2,256]{2,1,0:T(2,128)(2,1)S(1)}, u32[]{:S(2)}, u32[]{:S(2)}) %all-to-all-start.3) | async-done | bytes 131104 | tf_op jit(solution)/shard_map/all_to_all | solution.py:384
  125.2 1.2 shard_map.87
  126.4 6.5 %all-to-all-start.4 = ((bf16[128,2,128]{2,1,0:T(2,128)(2,1)}), bf16[128,2,128]{2,1,0:T(2,128)(2,1)S(1)}, u32[]{:S(2)}, u32[]{:S(2)}) async-start(bf16[128,2,128]{2,1,0:T(2,128)(2,1)} %shard_map.87), calls=%async_computation.4 | async-start | bytes 131072 | tf_op jit(solution)/shard_map/all_to_all | solution.py:390
  137.9 2.1 %shard_map.88 = bf16[512,128]{1,0:T(8,128)(2,1)S(1)} custom-call(s32[1]{0:T(128)} %bitcast.8.seq_place, s32[4]{0:T(128)S(1)} %copy-done.14, s32[2]{0:T(128)S(1)} %copy-done.13, bf16[512,128]{1,0:T(8,128)(2,1)S(1)} %get-tuple-element.29.queries, bf16[256,256]{1,0:T(8,128)(2,1)S(1)} %collective-permute-done.3.before, ...), custom_call_target="tpu_custom_call" | custom-call | tf_op jit(solution)/shard_map/pallas_call | solution.py:43
  140.1 4.3 %all-to-all-done.4 = bf16[128,2,128]{2,1,0:T(2,128)(2,1)S(1)} async-done(((bf16[128,2,128]{2,1,0:T(2,128)(2,1)}), bf16[128,2,128]{2,1,0:T(2,128)(2,1)S(1)}, u32[]{:S(2)}, u32[]{:S(2)}) %all-to-all-start.4) | async-done | bytes 65568 | tf_op jit(solution)/shard_map/all_to_all | solution.py:390
  144.4 11.9 %all_gather.3 = bf16[512,512]{1,0:T(8,128)(2,1)S(1)} all-gather(bf16[512,128]{1,0:T(8,128)(2,1)S(1)} %pad_maximum_fusion.3), channel_id=1, replica_groups=mesh['section'=4,'seq'=128] {'section'}, dimensions={1}, use_global_device_ids=true | all-gather | bytes 655360 | tf_op jit(solution)/shard_map/all_gather | solution.py:409
  156.4 1.7 %convolution_convert_fusion = bf16[512,1024]{1,0:T(8,128)(2,1)} fusion(bf16[512,512]{1,0:T(8,128)(2,1)S(1)} %all_gather.3, bf16[512,1024]{1,0:T(8,128)(2,1)S(1)} %copy-done), kind=kOutput, calls=%fused_computation | convolution fusion | flops 537395200 | bytes 2621440 | tf_op jit(solution)/shard_map/dot_general | solution.py:410
  (75 shorter events, 8.2 us)
Async XLA Ops:
  0.0 156.4 %copy-start = (bf16[512,1024]{1,0:T(8,128)(2,1)S(1)}, bf16[512,1024]{1,0:T(8,128)(2,1)}, u32[]{:S(2)}) copy-start(bf16[512,1024]{1,0:T(8,128)(2,1)} %param.13) | copy-start | bytes 3145732
  0.8 1.2 copy-start.1
  2.0 0.9 copy-start.3
  3.0 0.9 copy-start.5
  3.9 1.2 copy-start.7
  8.0 1.3 copy-start.15
  8.0 1.3 copy-start.16
  8.0 1.3 copy-start.17
  9.3 46.1 %all-to-all-start = ((bf16[128,2,1024]{2,1,0:T(2,128)(2,1)}), bf16[128,2,1024]{2,1,0:T(2,128)(2,1)S(1)}, u32[]{:S(2)}, u32[]{:S(2)}) async-start(bf16[128,2,1024]{2,1,0:T(2,128)(2,1)} %bitcast.31), calls=%async_computation | async-start | bytes 1048576 | tf_op jit(solution)/shard_map/all_to_all | solution.py:319
  27.7 21.8 %copy-start.2 = (bf16[4096,128]{1,0:T(8,128)(2,1)S(1)}, bf16[4096,128]{1,0:T(8,128)(2,1)}, u32[]{:S(2)}) copy-start(bf16[4096,128]{1,0:T(8,128)(2,1)} %query_weight.5) | copy-start | bytes 3145732
  27.8 11.9 %collective-permute-start = (bf16[1296,128]{1,0:T(8,128)(2,1)}, bf16[1296,128]{1,0:T(8,128)(2,1)S(1)}, u32[]{:S(2)}, u32[]{:S(2)}) collective-permute-start(bf16[1296,128]{1,0:T(8,128)(2,1)} %get-tuple-element.19), channel_id=1, source_target_pairs={{0,128},{128,256},{256,384},{384,0},{1,129},{129,257},{257,385},{3... | collective-permute-start | bytes 995336 | tf_op jit(solution)/shard_map/ppermute | solution.py:20
  31.0 16.7 %collective-permute-start.1 = (bf16[1296,128]{1,0:T(8,128)(2,1)}, bf16[1296,128]{1,0:T(8,128)(2,1)S(1)}, u32[]{:S(2)}, u32[]{:S(2)}) collective-permute-start(bf16[1296,128]{1,0:T(8,128)(2,1)} %copy-done.16), channel_id=1, source_target_pairs={{0,256},{128,384},{256,0},{384,128},{1,257},{129,385},{257,1},{385... | collective-permute-start | bytes 995336 | tf_op jit(solution)/shard_map/ppermute | solution.py:20
  35.4 14.2 %collective-permute-start.2 = (bf16[1296,128]{1,0:T(8,128)(2,1)}, bf16[1296,128]{1,0:T(8,128)(2,1)}, u32[]{:S(2)}, u32[]{:S(2)}) collective-permute-start(bf16[1296,128]{1,0:T(8,128)(2,1)} %copy-done.15), channel_id=1, source_target_pairs={{0,384},{128,0},{256,128},{384,256},{1,385},{129,1},{257,129},{385... | collective-permute-start | bytes 995336 | tf_op jit(solution)/shard_map/ppermute | solution.py:20
  39.5 10.1 %copy-start.19 = (f32[512,64]{1,0:T(8,128)}, f32[512,64]{1,0:T(8,128)S(1)}, u32[]{:S(2)}) copy-start(f32[512,64]{1,0:T(8,128)S(1)} %get-tuple-element.36) | copy-start | bytes 393220
  39.5 10.1 %copy-start.21 = (f32[512,64]{1,0:T(8,128)}, f32[512,64]{1,0:T(8,128)S(1)}, u32[]{:S(2)}) copy-start(f32[512,64]{1,0:T(8,128)S(1)} %get-tuple-element.37) | copy-start | bytes 393220
  39.5 10.1 %copy-start.23 = (f32[512,64]{1,0:T(8,128)}, f32[512,64]{1,0:T(8,128)S(1)}, u32[]{:S(2)}) copy-start(f32[512,64]{1,0:T(8,128)S(1)} %get-tuple-element.38) | copy-start | bytes 393220
  49.6 1.2 copy-start.8
  50.8 1.0 copy-start.10
  52.7 2.7 %copy-start.4 = (bf16[1024,128]{1,0:T(8,128)(2,1)S(1)}, bf16[1024,128]{1,0:T(8,128)(2,1)}, u32[]{:S(2)}) copy-start(bf16[1024,128]{1,0:T(8,128)(2,1)} %key_weight.3) | copy-start | bytes 786436
  52.7 2.7 %copy-start.6 = (bf16[1024,128]{1,0:T(8,128)(2,1)S(1)}, bf16[1024,128]{1,0:T(8,128)(2,1)}, u32[]{:S(2)}) copy-start(bf16[1024,128]{1,0:T(8,128)(2,1)} %value_weight.3) | copy-start | bytes 786436
  52.7 2.7 %copy-start.13 = (s32[2]{0:T(128)S(1)}, s32[2]{0:T(128)}, u32[]{:S(2)}) copy-start(s32[2]{0:T(128)} %header_ids.5) | copy-start | bytes 28
  55.4 1.0 copy-start.11
  58.4 32.6 %copy-start.20 = (f32[512,64]{1,0:T(8,128)S(1)}, f32[512,64]{1,0:T(8,128)}, u32[]{:S(2)}) copy-start(f32[512,64]{1,0:T(8,128)} %copy-done.19) | copy-start | bytes 393220
  58.4 32.6 %copy-start.22 = (f32[512,64]{1,0:T(8,128)S(1)}, f32[512,64]{1,0:T(8,128)}, u32[]{:S(2)}) copy-start(f32[512,64]{1,0:T(8,128)} %copy-done.21) | copy-start | bytes 393220
  58.4 32.6 %copy-start.24 = (f32[512,64]{1,0:T(8,128)S(1)}, f32[512,64]{1,0:T(8,128)}, u32[]{:S(2)}) copy-start(f32[512,64]{1,0:T(8,128)} %copy-done.23) | copy-start | bytes 393220
  58.4 16.1 %all-to-all-start.1 = ((bf16[4,784,128]{2,1,0:T(8,128)(2,1)}), bf16[4,784,128]{2,1,0:T(8,128)(2,1)S(1)}, u32[]{:S(2)}, u32[]{:S(2)}) async-start(bf16[4,784,128]{2,1,0:T(8,128)(2,1)} %shard_map.84), calls=%async_computation.1 | async-start | bytes 1605632 | tf_op jit(solution)/shard_map/all_to_all | solution.py:345
  75.4 29.5 %all-to-all-start.2 = ((bf16[128,2,384]{2,1,0:T(2,128)(2,1)}), bf16[128,2,384]{2,1,0:T(2,128)(2,1)S(1)}, u32[]{:S(2)}, u32[]{:S(2)}) async-start(bf16[128,2,384]{2,1,0:T(2,128)(2,1)} %shard_map.85), calls=%async_computation.2 | async-start | bytes 393216 | tf_op jit(solution)/shard_map/all_to_all | solution.py:355
  105.8 32.1 %copy-start.14 = (s32[4]{0:T(128)S(1)}, s32[4]{0:T(128)}, u32[]{:S(2)}) copy-start(s32[4]{0:T(128)} %reach.1) | copy-start | bytes 52
  106.8 18.4 %all-to-all-start.3 = ((bf16[128,2,256]{2,1,0:T(2,128)(2,1)}), bf16[128,2,256]{2,1,0:T(2,128)(2,1)S(1)}, u32[]{:S(2)}, u32[]{:S(2)}) async-start(bf16[128,2,256]{2,1,0:T(2,128)(2,1)} %reshape.71), calls=%async_computation.3 | async-start | bytes 262144 | tf_op jit(solution)/shard_map/all_to_all | solution.py:384
  112.4 25.5 %collective-permute-start.4 = (bf16[256,256]{1,0:T(8,128)(2,1)S(1)}, bf16[256,256]{1,0:T(8,128)(2,1)S(1)}, u32[]{:S(2)}, u32[]{:S(2)}) collective-permute-start(bf16[256,256]{1,0:T(8,128)(2,1)S(1)} %get-tuple-element.31), channel_id=1, source_target_pairs={{0,127},{1,0},{2,1},{3,2},{4,3},{5,4},{6,5},{7,6},{8,7},{9,8},{10,... | collective-permute-start | bytes 393224 | tf_op jit(solution)/shard_map/ppermute | solution.py:20
  115.3 22.6 %collective-permute-start.3 = (bf16[256,256]{1,0:T(8,128)(2,1)S(1)}, bf16[256,256]{1,0:T(8,128)(2,1)S(1)}, u32[]{:S(2)}, u32[]{:S(2)}) collective-permute-start(bf16[256,256]{1,0:T(8,128)(2,1)S(1)} %get-tuple-element.32), channel_id=1, source_target_pairs={{0,1},{1,2},{2,3},{3,4},{4,5},{5,6},{6,7},{7,8},{8,9},{9,10},{10,1... | collective-permute-start | bytes 393224 | tf_op jit(solution)/shard_map/ppermute | solution.py:20
  126.4 17.9 %all-to-all-start.4 = ((bf16[128,2,128]{2,1,0:T(2,128)(2,1)}), bf16[128,2,128]{2,1,0:T(2,128)(2,1)S(1)}, u32[]{:S(2)}, u32[]{:S(2)}) async-start(bf16[128,2,128]{2,1,0:T(2,128)(2,1)} %shard_map.87), calls=%async_computation.4 | async-start | bytes 131072 | tf_op jit(solution)/shard_map/all_to_all | solution.py:390
  (3 other events, 2.3 us)

commit v6 on v5

v6 whole, which is shorter than its diff:
```python
import functools
import math

import jax
import jax.numpy as jnp
from jax import lax
from jax.experimental import pallas as pl
from jax.experimental.pallas import tpu as pltpu
from jax.sharding import PartitionSpec as P

BLOCK = 128
REACH = 2

EPSILON = 1e-05
THETA = 500000.0


def shift(value, axis, by):
    count = lax.axis_size(axis)
    return lax.ppermute(value, axis, [(i, (i + by) % count) for i in range(count)])


def tables(positions, head_width):
    middle = head_width // 2
    frequency = jnp.exp(
        -(2.0 / head_width) * math.log(THETA) * jnp.arange(middle, dtype=jnp.float32)
    )
    angles = positions.astype(jnp.float32)[:, None] * frequency[None, :]
    cosine, sine = jnp.cos(angles), jnp.sin(angles)
    return jnp.concatenate([cosine, cosine], axis=1), jnp.concatenate([-sine, sine], axis=1)

BF16, F32 = jnp.bfloat16, jnp.float32
VMEM_LIMIT = 24 * 1024 * 1024


def call(kernel, outs, scalars, arrays, scratch=()):
    whole = pl.BlockSpec(memory_space=pltpu.VMEM)
    specs = [pl.BlockSpec(memory_space=pltpu.SMEM)] * len(scalars)
    specs += [whole] * len(arrays)
    return pl.pallas_call(
        kernel,
        out_shape=[jax.ShapeDtypeStruct(shape, dtype) for shape, dtype in outs],
        in_specs=specs,
        out_specs=[whole] * len(outs),
        scratch_shapes=list(scratch),
        compiler_params=pltpu.CompilerParams(vmem_limit_bytes=VMEM_LIMIT),
    )(*scalars, *arrays)


def turn(values, cosine, signed_sine):
    return values * cosine + pltpu.roll(values, values.shape[1] // 2, axis=1) * signed_sine


def spread_down(row, size):
    return jnp.transpose(jnp.broadcast_to(row, (size, size)))


def outgoing_kernel(sections, x, gain, query_weight, key_weight, value_weight, out, keyval, rows16):
    rows, part = x.shape
    size = BLOCK
    count = rows // size
    keyval_weight = jnp.concatenate([key_weight[...], value_weight[...]], axis=1)
    rows16[...] = jnp.zeros_like(rows16)
    for b in range(count):
        block = x[b * size : (b + 1) * size, :].astype(F32)
        total = jnp.sum(block * block, axis=1, keepdims=True)
        line = jnp.transpose(jnp.broadcast_to(total, (size, size)))[0:1, :]
        high = line.astype(BF16).astype(F32)
        rows16[b : b + 1, :] = high
        rows16[count + b : count + b + 1, :] = line - high
        block = block * gain[...]
        high = block.astype(BF16)
        low = (block - high.astype(F32)).astype(BF16)
        both = jnp.dot(
            jnp.concatenate([high, low], axis=0), keyval_weight, preferred_element_type=F32
        )
        keyval[b * size : (b + 1) * size, :] = (both[:size] + both[size:]).astype(BF16)
    width = keyval.shape[1] // 2
    for target in range(sections):
        out[target, 0:part, :] = query_weight[target * part : (target + 1) * part, :]
        block = keyval[target * size : (target + 1) * size, :]
        out[target, part : part + size, :] = block[:, :width]
        out[target, part + size : part + 2 * size, :] = block[:, width:]
        out[target, part + 2 * size : part + 2 * size + 16, :] = rows16[...].astype(BF16)


def partial_kernel(sections, place, x, gain, arrived, cosine, sine, out, squares, normed):
    rows, part = x.shape
    size = BLOCK
    count = rows // size
    head_width = arrived.shape[2]
    tail = jnp.sum(arrived[:, part + 2 * size : part + 2 * size + 16, :].astype(F32), axis=0)
    squares[0:count, :] = lax.rsqrt(
        (tail[0:count, :] + tail[count : 2 * count, :]) / (part * sections) + EPSILON
    )
    for b in range(count):
        scale = spread_down(squares[b : b + 1, :], size)
        scale = jnp.concatenate([scale] * (part // size), axis=1)
        block = x[b * size : (b + 1) * size, :].astype(F32) * scale * gain[...]
        normed[b * size : (b + 1) * size, :] = block.astype(BF16)
    for k in range(0, sections, 2):
        pair = jnp.concatenate([arrived[k, 0:part, :], arrived[k + 1, 0:part, :]], axis=1)
        value = jnp.dot(normed[...], pair, preferred_element_type=F32).astype(BF16)
        out[k, 0:rows, :] = value[:, :head_width]
        out[k + 1, 0:rows, :] = value[:, head_width:]
    scale = spread_down(squares[pl.ds(place[0], 1), :], size)
    keys = jnp.sum(arrived[:, part : part + size, :].astype(F32), axis=0)
    keys = turn(keys * scale, cosine[...], sine[...]).astype(BF16)
    values = jnp.sum(arrived[:, part + size : part + 2 * size, :].astype(F32), axis=0)
    values = (values * scale).astype(BF16)
    for target in range(sections):
        out[target, rows : rows + size, :] = keys
        out[target, rows + size : rows + 2 * size, :] = values


def finish_kernel(header_ids, arrived, cosine, sine, queries, keyval, picked):
    rows, head_width = queries.shape
    size = BLOCK
    count = rows // size
    for b in range(count):
        part = slice(b * size, (b + 1) * size)
        total = jnp.sum(arrived[:, part, :].astype(F32), axis=0)
        queries[part, :] = turn(total, cosine[part, :], sine[part, :]).astype(BF16)
        keyval[part, 0:head_width] = arrived[b, rows : rows + size, :]
        keyval[part, head_width:] = arrived[b, rows + size : rows + 2 * size, :]
    for h in range(picked.shape[0] // size):
        start = pl.multiple_of(lax.rem(header_ids[h], count) * size, size)
        picked[h * size : (h + 1) * size, 0:head_width] = queries[pl.ds(start, size), :]
        picked[h * size : (h + 1) * size, head_width:] = keyval[pl.ds(start, size), :]


def repeat_kernel(seq_place, header_ids, local_blocks, spread, out):
    header = lax.div(seq_place[0] * spread.shape[1], BLOCK)
    rows = spread[lax.div(header_ids[header], local_blocks[0])]
    out[...] = jnp.broadcast_to(rows[None], out.shape)


def window_kernel(
    total_blocks, seq_place, reach, header_ids, queries, before, here, after, header, out
):
    rows, head_width = queries.shape
    size = BLOCK
    count = rows // size
    parts = [before[j * size : (j + 1) * size, :] for j in range(REACH)]
    parts += [here[j * size : (j + 1) * size, :] for j in range(count)]
    parts += [after[j * size : (j + 1) * size, :] for j in range(REACH)]
    head_keys = header[:, head_width : 2 * head_width]
    head_values = header[:, 2 * head_width :]
    for b in range(count):
        near = parts[b : b + 2 * REACH + 1]
        keys = jnp.concatenate([part[:, :head_width] for part in near] + [head_keys], axis=0)
        values = jnp.concatenate([part[:, head_width:] for part in near] + [head_values], axis=0)
        scores = lax.dot_general(
            queries[b * size : (b + 1) * size, :],
            keys,
            (((1,), (1,)), ((), ())),
            preferred_element_type=F32,
        ) * (1.0 / math.sqrt(head_width))
        pieces = []
        for j in range(2 * REACH + 1):
            block = seq_place[0] * count + b + j - REACH
            allowed = (block >= 0) & (block < total_blocks) & (abs(j - REACH) <= reach[b])
            for h in range(2):
                allowed = allowed & (block != header_ids[h])
            pieces.append(
                jnp.where(allowed, scores[:, j * size : (j + 1) * size], -jnp.inf)
            )
        pieces.append(scores[:, (2 * REACH + 1) * size :])
        scores = jnp.concatenate(pieces, axis=1)
        weights = jnp.exp(scores - jnp.max(scores, axis=1, keepdims=True))
        total = jnp.sum(weights, axis=1, keepdims=True)
        mixed = jnp.dot(weights.astype(BF16), values, preferred_element_type=F32)
        out[b * size : (b + 1) * size, :] = (mixed / total).astype(BF16)


def merge_kernel(parts, out):
    head_width = out.shape[2]
    everything = parts[...].astype(F32)
    level = everything[:, :, head_width:]
    level = level[:, :, 0:1] + level[:, :, 32:33] + level[:, :, 64:65]
    factor = jnp.exp(level - jnp.max(level, axis=0, keepdims=True))
    total = jnp.sum(everything[:, :, :head_width] * factor, axis=0)
    result = (total / jnp.sum(factor, axis=0)).astype(BF16)
    out[...] = jnp.broadcast_to(result[None], out.shape)


def on_device(
    hidden,
    norm_gain,
    query_weight,
    key_weight,
    value_weight,
    output_weight,
    block_reach,
    header_ids,
):
    bf16, f32 = jnp.bfloat16, jnp.float32
    rows, part = hidden.shape
    head_width = key_weight.shape[1]
    sections = lax.axis_size("section")
    shards = lax.axis_size("seq")
    local_blocks = rows // BLOCK
    total_blocks = local_blocks * shards
    section_place = lax.axis_index("section")
    seq_place = lax.axis_index("seq")
    headers = header_ids.shape[0]
    mine = headers * BLOCK // shards
    gain = norm_gain.astype(f32)[None, :]

    places = [place.astype(jnp.int32).reshape(1) for place in (section_place, seq_place)]
    tall = part + 2 * BLOCK + 16
    (outgoing,) = call(
        functools.partial(outgoing_kernel, sections),
        [((sections, tall, head_width), bf16)],
        [],
        [hidden, gain, query_weight, key_weight, value_weight],
        [pltpu.VMEM((rows, 2 * head_width), bf16), pltpu.VMEM((16, head_width), f32)],
    )
    incoming = lax.all_to_all(outgoing, "section", 0, 0)
    own_positions = seq_place * rows + jnp.arange(rows, dtype=jnp.int32)
    own_tables = tables(own_positions, head_width)
    block_tables = [
        lax.dynamic_slice_in_dim(table, section_place * BLOCK, BLOCK, axis=0)
        for table in own_tables
    ]
    (payload,) = call(
        functools.partial(partial_kernel, sections),
        [((sections, rows + 2 * BLOCK, head_width), bf16)],
        [places[0]],
        [hidden, gain, incoming, *block_tables],
        [pltpu.VMEM((8, head_width), f32), pltpu.VMEM((rows, part), bf16)],
    )
    arrived = lax.all_to_all(payload, "section", 0, 0)
    queries, stacked, picked = call(
        finish_kernel,
        [
            ((rows, head_width), bf16),
            ((rows, 2 * head_width), bf16),
            ((headers * BLOCK, 3 * head_width), bf16),
        ],
        [header_ids],
        [arrived, *own_tables],
    )

    spread = lax.all_to_all(picked.reshape(shards, mine, 3 * head_width), "seq", 0, 0)
    (header_copies,) = call(
        repeat_kernel,
        [((shards, mine, 3 * head_width), bf16)],
        [places[1], header_ids, jnp.full((1,), local_blocks, jnp.int32)],
        [spread],
    )
    header_copies, edges = lax.optimization_barrier((header_copies, stacked))
    header_pack = lax.all_to_all(header_copies, "seq", 0, 0).reshape(-1, 3 * head_width)
    margin_rows = REACH * BLOCK
    before = shift(edges[rows - margin_rows :], "seq", 1)
    after = shift(edges[:margin_rows], "seq", -1)
    keys, values = stacked[:, :head_width], stacked[:, head_width:]
    head_queries = header_pack[:, :head_width]
    head_keys = header_pack[:, head_width : 2 * head_width]
    head_values = header_pack[:, 2 * head_width :]

    inverse_root = 1.0 / math.sqrt(head_width)
    far_scores = (
        jnp.einsum("qd,kd->qk", head_queries, keys, preferred_element_type=f32) * inverse_root
    )
    far_max = jnp.max(far_scores, axis=1, keepdims=True)
    far_weights = jnp.exp(far_scores - far_max)
    far_total = jnp.sum(far_weights, axis=1, keepdims=True)
    far_out = jnp.dot(far_weights.astype(bf16), values, preferred_element_type=f32) / far_total
    far_level = far_max + jnp.log(far_total)
    first = far_level.astype(bf16).astype(f32)
    second = (far_level - first).astype(bf16).astype(f32)
    third = far_level - first - second
    lane = lax.broadcasted_iota(jnp.int32, far_out.shape, 1)
    level = jnp.where(lane < 32, first, jnp.where(lane < 64, second, third))
    partial = jnp.concatenate([far_out, level], axis=1).astype(bf16)
    partial, queries = lax.optimization_barrier((partial, queries))
    parts = lax.all_to_all(partial.reshape(shards, mine, 2 * head_width), "seq", 0, 0)
    (result_copies,) = call(merge_kernel, [((shards, mine, head_width), bf16)], [], [parts])
    header_all = lax.all_to_all(result_copies, "seq", 0, 0).reshape(
        headers, BLOCK, head_width
    )

    (mixed,) = call(
        functools.partial(window_kernel, total_blocks),
        [((rows, head_width), bf16)],
        [places[1], block_reach, header_ids],
        [queries, before, stacked, after, header_pack],
    )

    blocks = []
    for b in range(local_blocks):
        block = mixed[b * BLOCK : (b + 1) * BLOCK]
        for h in range(headers):
            here = header_ids[h] == seq_place * local_blocks + b
            block = jnp.where(here, header_all[h], block)
        blocks.append(block)
    attended = jnp.concatenate(blocks, axis=0)
    gathered = lax.all_gather(attended, "section", axis=1, tiled=True)
    return jnp.dot(gathered, output_weight, preferred_element_type=f32).astype(bf16)


def solution(mesh):
    return jax.shard_map(
        on_device,
        mesh=mesh,
        in_specs=(
            P("seq", "section"),
            P("section"),
            P(None, "section"),
            P("section", None),
            P("section", None),
            P(None, "section"),
            P("seq"),
            P(),
        ),
        out_specs=P("seq", "section"),
        check_vma=False,
    )
```

time: 160 us -> 157 us (0.981)
  blocking collectives: 11.9 us -> 52.4 us
  starting transfers between devices: 67.1 us -> 32.9 us
  Pallas kernels: 11.1 us -> 6.77 us
  local copies, waits for them, and re-layouts: 12.7 us -> 10.1 us
    all_to_all x0 -> x1, blocking collectives: none -> 40.5 us  [on_device(): lax.all_to_all(picked.reshape(shards, mine, 3 * head_width), 'seq', 0, 0)]
    all_to_all x1, starting transfers between devices: 18.4 us -> 4.84 us  [on_device(): incoming = lax.all_to_all(outgoing, 'section', 0, 0)]
    ppermute x5 -> x2, starting transfers between devices: 16.2 us -> 5.47 us  [shift(): lax.ppermute(value, axis, [(i, (i + by) % count) for i in range(count)])]
    all_to_all x1, waiting for transfers between devices: 0.01 us -> 10.2 us  [on_device(): incoming = lax.all_to_all(outgoing, 'section', 0, 0)]
    all_to_all x1, starting transfers between devices: 15.5 us -> 5.56 us  [on_device(): lax.all_to_all(header_copies, 'seq', 0, 0).reshape(-1, 3 * head_width)]
    ppermute x5 -> x2, waiting for transfers between devices: 9.19 us -> 0.01 us  [shift(): lax.ppermute(value, axis, [(i, (i + by) % count) for i in range(count)])]
    pallas_call x7 -> x6, Pallas kernels: 11.1 us -> 6.77 us  [call(): pl.pallas_call(kernel, out_shape=[jax.ShapeDtypeStruct(shape, dtype) for...]
    unnamed x50 -> x36, local copies, waits for them, and re-layouts: 9.87 us -> 8.47 us
  transfers between devices with their start and end apart: 10 -> 7, of which waited for: 6 -> 5; matrix products, arithmetic and copies ran while one was open for 2% -> 1% of each run, Pallas kernels for 4% -> 2%
where the time goes in v6:
time: 157 us; the launch traced here: 156 us
  blocking collectives  52.4 us (33%)
  waiting for transfers between devices  43.5 us (28%)
  starting transfers between devices  32.9 us (21%)
  local copies, waits for them, and re-layouts  10.1 us (6%)
  Pallas kernels  6.77 us (4%)
  between operations  5.23 us (3%)
  other arithmetic  2.49 us (2%)
  matrix products  2.3 us (1%)
    all_to_all x1, blocking collectives, on_device(): lax.all_to_all(picked.reshape(shards, mine, 3 * head_width), 'seq', 0, 0)  40.5 us
    all_to_all x1, waiting for transfers between devices, on_device(): lax.all_to_all(header_copies, 'seq', 0, 0).reshape(-1, 3 * head_width)  14.1 us
    all_gather x1, blocking collectives, on_device(): gathered = lax.all_gather(attended, 'section', axis=1, tiled=True)  11.9 us
    all_to_all x1, waiting for transfers between devices, on_device(): incoming = lax.all_to_all(outgoing, 'section', 0, 0)  10.2 us
    unnamed x36, local copies, waits for them, and re-layouts  8.47 us
    all_to_all x1, waiting for transfers between devices, on_device(): arrived = lax.all_to_all(payload, 'section', 0, 0)  8.06 us
    all_to_all x1, starting transfers between devices, on_device(): lax.all_to_all(result_copies, 'seq', 0, 0)  7.82 us
    all_to_all x1, waiting for transfers between devices, on_device(): lax.all_to_all(partial.reshape(shards, mine, 2 * head_width), 'seq', 0, 0)  7.33 us
  transfers between devices with their start and end apart: 7, of which 5 were waited for; matrix products, arithmetic and copies ran while one was open for 1% of the time, Pallas kernels for 2%

profile of v6, /device:TPU:1, one launch (start us, length us, event | category | flops | bytes accessed | tf_op | source)
XLA Modules:
  0.0 155.7 jit_solution(18037684223517304572)
XLA Ops:
  0.0 0.8 broadcast_in_dim.38
  0.8 1.2 copy-done.2
  2.0 1.2 copy-done.5
  3.2 0.9 copy-done.6
  4.2 0.9 copy-done.7
  5.1 0.8 shard_map.82
  5.9 1.1 copy-done.1
  7.6 4.8 %all-to-all-start = ((bf16[4,1296,128]{2,1,0:T(8,128)(2,1)}), bf16[4,1296,128]{2,1,0:T(8,128)(2,1)S(1)}, u32[]{:S(2)}, u32[]{:S(2)}) async-start(bf16[4,1296,128]{2,1,0:T(8,128)(2,1)} %copy-done.1), calls=%async_computation | async-start | bytes 2654208 | tf_op jit(solution)/shard_map/all_to_all | solution.py:219
  12.4 1.0 multiply_sine_fusion
  13.5 0.7 copy-done.12
  14.4 10.2 %all-to-all-done.arrived = bf16[4,1296,128]{2,1,0:T(8,128)(2,1)S(1)} async-done(((bf16[4,1296,128]{2,1,0:T(8,128)(2,1)}), bf16[4,1296,128]{2,1,0:T(8,128)(2,1)S(1)}, u32[]{:S(2)}, u32[]{:S(2)}) %all-to-all-start) | async-done | bytes 1327136 | tf_op jit(solution)/shard_map/all_to_all | solution.py:219
  24.7 0.7 copy-done.9
  25.4 0.8 shard_map.83
  26.2 0.9 copy-done.4
  27.1 3.6 %all-to-all-start.1 = ((bf16[4,768,128]{2,1,0:T(8,128)(2,1)}), bf16[4,768,128]{2,1,0:T(8,128)(2,1)S(1)}, u32[]{:S(2)}, u32[]{:S(2)}) async-start(bf16[4,768,128]{2,1,0:T(8,128)(2,1)} %copy-done.4), calls=%async_computation.1 | async-start | bytes 1572864 | tf_op jit(solution)/shard_map/all_to_all | solution.py:233
  30.9 8.1 %all-to-all-done.1.arrived = bf16[4,768,128]{2,1,0:T(8,128)(2,1)S(1)} async-done(((bf16[4,768,128]{2,1,0:T(8,128)(2,1)}), bf16[4,768,128]{2,1,0:T(8,128)(2,1)S(1)}, u32[]{:S(2)}, u32[]{:S(2)}) %all-to-all-start.1) | async-done | bytes 786464 | tf_op jit(solution)/shard_map/all_to_all | solution.py:233
  39.0 0.7 shard_map.84
  39.8 40.5 %all_to_all.30.spread = bf16[128,2,384]{2,1,0:T(2,128)(2,1)S(1)} all-to-all(bf16[128,2,384]{2,1,0:T(2,128)(2,1)S(1)} %reshape.62), channel_id=1, replica_groups=mesh['section'=4,'seq'=128] {'seq'}, dimensions={0} | all-to-all | bytes 393216 | tf_op jit(solution)/shard_map/all_to_all | solution.py:245
  80.3 1.3 shard_map.85
  81.6 5.6 %all-to-all-start.3 = ((bf16[128,2,384]{2,1,0:T(2,128)(2,1)}), bf16[128,2,384]{2,1,0:T(2,128)(2,1)S(1)}, u32[]{:S(2)}, u32[]{:S(2)}) async-start(bf16[128,2,384]{2,1,0:T(2,128)(2,1)} %shard_map.85), calls=%async_computation.3 | async-start | bytes 393216 | tf_op jit(solution)/shard_map/all_to_all | solution.py:253
  87.2 14.1 %all-to-all-done.3 = bf16[128,2,384]{2,1,0:T(2,128)(2,1)S(1)} async-done(((bf16[128,2,384]{2,1,0:T(2,128)(2,1)}), bf16[128,2,384]{2,1,0:T(2,128)(2,1)S(1)}, u32[]{:S(2)}, u32[]{:S(2)}) %all-to-all-start.3) | async-done | bytes 196640 | tf_op jit(solution)/shard_map/all_to_all | solution.py:253
  102.4 0.7 reshape.64
  103.2 5.6 %all-to-all-start.4 = ((bf16[128,2,256]{2,1,0:T(2,128)(2,1)}), bf16[128,2,256]{2,1,0:T(2,128)(2,1)S(1)}, u32[]{:S(2)}, u32[]{:S(2)}) async-start(bf16[128,2,256]{2,1,0:T(2,128)(2,1)} %reshape.64), calls=%async_computation.4 | async-start | bytes 262144 | tf_op jit(solution)/shard_map/all_to_all | solution.py:278
  108.8 3.5 %collective-permute-start = (bf16[256,256]{1,0:T(8,128)(2,1)S(1)}, bf16[256,256]{1,0:T(8,128)(2,1)S(1)}, u32[]{:S(2)}, u32[]{:S(2)}) collective-permute-start(bf16[256,256]{1,0:T(8,128)(2,1)S(1)} %get-tuple-element.20), channel_id=1, source_target_pairs={{0,1},{1,2},{2,3},{3,4},{4,5},{5,6},{6,7},{7,8},{8,9},{9,10},{10,1... | collective-permute-start | bytes 393224 | tf_op jit(solution)/shard_map/ppermute | solution.py:20
  112.3 1.9 %collective-permute-start.1 = (bf16[256,256]{1,0:T(8,128)(2,1)S(1)}, bf16[256,256]{1,0:T(8,128)(2,1)S(1)}, u32[]{:S(2)}, u32[]{:S(2)}) collective-permute-start(bf16[256,256]{1,0:T(8,128)(2,1)S(1)} %get-tuple-element.19), channel_id=1, source_target_pairs={{0,127},{1,0},{2,1},{3,2},{4,3},{5,4},{6,5},{7,6},{8,7},{9,8},{10,... | collective-permute-start | bytes 393224 | tf_op jit(solution)/shard_map/ppermute | solution.py:20
  114.2 7.3 %all-to-all-done.4.parts = bf16[128,2,256]{2,1,0:T(2,128)(2,1)S(1)} async-done(((bf16[128,2,256]{2,1,0:T(2,128)(2,1)}), bf16[128,2,256]{2,1,0:T(2,128)(2,1)S(1)}, u32[]{:S(2)}, u32[]{:S(2)}) %all-to-all-start.4) | async-done | bytes 131104 | tf_op jit(solution)/shard_map/all_to_all | solution.py:278
  121.6 1.2 shard_map.86
  122.7 7.8 %all-to-all-start.5 = ((bf16[128,2,128]{2,1,0:T(2,128)(2,1)}), bf16[128,2,128]{2,1,0:T(2,128)(2,1)S(1)}, u32[]{:S(2)}, u32[]{:S(2)}) async-start(bf16[128,2,128]{2,1,0:T(2,128)(2,1)} %shard_map.86), calls=%async_computation.5 | async-start | bytes 131072 | tf_op jit(solution)/shard_map/all_to_all | solution.py:280
  136.1 2.1 %shard_map.87 = bf16[512,128]{1,0:T(8,128)(2,1)S(1)} custom-call(s32[1]{0:T(128)} %bitcast.1.seq_place, s32[4]{0:T(128)S(1)} %copy-done.11, s32[2]{0:T(128)S(1)} %copy-done.10, bf16[512,128]{1,0:T(8,128)(2,1)S(1)} %get-tuple-element.17.queries, bf16[256,256]{1,0:T(8,128)(2,1)S(1)} %collective-permute-done.before, ...), custom_call_target="tpu_custom_call" | custom-call | tf_op jit(solution)/shard_map/pallas_call | solution.py:40
  138.2 3.7 %all-to-all-done.5 = bf16[128,2,128]{2,1,0:T(2,128)(2,1)S(1)} async-done(((bf16[128,2,128]{2,1,0:T(2,128)(2,1)}), bf16[128,2,128]{2,1,0:T(2,128)(2,1)S(1)}, u32[]{:S(2)}, u32[]{:S(2)}) %all-to-all-start.5) | async-done | bytes 65568 | tf_op jit(solution)/shard_map/all_to_all | solution.py:280
  142.0 11.9 %all_gather.3 = bf16[512,512]{1,0:T(8,128)(2,1)S(1)} all-gather(bf16[512,128]{1,0:T(8,128)(2,1)S(1)} %pad_maximum_fusion.3), channel_id=1, replica_groups=mesh['section'=4,'seq'=128] {'section'}, dimensions={1}, use_global_device_ids=true | all-gather | bytes 655360 | tf_op jit(solution)/shard_map/all_gather | solution.py:299
  154.0 1.7 %convolution_convert_fusion = bf16[512,1024]{1,0:T(8,128)(2,1)} fusion(bf16[512,512]{1,0:T(8,128)(2,1)S(1)} %all_gather.3, bf16[512,1024]{1,0:T(8,128)(2,1)S(1)} %copy-done), kind=kOutput, calls=%fused_computation | convolution fusion | flops 537395200 | bytes 2621440 | tf_op jit(solution)/shard_map/dot_general | solution.py:300
  (50 shorter events, 3.1 us)
Async XLA Ops:
  0.0 154.0 %copy-start = (bf16[512,1024]{1,0:T(8,128)(2,1)S(1)}, bf16[512,1024]{1,0:T(8,128)(2,1)}, u32[]{:S(2)}) copy-start(bf16[512,1024]{1,0:T(8,128)(2,1)} %param.13) | copy-start | bytes 3145732
  0.8 1.2 copy-start.2
  2.0 1.2 copy-start.5
  3.2 0.9 copy-start.6
  4.2 0.9 copy-start.7
  5.9 1.1 copy-start.1
  7.0 0.6 copy-start.8
  7.6 17.1 %all-to-all-start = ((bf16[4,1296,128]{2,1,0:T(8,128)(2,1)}), bf16[4,1296,128]{2,1,0:T(8,128)(2,1)S(1)}, u32[]{:S(2)}, u32[]{:S(2)}) async-start(bf16[4,1296,128]{2,1,0:T(8,128)(2,1)} %copy-done.1), calls=%async_computation | async-start | bytes 2654208 | tf_op jit(solution)/shard_map/all_to_all | solution.py:219
  12.4 12.3 %copy-start.3 = (bf16[512,1024]{1,0:T(8,128)(2,1)S(1)}, bf16[512,1024]{1,0:T(8,128)(2,1)}, u32[]{:S(2)}) copy-start(bf16[512,1024]{1,0:T(8,128)(2,1)} %x.3) | copy-start | bytes 3145732
  13.4 0.7 copy-start.12
  13.4 0.8 copy-start.14
  13.5 0.9 copy-start.16
  24.7 0.7 copy-start.9
  26.2 0.9 copy-start.4
  27.0 3.7 %copy-start.13 = (f32[512,64]{1,0:T(8,128)S(1)}, f32[512,64]{1,0:T(8,128)}, u32[]{:S(2)}) copy-start(f32[512,64]{1,0:T(8,128)} %copy-done.12) | copy-start | bytes 393220
  27.0 3.7 %copy-start.15 = (f32[512,64]{1,0:T(8,128)S(1)}, f32[512,64]{1,0:T(8,128)}, u32[]{:S(2)}) copy-start(f32[512,64]{1,0:T(8,128)} %copy-done.14) | copy-start | bytes 393220
  27.0 3.7 %copy-start.17 = (f32[512,64]{1,0:T(8,128)S(1)}, f32[512,64]{1,0:T(8,128)}, u32[]{:S(2)}) copy-start(f32[512,64]{1,0:T(8,128)} %copy-done.16) | copy-start | bytes 393220
  27.0 12.0 %copy-start.10 = (s32[2]{0:T(128)S(1)}, s32[2]{0:T(128)}, u32[]{:S(2)}) copy-start(s32[2]{0:T(128)} %header_ids.5) | copy-start | bytes 28
  27.1 11.9 %all-to-all-start.1 = ((bf16[4,768,128]{2,1,0:T(8,128)(2,1)}), bf16[4,768,128]{2,1,0:T(8,128)(2,1)S(1)}, u32[]{:S(2)}, u32[]{:S(2)}) async-start(bf16[4,768,128]{2,1,0:T(8,128)(2,1)} %copy-done.4), calls=%async_computation.1 | async-start | bytes 1572864 | tf_op jit(solution)/shard_map/all_to_all | solution.py:233
  81.6 19.7 %all-to-all-start.3 = ((bf16[128,2,384]{2,1,0:T(2,128)(2,1)}), bf16[128,2,384]{2,1,0:T(2,128)(2,1)S(1)}, u32[]{:S(2)}, u32[]{:S(2)}) async-start(bf16[128,2,384]{2,1,0:T(2,128)(2,1)} %shard_map.85), calls=%async_computation.3 | async-start | bytes 393216 | tf_op jit(solution)/shard_map/all_to_all | solution.py:253
  101.9 34.2 %copy-start.11 = (s32[4]{0:T(128)S(1)}, s32[4]{0:T(128)}, u32[]{:S(2)}) copy-start(s32[4]{0:T(128)} %reach.1) | copy-start | bytes 52
  103.2 18.4 %all-to-all-start.4 = ((bf16[128,2,256]{2,1,0:T(2,128)(2,1)}), bf16[128,2,256]{2,1,0:T(2,128)(2,1)S(1)}, u32[]{:S(2)}, u32[]{:S(2)}) async-start(bf16[128,2,256]{2,1,0:T(2,128)(2,1)} %reshape.64), calls=%async_computation.4 | async-start | bytes 262144 | tf_op jit(solution)/shard_map/all_to_all | solution.py:278
  108.8 27.3 %collective-permute-start = (bf16[256,256]{1,0:T(8,128)(2,1)S(1)}, bf16[256,256]{1,0:T(8,128)(2,1)S(1)}, u32[]{:S(2)}, u32[]{:S(2)}) collective-permute-start(bf16[256,256]{1,0:T(8,128)(2,1)S(1)} %get-tuple-element.20), channel_id=1, source_target_pairs={{0,1},{1,2},{2,3},{3,4},{4,5},{5,6},{6,7},{7,8},{8,9},{9,10},{10,1... | collective-permute-start | bytes 393224 | tf_op jit(solution)/shard_map/ppermute | solution.py:20
  112.3 23.8 %collective-permute-start.1 = (bf16[256,256]{1,0:T(8,128)(2,1)S(1)}, bf16[256,256]{1,0:T(8,128)(2,1)S(1)}, u32[]{:S(2)}, u32[]{:S(2)}) collective-permute-start(bf16[256,256]{1,0:T(8,128)(2,1)S(1)} %get-tuple-element.19), channel_id=1, source_target_pairs={{0,127},{1,0},{2,1},{3,2},{4,3},{5,4},{6,5},{7,6},{8,7},{9,8},{10,... | collective-permute-start | bytes 393224 | tf_op jit(solution)/shard_map/ppermute | solution.py:20
  122.7 19.2 %all-to-all-start.5 = ((bf16[128,2,128]{2,1,0:T(2,128)(2,1)}), bf16[128,2,128]{2,1,0:T(2,128)(2,1)S(1)}, u32[]{:S(2)}, u32[]{:S(2)}) async-start(bf16[128,2,128]{2,1,0:T(2,128)(2,1)} %shard_map.86), calls=%async_computation.5 | async-start | bytes 131072 | tf_op jit(solution)/shard_map/all_to_all | solution.py:280

commit v7 on v6

--- a/solution.py
+++ b/solution.py
@@ -173,6 +173,24 @@
         out[b * size : (b + 1) * size, :] = (mixed / total).astype(BF16)
 
 
+def place_kernel(seq_place, header_ids, attended, weight, _, out, block, semaphore):
+    size = BLOCK
+    count = out.shape[0] // size
+    for h in range(2):
+
+        @pl.when(lax.div(header_ids[h], count) == seq_place[0])
+        def _():
+            rows = slice(h * size, (h + 1) * size)
+            left = jnp.concatenate(
+                [attended[s, rows, :] for s in range(attended.shape[0])], axis=1
+            )
+            block[...] = jnp.dot(left, weight[...], preferred_element_type=F32).astype(BF16)
+            start = pl.multiple_of(lax.rem(header_ids[h], count) * size, size)
+            copy = pltpu.make_async_copy(block, out.at[pl.ds(start, size), :], semaphore)
+            copy.start()
+            copy.wait()
+
+
 def merge_kernel(parts, out):
     head_width = out.shape[2]
     everything = parts[...].astype(F32)
@@ -274,30 +292,38 @@
     lane = lax.broadcasted_iota(jnp.int32, far_out.shape, 1)
     level = jnp.where(lane < 32, first, jnp.where(lane < 64, second, third))
     partial = jnp.concatenate([far_out, level], axis=1).astype(bf16)
-    partial, queries = lax.optimization_barrier((partial, queries))
+    partial, queries, before, after = lax.optimization_barrier(
+        (partial, queries, before, after)
+    )
     parts = lax.all_to_all(partial.reshape(shards, mine, 2 * head_width), "seq", 0, 0)
-    (result_copies,) = call(merge_kernel, [((shards, mine, head_width), bf16)], [], [parts])
-    header_all = lax.all_to_all(result_copies, "seq", 0, 0).reshape(
-        headers, BLOCK, head_width
-    )
-
+    everywhere = sections * shards
     (mixed,) = call(
         functools.partial(window_kernel, total_blocks),
         [((rows, head_width), bf16)],
         [places[1], block_reach, header_ids],
         [queries, before, stacked, after, header_pack],
     )
-
-    blocks = []
-    for b in range(local_blocks):
-        block = mixed[b * BLOCK : (b + 1) * BLOCK]
-        for h in range(headers):
-            here = header_ids[h] == seq_place * local_blocks + b
-            block = jnp.where(here, header_all[h], block)
-        blocks.append(block)
-    attended = jnp.concatenate(blocks, axis=0)
-    gathered = lax.all_gather(attended, "section", axis=1, tiled=True)
-    return jnp.dot(gathered, output_weight, preferred_element_type=f32).astype(bf16)
+    (result_copies,) = call(
+        merge_kernel, [((everywhere, mine, head_width), bf16)], [], [parts]
+    )
+    result_copies, mixed = lax.optimization_barrier((result_copies, mixed))
+    header_all = lax.all_to_all(result_copies, ("section", "seq"), 0, 0).reshape(
+        sections, headers * BLOCK, head_width
+    )
+    gathered = lax.all_gather(mixed, "section", axis=1, tiled=True)
+    result = jnp.dot(gathered, output_weight, preferred_element_type=f32).astype(bf16)
+    whole = pl.BlockSpec(memory_space=pltpu.VMEM)
+    scalar = pl.BlockSpec(memory_space=pltpu.SMEM)
+    anywhere = pl.BlockSpec(memory_space=pl.ANY)
+    return pl.pallas_call(
+        place_kernel,
+        out_shape=jax.ShapeDtypeStruct(result.shape, bf16),
+        in_specs=[scalar, scalar, whole, whole, anywhere],
+        out_specs=anywhere,
+        scratch_shapes=[pltpu.VMEM((BLOCK, result.shape[1]), bf16), pltpu.SemaphoreType.DMA],
+        input_output_aliases={4: 0},
+        compiler_params=pltpu.CompilerParams(vmem_limit_bytes=VMEM_LIMIT),
+    )(places[1], header_ids, header_all, output_weight, result)
 
 
 def solution(mesh):

time: 157 us -> 153 us (0.975)
  between operations: 5.23 us -> 0.35 us
  local copies, waits for them, and re-layouts: 10.1 us -> 5.35 us
  waiting for transfers between devices: 43.5 us -> 39.3 us
  starting transfers between devices: 32.9 us -> 36.4 us
  blocking collectives: 52.4 us -> 55.2 us
  Pallas kernels: 6.77 us -> 9.48 us
    all_to_all x1, waiting for transfers between devices: 14.1 us -> 8.84 us  [on_device(): lax.all_to_all(header_copies, 'seq', 0, 0).reshape(-1, 3 * head_width)]
    unnamed x36 -> x16, local copies, waits for them, and re-layouts: 8.47 us -> 4.36 us
    all_to_all x1, waiting for transfers between devices: 7.33 us -> 10.6 us  [on_device(): lax.all_to_all(partial.reshape(shards, mine, 2 * head_width), 'seq', 0, 0)]
    all_to_all x1, waiting for transfers between devices: 3.73 us -> 0.61 us  [on_device(): lax.all_to_all(result_copies, ('section', 'seq'), 0, 0)]
    all_gather x1, blocking collectives: 11.9 us -> 14.7 us  [on_device(): gathered = lax.all_gather(mixed, 'section', axis=1, tiled=True)]
    all_to_all x1, starting transfers between devices: 5.56 us -> 8.09 us  [on_device(): lax.all_to_all(partial.reshape(shards, mine, 2 * head_width), 'seq', 0, 0)]
    pallas_call x6, Pallas kernels: 6.77 us -> 8.91 us  [call(): pl.pallas_call(kernel, out_shape=[jax.ShapeDtypeStruct(shape, dtype) for...]
  transfers between devices with their start and end apart: 7 -> 7, of which waited for: 5 -> 5; matrix products, arithmetic and copies ran while one was open for 1% -> 3% of each run, Pallas kernels for 2% -> 1%
where the time goes in v7:
time: 153 us; the launch traced here: 151 us
  blocking collectives  55.2 us (36%)
  waiting for transfers between devices  39.3 us (26%)
  starting transfers between devices  36.4 us (24%)
  Pallas kernels  9.48 us (6%)
  local copies, waits for them, and re-layouts  5.35 us (3%)
  other arithmetic  2.36 us (2%)
  matrix products  2.31 us (2%)
    all_to_all x1, blocking collectives, on_device(): lax.all_to_all(picked.reshape(shards, mine, 3 * head_width), 'seq', 0, 0)  40.5 us
    all_gather x1, blocking collectives, on_device(): gathered = lax.all_gather(mixed, 'section', axis=1, tiled=True)  14.7 us
    all_to_all x1, waiting for transfers between devices, on_device(): incoming = lax.all_to_all(outgoing, 'section', 0, 0)  11.1 us
    all_to_all x1, waiting for transfers between devices, on_device(): lax.all_to_all(partial.reshape(shards, mine, 2 * head_width), 'seq', 0, 0)  10.6 us
    pallas_call x6, Pallas kernels, call(): pl.pallas_call(kernel, out_shape=[jax.ShapeDtypeStruct(shape, dtype) for...  8.91 us
    all_to_all x1, waiting for transfers between devices, on_device(): lax.all_to_all(header_copies, 'seq', 0, 0).reshape(-1, 3 * head_width)  8.84 us
    all_to_all x1, starting transfers between devices, on_device(): lax.all_to_all(result_copies, ('section', 'seq'), 0, 0)  8.76 us
    all_to_all x1, waiting for transfers between devices, on_device(): arrived = lax.all_to_all(payload, 'section', 0, 0)  8.09 us
  transfers between devices with their start and end apart: 7, of which 5 were waited for; matrix products, arithmetic and copies ran while one was open for 3% of the time, Pallas kernels for 1%

profile of v7, /device:TPU:1, one launch (start us, length us, event | category | flops | bytes accessed | tf_op | source)
XLA Modules:
  0.0 150.7 jit_solution(15041463350197440624)
XLA Ops:
  0.0 0.7 broadcast_in_dim.38
  0.7 1.2 copy-done
  1.9 1.2 copy-done.2
  3.1 0.9 copy-done.4
  4.1 0.9 copy-done.5
  5.0 1.9 %shard_map.82 = bf16[4,1296,128]{2,1,0:T(8,128)(2,1)} custom-call(bf16[512,1024]{1,0:T(8,128)(2,1)S(1)} %copy-done, f32[1,1024]{1,0:T(1,128)S(1)} %bitcast.7, bf16[4096,128]{1,0:T(8,128)(2,1)S(1)} %copy-done.2, bf16[1024,128]{1,0:T(8,128)(2,1)S(1)} %copy-done.4, bf16[1024,128]{1,0:T(8,128)(2,1)S(1)} %copy-done.5), custom_call_target="tpu_custom_call" | custom-call | tf_op jit(solution)/shard_map/pallas_call | solution.py:40
  6.9 4.8 %all-to-all-start = ((bf16[4,1296,128]{2,1,0:T(8,128)(2,1)}), bf16[4,1296,128]{2,1,0:T(8,128)(2,1)S(1)}, u32[]{:S(2)}, u32[]{:S(2)}) async-start(bf16[4,1296,128]{2,1,0:T(8,128)(2,1)} %shard_map.82), calls=%async_computation | async-start | bytes 2654208 | tf_op jit(solution)/shard_map/all_to_all | solution.py:237
  11.8 1.0 multiply_sine_fusion
  12.9 11.1 %all-to-all-done.arrived = bf16[4,1296,128]{2,1,0:T(8,128)(2,1)S(1)} async-done(((bf16[4,1296,128]{2,1,0:T(8,128)(2,1)}), bf16[4,1296,128]{2,1,0:T(8,128)(2,1)S(1)}, u32[]{:S(2)}, u32[]{:S(2)}) %all-to-all-start) | async-done | bytes 1327136 | tf_op jit(solution)/shard_map/all_to_all | solution.py:237
  24.0 1.6 %shard_map.83 = bf16[4,768,128]{2,1,0:T(8,128)(2,1)} custom-call(s32[1]{0:T(128)} %bitcast.1.place, bf16[512,1024]{1,0:T(8,128)(2,1)S(1)} %copy-done.1, f32[1,1024]{1,0:T(1,128)S(1)} %bitcast.8, bf16[4,1296,128]{2,1,0:T(8,128)(2,1)S(1)} %all-to-all-done.arrived, f32[128,128]{1,0:T(8,128)S(1)} %get-tuple-element.37.cosine, f32[128,128]{1,0:T(8,128)S(1)} %get-tuple-element.36.sine), custom_call_target="tpu_custom_call" | custom-call | tf_op jit(solution)/shard_map/pallas_call | solution.py:40
  25.7 3.6 %all-to-all-start.1 = ((bf16[4,768,128]{2,1,0:T(8,128)(2,1)}), bf16[4,768,128]{2,1,0:T(8,128)(2,1)S(1)}, u32[]{:S(2)}, u32[]{:S(2)}) async-start(bf16[4,768,128]{2,1,0:T(8,128)(2,1)} %shard_map.83), calls=%async_computation.1 | async-start | bytes 1572864 | tf_op jit(solution)/shard_map/all_to_all | solution.py:251
  29.5 8.1 %all-to-all-done.1.arrived = bf16[4,768,128]{2,1,0:T(8,128)(2,1)S(1)} async-done(((bf16[4,768,128]{2,1,0:T(8,128)(2,1)}), bf16[4,768,128]{2,1,0:T(8,128)(2,1)S(1)}, u32[]{:S(2)}, u32[]{:S(2)}) %all-to-all-start.1) | async-done | bytes 786464 | tf_op jit(solution)/shard_map/all_to_all | solution.py:251
  37.6 0.7 shard_map.84
  38.4 40.5 %all_to_all.30.spread = bf16[128,2,384]{2,1,0:T(2,128)(2,1)S(1)} all-to-all(bf16[128,2,384]{2,1,0:T(2,128)(2,1)S(1)} %reshape.60), channel_id=1, replica_groups=mesh['section'=4,'seq'=128] {'seq'}, dimensions={0} | all-to-all | bytes 393216 | tf_op jit(solution)/shard_map/all_to_all | solution.py:263
  78.9 1.3 shard_map.85
  80.2 5.6 %all-to-all-start.3 = ((bf16[128,2,384]{2,1,0:T(2,128)(2,1)}), bf16[128,2,384]{2,1,0:T(2,128)(2,1)S(1)}, u32[]{:S(2)}, u32[]{:S(2)}) async-start(bf16[128,2,384]{2,1,0:T(2,128)(2,1)} %shard_map.85), calls=%async_computation.3 | async-start | bytes 393216 | tf_op jit(solution)/shard_map/all_to_all | solution.py:271
  85.8 3.5 %collective-permute-start = (bf16[256,256]{1,0:T(8,128)(2,1)S(1)}, bf16[256,256]{1,0:T(8,128)(2,1)S(1)}, u32[]{:S(2)}, u32[]{:S(2)}) collective-permute-start(bf16[256,256]{1,0:T(8,128)(2,1)S(1)} %get-tuple-element.28), channel_id=1, source_target_pairs={{0,1},{1,2},{2,3},{3,4},{4,5},{5,6},{6,7},{7,8},{8,9},{9,10},{10,1... | collective-permute-start | bytes 393224 | tf_op jit(solution)/shard_map/ppermute | solution.py:20
  89.3 1.9 %collective-permute-start.1 = (bf16[256,256]{1,0:T(8,128)(2,1)S(1)}, bf16[256,256]{1,0:T(8,128)(2,1)S(1)}, u32[]{:S(2)}, u32[]{:S(2)}) collective-permute-start(bf16[256,256]{1,0:T(8,128)(2,1)S(1)} %get-tuple-element.27), channel_id=1, source_target_pairs={{0,127},{1,0},{2,1},{3,2},{4,3},{5,4},{6,5},{7,6},{8,7},{9,8},{10,... | collective-permute-start | bytes 393224 | tf_op jit(solution)/shard_map/ppermute | solution.py:20
  91.2 8.8 %all-to-all-done.3 = bf16[128,2,384]{2,1,0:T(2,128)(2,1)S(1)} async-done(((bf16[128,2,384]{2,1,0:T(2,128)(2,1)}), bf16[128,2,384]{2,1,0:T(2,128)(2,1)S(1)}, u32[]{:S(2)}, u32[]{:S(2)}) %all-to-all-start.3) | async-done | bytes 196640 | tf_op jit(solution)/shard_map/all_to_all | solution.py:271
  100.2 0.3 fusion.14
  100.5 0.2 fusion.1
  100.7 0.3 fusion
  101.3 0.7 reshape.62
  102.0 8.1 %all-to-all-start.4 = ((bf16[128,2,256]{2,1,0:T(2,128)(2,1)}), bf16[128,2,256]{2,1,0:T(2,128)(2,1)S(1)}, u32[]{:S(2)}, u32[]{:S(2)}) async-start(bf16[128,2,256]{2,1,0:T(2,128)(2,1)} %reshape.62), calls=%async_computation.4 | async-start | bytes 262144 | tf_op jit(solution)/shard_map/all_to_all | solution.py:298
  110.2 2.1 %shard_map.87 = bf16[512,128]{1,0:T(8,128)(2,1)S(1)} custom-call(s32[1]{0:T(128)} %bitcast.seq_place, s32[4]{0:T(128)S(1)} %copy-done.7, s32[2]{0:T(128)S(1)} %copy-done.6, bf16[512,128]{1,0:T(8,128)(2,1)S(1)} %get-tuple-element.22.queries, bf16[256,256]{1,0:T(8,128)(2,1)S(1)} %collective-permute-done.before, bf16[512,256]{1,0:T(8,128)(2,1)S(1)} %get-tuple-element.20.here, ...), custom_call_target="tpu_custom_call" | custom-call | tf_op jit(solution)/shard_map/pallas_call | solution.py:40
  112.3 10.6 %all-to-all-done.4.parts = bf16[128,2,256]{2,1,0:T(2,128)(2,1)S(1)} async-done(((bf16[128,2,256]{2,1,0:T(2,128)(2,1)}), bf16[128,2,256]{2,1,0:T(2,128)(2,1)S(1)}, u32[]{:S(2)}, u32[]{:S(2)}) %all-to-all-start.4) | async-done | bytes 131104 | tf_op jit(solution)/shard_map/all_to_all | solution.py:298
  122.9 1.3 shard_map.86
  124.2 8.8 %all-to-all-start.5 = ((bf16[512,2,128]{2,1,0:T(2,128)(2,1)}), bf16[512,2,128]{2,1,0:T(2,128)(2,1)S(1)}, u32[]{:S(2)}, u32[]{:S(2)}) async-start(bf16[512,2,128]{2,1,0:T(2,128)(2,1)} %shard_map.86), calls=%async_computation.5 | async-start | bytes 524288 | tf_op jit(solution)/shard_map/all_to_all | solution.py:310
  133.0 14.7 %all_gather.3 = bf16[512,512]{1,0:T(8,128)(2,1)S(1)} all-gather(bf16[512,128]{1,0:T(8,128)(2,1)S(1)} %shard_map.87), channel_id=1, replica_groups=mesh['section'=4,'seq'=128] {'section'}, dimensions={1}, use_global_device_ids=true | all-gather | bytes 655360 | tf_op jit(solution)/shard_map/all_gather | solution.py:313
  147.6 1.7 %convolution_convert_fusion._ = bf16[512,1024]{1,0:T(8,128)(2,1)} fusion(bf16[512,512]{1,0:T(8,128)(2,1)S(1)} %all_gather.3, bf16[512,1024]{1,0:T(8,128)(2,1)S(1)} %copy-done.3), kind=kOutput, calls=%fused_computation | convolution fusion | flops 537395200 | bytes 2621440 | tf_op jit(solution)/shard_map/dot_general | solution.py:314
  149.3 0.6 all-to-all-done.5
  149.9 0.6 shard_map.88
  (27 shorter events, 0.8 us)
Async XLA Ops:
  0.7 1.2 copy-start
  1.9 1.2 copy-start.2
  3.1 0.9 copy-start.4
  4.1 0.9 copy-start.5
  6.9 17.1 %all-to-all-start = ((bf16[4,1296,128]{2,1,0:T(8,128)(2,1)}), bf16[4,1296,128]{2,1,0:T(8,128)(2,1)S(1)}, u32[]{:S(2)}, u32[]{:S(2)}) async-start(bf16[4,1296,128]{2,1,0:T(8,128)(2,1)} %shard_map.82), calls=%async_computation | async-start | bytes 2654208 | tf_op jit(solution)/shard_map/all_to_all | solution.py:237
  11.7 12.3 %copy-start.1 = (bf16[512,1024]{1,0:T(8,128)(2,1)S(1)}, bf16[512,1024]{1,0:T(8,128)(2,1)}, u32[]{:S(2)}) copy-start(bf16[512,1024]{1,0:T(8,128)(2,1)} %x.3) | copy-start | bytes 3145732
  25.7 11.9 %copy-start.6 = (s32[2]{0:T(128)S(1)}, s32[2]{0:T(128)}, u32[]{:S(2)}) copy-start(s32[2]{0:T(128)} %header_ids.7) | copy-start | bytes 28
  25.7 11.9 %all-to-all-start.1 = ((bf16[4,768,128]{2,1,0:T(8,128)(2,1)}), bf16[4,768,128]{2,1,0:T(8,128)(2,1)S(1)}, u32[]{:S(2)}, u32[]{:S(2)}) async-start(bf16[4,768,128]{2,1,0:T(8,128)(2,1)} %shard_map.83), calls=%async_computation.1 | async-start | bytes 1572864 | tf_op jit(solution)/shard_map/all_to_all | solution.py:251
  80.2 19.9 %all-to-all-start.3 = ((bf16[128,2,384]{2,1,0:T(2,128)(2,1)}), bf16[128,2,384]{2,1,0:T(2,128)(2,1)S(1)}, u32[]{:S(2)}, u32[]{:S(2)}) async-start(bf16[128,2,384]{2,1,0:T(2,128)(2,1)} %shard_map.85), calls=%async_computation.3 | async-start | bytes 393216 | tf_op jit(solution)/shard_map/all_to_all | solution.py:271
  85.8 15.4 %collective-permute-start = (bf16[256,256]{1,0:T(8,128)(2,1)S(1)}, bf16[256,256]{1,0:T(8,128)(2,1)S(1)}, u32[]{:S(2)}, u32[]{:S(2)}) collective-permute-start(bf16[256,256]{1,0:T(8,128)(2,1)S(1)} %get-tuple-element.28), channel_id=1, source_target_pairs={{0,1},{1,2},{2,3},{3,4},{4,5},{5,6},{6,7},{7,8},{8,9},{9,10},{10,1... | collective-permute-start | bytes 393224 | tf_op jit(solution)/shard_map/ppermute | solution.py:20
  89.3 11.9 %collective-permute-start.1 = (bf16[256,256]{1,0:T(8,128)(2,1)S(1)}, bf16[256,256]{1,0:T(8,128)(2,1)S(1)}, u32[]{:S(2)}, u32[]{:S(2)}) collective-permute-start(bf16[256,256]{1,0:T(8,128)(2,1)S(1)} %get-tuple-element.27), channel_id=1, source_target_pairs={{0,127},{1,0},{2,1},{3,2},{4,3},{5,4},{6,5},{7,6},{8,7},{9,8},{10,... | collective-permute-start | bytes 393224 | tf_op jit(solution)/shard_map/ppermute | solution.py:20
  100.5 9.7 %copy-start.7 = (s32[4]{0:T(128)S(1)}, s32[4]{0:T(128)}, u32[]{:S(2)}) copy-start(s32[4]{0:T(128)} %reach.1) | copy-start | bytes 52
  102.0 20.8 %all-to-all-start.4 = ((bf16[128,2,256]{2,1,0:T(2,128)(2,1)}), bf16[128,2,256]{2,1,0:T(2,128)(2,1)S(1)}, u32[]{:S(2)}, u32[]{:S(2)}) async-start(bf16[128,2,256]{2,1,0:T(2,128)(2,1)} %reshape.62), calls=%async_computation.4 | async-start | bytes 262144 | tf_op jit(solution)/shard_map/all_to_all | solution.py:298
  110.1 37.5 %copy-start.3 = (bf16[512,1024]{1,0:T(8,128)(2,1)S(1)}, bf16[512,1024]{1,0:T(8,128)(2,1)}, u32[]{:S(2)}) copy-start(bf16[512,1024]{1,0:T(8,128)(2,1)} %weight.1) | copy-start | bytes 3145732
  124.2 25.8 %all-to-all-start.5 = ((bf16[512,2,128]{2,1,0:T(2,128)(2,1)}), bf16[512,2,128]{2,1,0:T(2,128)(2,1)S(1)}, u32[]{:S(2)}, u32[]{:S(2)}) async-start(bf16[512,2,128]{2,1,0:T(2,128)(2,1)} %shard_map.86), calls=%async_computation.5 | async-start | bytes 524288 | tf_op jit(solution)/shard_map/all_to_all | solution.py:310

commit v8 on v7

--- a/solution.py
+++ b/solution.py
@@ -33,7 +33,7 @@
 VMEM_LIMIT = 24 * 1024 * 1024
 
 
-def call(kernel, outs, scalars, arrays, scratch=()):
+def call(kernel, outs, scalars, arrays, scratch=(), flops=0):
     whole = pl.BlockSpec(memory_space=pltpu.VMEM)
     specs = [pl.BlockSpec(memory_space=pltpu.SMEM)] * len(scalars)
     specs += [whole] * len(arrays)
@@ -44,6 +44,9 @@
         out_specs=[whole] * len(outs),
         scratch_shapes=list(scratch),
         compiler_params=pltpu.CompilerParams(vmem_limit_bytes=VMEM_LIMIT),
+        cost_estimate=(
+            pl.CostEstimate(flops=flops, bytes_accessed=0, transcendentals=0) if flops else None
+        ),
     )(*scalars, *arrays)
 
 
@@ -55,13 +58,53 @@
     return jnp.transpose(jnp.broadcast_to(row, (size, size)))
 
 
-def outgoing_kernel(sections, x, gain, query_weight, key_weight, value_weight, out, keyval, rows16):
+def outgoing_kernel(
+    sections,
+    gain,
+    hidden,
+    query_weight,
+    key_weight,
+    value_weight,
+    out,
+    x,
+    keyval_weight,
+    tail,
+    rows16,
+    block_sems,
+    weight_sems,
+    direct_sems,
+    tail_sem,
+):
     rows, part = x.shape
     size = BLOCK
     count = rows // size
-    keyval_weight = jnp.concatenate([key_weight[...], value_weight[...]], axis=1)
+    width = key_weight.shape[1]
+    loads = [
+        pltpu.make_async_copy(key_weight, keyval_weight.at[0], weight_sems.at[0]),
+        pltpu.make_async_copy(value_weight, keyval_weight.at[1], weight_sems.at[1]),
+    ]
+    blocks = [
+        pltpu.make_async_copy(
+            hidden.at[pl.ds(b * size, size), :], x.at[pl.ds(b * size, size), :], block_sems.at[b]
+        )
+        for b in range(count)
+    ]
+    direct = [
+        pltpu.make_async_copy(
+            query_weight.at[pl.ds(t * part, part), :],
+            out.at[t, pl.ds(0, part), :],
+            direct_sems.at[t],
+        )
+        for t in range(sections)
+    ]
+    for copy in loads + blocks + direct:
+        copy.start()
     rows16[...] = jnp.zeros_like(rows16)
+    for copy in loads:
+        copy.wait()
+    both_weights = jnp.concatenate([keyval_weight[0], keyval_weight[1]], axis=1)
     for b in range(count):
+        blocks[b].wait()
         block = x[b * size : (b + 1) * size, :].astype(F32)
         total = jnp.sum(block * block, axis=1, keepdims=True)
         line = jnp.transpose(jnp.broadcast_to(total, (size, size)))[0:1, :]
@@ -72,16 +115,18 @@
         high = block.astype(BF16)
         low = (block - high.astype(F32)).astype(BF16)
         both = jnp.dot(
-            jnp.concatenate([high, low], axis=0), keyval_weight, preferred_element_type=F32
+            jnp.concatenate([high, low], axis=0), both_weights, preferred_element_type=F32
         )
-        keyval[b * size : (b + 1) * size, :] = (both[:size] + both[size:]).astype(BF16)
-    width = keyval.shape[1] // 2
-    for target in range(sections):
-        out[target, 0:part, :] = query_weight[target * part : (target + 1) * part, :]
-        block = keyval[target * size : (target + 1) * size, :]
-        out[target, part : part + size, :] = block[:, :width]
-        out[target, part + size : part + 2 * size, :] = block[:, width:]
-        out[target, part + 2 * size : part + 2 * size + 16, :] = rows16[...].astype(BF16)
+        both = (both[:size] + both[size:]).astype(BF16)
+        tail[b, 0:size, :] = both[:, :width]
+        tail[b, size : 2 * size, :] = both[:, width:]
+    for t in range(sections):
+        tail[t, 2 * size : 2 * size + 16, :] = rows16[...].astype(BF16)
+    last = pltpu.make_async_copy(tail, out.at[:, pl.ds(part, 2 * size + 16), :], tail_sem)
+    last.start()
+    for copy in direct:
+        copy.wait()
+    last.wait()
 
 
 def partial_kernel(sections, place, x, gain, arrived, cosine, sine, out, squares, normed):
@@ -170,7 +215,29 @@
         weights = jnp.exp(scores - jnp.max(scores, axis=1, keepdims=True))
         total = jnp.sum(weights, axis=1, keepdims=True)
         mixed = jnp.dot(weights.astype(BF16), values, preferred_element_type=F32)
-        out[b * size : (b + 1) * size, :] = (mixed / total).astype(BF16)
+        mixed = (mixed / total).astype(BF16)
+        out[b * size : (b + 1) * size, :] = jnp.concatenate([mixed, mixed], axis=1)
+
+
+def far_kernel(header, keyval, out):
+    head_width = header.shape[1] // 3
+    scores = lax.dot_general(
+        header[:, 0:head_width],
+        keyval[:, 0:head_width],
+        (((1,), (1,)), ((), ())),
+        preferred_element_type=F32,
+    ) * (1.0 / math.sqrt(head_width))
+    top = jnp.max(scores, axis=1, keepdims=True)
+    weights = jnp.exp(scores - top)
+    total = jnp.sum(weights, axis=1, keepdims=True)
+    mixed = jnp.dot(weights.astype(BF16), keyval[:, head_width:], preferred_element_type=F32)
+    level = jnp.broadcast_to(top + jnp.log(total), mixed.shape)
+    first = level.astype(BF16).astype(F32)
+    second = (level - first).astype(BF16).astype(F32)
+    lane = lax.broadcasted_iota(jnp.int32, mixed.shape, 1)
+    level = jnp.where(lane < 32, first, jnp.where(lane < 64, second, level - first - second))
+    out[:, 0:head_width] = (mixed / total).astype(BF16)
+    out[:, head_width:] = level.astype(BF16)
 
 
 def place_kernel(seq_place, header_ids, attended, weight, _, out, block, semaphore):
@@ -227,13 +294,23 @@
 
     places = [place.astype(jnp.int32).reshape(1) for place in (section_place, seq_place)]
     tall = part + 2 * BLOCK + 16
-    (outgoing,) = call(
+    hbm = pl.BlockSpec(memory_space=pltpu.HBM)
+    outgoing = pl.pallas_call(
         functools.partial(outgoing_kernel, sections),
-        [((sections, tall, head_width), bf16)],
-        [],
-        [hidden, gain, query_weight, key_weight, value_weight],
-        [pltpu.VMEM((rows, 2 * head_width), bf16), pltpu.VMEM((16, head_width), f32)],
-    )
+        out_shape=jax.ShapeDtypeStruct((sections, tall, head_width), bf16),
+        in_specs=[pl.BlockSpec(memory_space=pltpu.VMEM)] + [hbm] * 4,
+        out_specs=hbm,
+        scratch_shapes=[
+            pltpu.VMEM((rows, part), bf16),
+            pltpu.VMEM((2, part, head_width), bf16),
+            pltpu.VMEM((sections, tall - part, head_width), bf16),
+            pltpu.VMEM((16, head_width), f32),
+            pltpu.SemaphoreType.DMA((local_blocks,)),
+            pltpu.SemaphoreType.DMA((2,)),
+            pltpu.SemaphoreType.DMA((sections,)),
+            pltpu.SemaphoreType.DMA,
+        ],
+    )(gain, hidden, query_weight, key_weight, value_weight)
     incoming = lax.all_to_all(outgoing, "section", 0, 0)
     own_positions = seq_place * rows + jnp.arange(rows, dtype=jnp.int32)
     own_tables = tables(own_positions, head_width)
@@ -272,26 +349,12 @@
     margin_rows = REACH * BLOCK
     before = shift(edges[rows - margin_rows :], "seq", 1)
     after = shift(edges[:margin_rows], "seq", -1)
-    keys, values = stacked[:, :head_width], stacked[:, head_width:]
-    head_queries = header_pack[:, :head_width]
-    head_keys = header_pack[:, head_width : 2 * head_width]
-    head_values = header_pack[:, 2 * head_width :]
-
-    inverse_root = 1.0 / math.sqrt(head_width)
-    far_scores = (
-        jnp.einsum("qd,kd->qk", head_queries, keys, preferred_element_type=f32) * inverse_root
-    )
-    far_max = jnp.max(far_scores, axis=1, keepdims=True)
-    far_weights = jnp.exp(far_scores - far_max)
-    far_total = jnp.sum(far_weights, axis=1, keepdims=True)
-    far_out = jnp.dot(far_weights.astype(bf16), values, preferred_element_type=f32) / far_total
-    far_level = far_max + jnp.log(far_total)
-    first = far_level.astype(bf16).astype(f32)
-    second = (far_level - first).astype(bf16).astype(f32)
-    third = far_level - first - second
-    lane = lax.broadcasted_iota(jnp.int32, far_out.shape, 1)
-    level = jnp.where(lane < 32, first, jnp.where(lane < 64, second, third))
-    partial = jnp.concatenate([far_out, level], axis=1).astype(bf16)
+    (partial,) = call(
+        far_kernel,
+        [((headers * BLOCK, 2 * head_width), bf16)],
+        [],
+        [header_pack, stacked],
+    )
     partial, queries, before, after = lax.optimization_barrier(
         (partial, queries, before, after)
     )
@@ -299,18 +362,19 @@
     everywhere = sections * shards
     (mixed,) = call(
         functools.partial(window_kernel, total_blocks),
-        [((rows, head_width), bf16)],
+        [((rows, 2 * head_width), bf16)],
         [places[1], block_reach, header_ids],
         [queries, before, stacked, after, header_pack],
     )
     (result_copies,) = call(
-        merge_kernel, [((everywhere, mine, head_width), bf16)], [], [parts]
-    )
-    result_copies, mixed = lax.optimization_barrier((result_copies, mixed))
+        merge_kernel, [((everywhere, mine, head_width), bf16)], [], [parts], flops=10**11
+    )
+    result_copies, _ = lax.optimization_barrier((result_copies, mixed))
     header_all = lax.all_to_all(result_copies, ("section", "seq"), 0, 0).reshape(
         sections, headers * BLOCK, head_width
     )
-    gathered = lax.all_gather(mixed, "section", axis=1, tiled=True)
+    gathered = lax.all_gather(mixed, "section")
+    gathered = jnp.concatenate([gathered[k, :, :head_width] for k in range(sections)], axis=1)
     result = jnp.dot(gathered, output_weight, preferred_element_type=f32).astype(bf16)
     whole = pl.BlockSpec(memory_space=pltpu.VMEM)
     scalar = pl.BlockSpec(memory_space=pltpu.SMEM)

time: 153 us -> 192 us (1.25); the launches traced: 151 us -> 192 us
  Pallas kernels: 9.48 us -> 42.5 us
  blocking collectives: 55.2 us -> 40.5 us
  between operations: 0.35 us -> 13.6 us
  waiting for transfers between devices: 39.3 us -> 51.9 us
  local copies, waits for them, and re-layouts: 5.35 us -> 2.02 us
    pallas_call x0 -> x1, Pallas kernels: none -> 33.7 us  [on_device(): pl.pallas_call(functools.partial(outgoing_kernel, sections), out_shape=ja...]
    all_gather x1 -> x0, blocking collectives: 14.7 us -> none  [on_device(): gathered = lax.all_gather(mixed, 'section', axis=1, tiled=True)]
    all_gather x0 -> x1, waiting for transfers between devices: none -> 8.07 us  [on_device(): gathered = lax.all_gather(mixed, 'section')]
    all_to_all x1, waiting for transfers between devices: 0.61 us -> 6.08 us  [on_device(): lax.all_to_all(result_copies, ('section', 'seq'), 0, 0)]
    unnamed x16 -> x10, local copies, waits for them, and re-layouts: 4.36 us -> 0.02 us
  transfers between devices with their start and end apart: 7 -> 8, of which waited for: 5 -> 6; matrix products, arithmetic and copies ran while one was open for 3% -> 2% of each run, Pallas kernels for 1% -> 2%
where the time goes in v8:
time: 192 us
  waiting for transfers between devices  51.9 us (27%)
  Pallas kernels  42.5 us (22%)
  blocking collectives  40.5 us (21%)
  starting transfers between devices  37 us (19%)
  between operations  13.6 us (7%)
  other arithmetic  2.59 us (1%)
  local copies, waits for them, and re-layouts  2.02 us (1%)
    all_to_all x1, blocking collectives, on_device(): lax.all_to_all(picked.reshape(shards, mine, 3 * head_width), 'seq', 0, 0)  40.5 us
    pallas_call x1, Pallas kernels, on_device(): pl.pallas_call(functools.partial(outgoing_kernel, sections), out_shape=ja...  33.7 us
    all_to_all x1, waiting for transfers between devices, on_device(): incoming = lax.all_to_all(outgoing, 'section', 0, 0)  11.1 us
    all_to_all x1, waiting for transfers between devices, on_device(): lax.all_to_all(partial.reshape(shards, mine, 2 * head_width), 'seq', 0, 0)  9.63 us
    all_to_all x1, waiting for transfers between devices, on_device(): lax.all_to_all(header_copies, 'seq', 0, 0).reshape(-1, 3 * head_width)  8.85 us
    all_to_all x1, starting transfers between devices, on_device(): lax.all_to_all(result_copies, ('section', 'seq'), 0, 0)  8.7 us
    all_to_all x1, starting transfers between devices, on_device(): lax.all_to_all(partial.reshape(shards, mine, 2 * head_width), 'seq', 0, 0)  8.62 us
    pallas_call x6, Pallas kernels, call(): pl.pallas_call(kernel, out_shape=[jax.ShapeDtypeStruct(shape, dtype) for...  8.27 us
  transfers between devices with their start and end apart: 8, of which 6 were waited for; matrix products, arithmetic and copies ran while one was open for 2% of the time, Pallas kernels for 2%

profile of v8, /device:TPU:1, one launch (start us, length us, event | category | flops | bytes accessed | tf_op | source)
XLA Modules:
  0.0 191.8 jit_solution(15674148188873446786)
XLA Ops:
  6.5 1.3 broadcast_in_dim.9
  7.8 33.7 %shard_map.82 = bf16[4,1296,128]{2,1,0:T(8,128)(2,1)} custom-call(f32[1,1024]{1,0:T(1,128)} %bitcast.15, bf16[512,1024]{1,0:T(8,128)(2,1)} %x.1, bf16[4096,128]{1,0:T(8,128)(2,1)} %query_weight.1, bf16[1024,128]{1,0:T(8,128)(2,1)} %key_weight.1, bf16[1024,128]{1,0:T(8,128)(2,1)} %value_weight.1), custom_call_target="tpu_custom_call" | custom-call | tf_op jit(solution)/shard_map/pallas_call | solution.py:298
  41.5 4.9 %all-to-all-start = ((bf16[4,1296,128]{2,1,0:T(8,128)(2,1)}), bf16[4,1296,128]{2,1,0:T(8,128)(2,1)S(1)}, u32[]{:S(2)}, u32[]{:S(2)}) async-start(bf16[4,1296,128]{2,1,0:T(8,128)(2,1)} %shard_map.82), calls=%async_computation | async-start | bytes 2654208 | tf_op jit(solution)/shard_map/all_to_all | solution.py:314
  46.4 1.0 multiply_sine_fusion
  47.4 0.1 fusion.8
  47.5 11.1 %all-to-all-done.arrived = bf16[4,1296,128]{2,1,0:T(8,128)(2,1)S(1)} async-done(((bf16[4,1296,128]{2,1,0:T(8,128)(2,1)}), bf16[4,1296,128]{2,1,0:T(8,128)(2,1)S(1)}, u32[]{:S(2)}, u32[]{:S(2)}) %all-to-all-start) | async-done | bytes 1327136 | tf_op jit(solution)/shard_map/all_to_all | solution.py:314
  58.6 1.6 shard_map.83
  60.2 3.6 %all-to-all-start.1 = ((bf16[4,768,128]{2,1,0:T(8,128)(2,1)}), bf16[4,768,128]{2,1,0:T(8,128)(2,1)S(1)}, u32[]{:S(2)}, u32[]{:S(2)}) async-start(bf16[4,768,128]{2,1,0:T(8,128)(2,1)} %shard_map.83), calls=%async_computation.1 | async-start | bytes 1572864 | tf_op jit(solution)/shard_map/all_to_all | solution.py:328
  63.9 0.2 pad_maximum_fusion
  64.1 8.1 %all-to-all-done.1.arrived = bf16[4,768,128]{2,1,0:T(8,128)(2,1)S(1)} async-done(((bf16[4,768,128]{2,1,0:T(8,128)(2,1)}), bf16[4,768,128]{2,1,0:T(8,128)(2,1)S(1)}, u32[]{:S(2)}, u32[]{:S(2)}) %all-to-all-start.1) | async-done | bytes 786464 | tf_op jit(solution)/shard_map/all_to_all | solution.py:328
  72.2 0.7 shard_map.84
  72.9 0.1 reshape.30
  73.0 40.5 %all_to_all.30.spread = bf16[128,2,384]{2,1,0:T(2,128)(2,1)S(1)} all-to-all(bf16[128,2,384]{2,1,0:T(2,128)(2,1)S(1)} %reshape.30), channel_id=1, replica_groups=mesh['section'=4,'seq'=128] {'seq'}, dimensions={0} | all-to-all | bytes 393216 | tf_op jit(solution)/shard_map/all_to_all | solution.py:340
  113.5 1.3 shard_map.85
  114.8 5.6 %all-to-all-start.3 = ((bf16[128,2,384]{2,1,0:T(2,128)(2,1)}), bf16[128,2,384]{2,1,0:T(2,128)(2,1)S(1)}, u32[]{:S(2)}, u32[]{:S(2)}) async-start(bf16[128,2,384]{2,1,0:T(2,128)(2,1)} %shard_map.85), calls=%async_computation.3 | async-start | bytes 393216 | tf_op jit(solution)/shard_map/all_to_all | solution.py:348
  120.4 3.5 %collective-permute-start = (bf16[256,256]{1,0:T(8,128)(2,1)S(1)}, bf16[256,256]{1,0:T(8,128)(2,1)S(1)}, u32[]{:S(2)}, u32[]{:S(2)}) collective-permute-start(bf16[256,256]{1,0:T(8,128)(2,1)S(1)} %get-tuple-element.30), channel_id=1, source_target_pairs={{0,1},{1,2},{2,3},{3,4},{4,5},{5,6},{6,7},{7,8},{8,9},{9,10},{10,1... | collective-permute-start | bytes 393224 | tf_op jit(solution)/shard_map/ppermute | solution.py:20
  123.9 1.9 %collective-permute-start.1 = (bf16[256,256]{1,0:T(8,128)(2,1)S(1)}, bf16[256,256]{1,0:T(8,128)(2,1)S(1)}, u32[]{:S(2)}, u32[]{:S(2)}) collective-permute-start(bf16[256,256]{1,0:T(8,128)(2,1)S(1)} %get-tuple-element.29), channel_id=1, source_target_pairs={{0,127},{1,0},{2,1},{3,2},{4,3},{5,4},{6,5},{7,6},{8,7},{9,8},{10,... | collective-permute-start | bytes 393224 | tf_op jit(solution)/shard_map/ppermute | solution.py:20
  125.8 8.9 %all-to-all-done.3 = bf16[128,2,384]{2,1,0:T(2,128)(2,1)S(1)} async-done(((bf16[128,2,384]{2,1,0:T(2,128)(2,1)}), bf16[128,2,384]{2,1,0:T(2,128)(2,1)S(1)}, u32[]{:S(2)}, u32[]{:S(2)}) %all-to-all-start.3) | async-done | bytes 196640 | tf_op jit(solution)/shard_map/all_to_all | solution.py:348
  134.7 0.1 reshape.31.header
  134.8 0.5 shard_map.86
  135.3 0.7 reshape.32
  136.0 8.6 %all-to-all-start.4 = ((bf16[128,2,256]{2,1,0:T(2,128)(2,1)}), bf16[128,2,256]{2,1,0:T(2,128)(2,1)S(1)}, u32[]{:S(2)}, u32[]{:S(2)}) async-start(bf16[128,2,256]{2,1,0:T(2,128)(2,1)} %reshape.32), calls=%async_computation.4 | async-start | bytes 262144 | tf_op jit(solution)/shard_map/all_to_all | solution.py:361
  144.6 0.2 all-gather.3.cloned.1.call-start
  144.8 2.8 %shard_map.88 = bf16[512,256]{1,0:T(8,128)(2,1)} custom-call(s32[1]{0:T(128)} %bitcast.seq_place, s32[4]{0:T(128)S(1)} %copy-done.4, s32[2]{0:T(128)S(1)} %copy-done.3, bf16[512,128]{1,0:T(8,128)(2,1)S(1)} %get-tuple-element.21.queries, bf16[256,256]{1,0:T(8,128)(2,1)S(1)} %collective-permute-done.before, ...), custom_call_target="tpu_custom_call" | custom-call | tf_op jit(solution)/shard_map/pallas_call | solution.py:40
  147.7 9.6 %all-to-all-done.4.parts = bf16[128,2,256]{2,1,0:T(2,128)(2,1)S(1)} async-done(((bf16[128,2,256]{2,1,0:T(2,128)(2,1)}), bf16[128,2,256]{2,1,0:T(2,128)(2,1)S(1)}, u32[]{:S(2)}, u32[]{:S(2)}) %all-to-all-start.4) | async-done | bytes 131104 | tf_op jit(solution)/shard_map/all_to_all | solution.py:361
  157.3 1.3 shard_map.87
  158.7 8.7 %all-to-all-start.5 = ((bf16[512,2,128]{2,1,0:T(2,128)(2,1)}), bf16[512,2,128]{2,1,0:T(2,128)(2,1)S(1)}, u32[]{:S(2)}, u32[]{:S(2)}) async-start(bf16[512,2,128]{2,1,0:T(2,128)(2,1)} %shard_map.87), calls=%async_computation.5 | async-start | bytes 524288 | tf_op jit(solution)/shard_map/all_to_all | solution.py:373
  167.4 8.1 %all-gather.3.cloned.1.call-done = bf16[2048,256]{1,0:T(8,128)(2,1)} async-done(((bf16[512,256]{1,0:T(8,128)(2,1)}), bf16[2048,256]{1,0:T(8,128)(2,1)}) %all-gather.3.cloned.1.call-update) | async-done | bytes 1048592 | tf_op jit(solution)/shard_map/all_gather | solution.py:376
  175.4 1.1 slice_bitcast_fusion.3
  176.6 1.7 convolution_convert_fusion._
  178.3 6.1 %all-to-all-done.5 = bf16[512,2,128]{2,1,0:T(2,128)(2,1)S(1)} async-done(((bf16[512,2,128]{2,1,0:T(2,128)(2,1)}), bf16[512,2,128]{2,1,0:T(2,128)(2,1)S(1)}, u32[]{:S(2)}, u32[]{:S(2)}) %all-to-all-start.5) | async-done | bytes 262176 | tf_op jit(solution)/shard_map/all_to_all | solution.py:373
  184.3 0.6 shard_map.89
  (16 shorter events, 0.1 us)
Async XLA Ops:
  41.5 17.1 %all-to-all-start = ((bf16[4,1296,128]{2,1,0:T(8,128)(2,1)}), bf16[4,1296,128]{2,1,0:T(8,128)(2,1)S(1)}, u32[]{:S(2)}, u32[]{:S(2)}) async-start(bf16[4,1296,128]{2,1,0:T(8,128)(2,1)} %shard_map.82), calls=%async_computation | async-start | bytes 2654208 | tf_op jit(solution)/shard_map/all_to_all | solution.py:314
  46.3 12.3 %copy-start = (bf16[512,1024]{1,0:T(8,128)(2,1)S(1)}, bf16[512,1024]{1,0:T(8,128)(2,1)}, u32[]{:S(2)}) copy-start(bf16[512,1024]{1,0:T(8,128)(2,1)} %x.1) | copy-start | bytes 3145732
  46.3 12.3 %copy-start.2 = (f32[1024]{0:T(1024)S(1)}, f32[1024]{0:T(1024)}, u32[]{:S(2)}) copy-start(f32[1024]{0:T(1024)} %broadcast_in_dim.9) | copy-start | bytes 12292
  60.2 11.9 %copy-start.3 = (s32[2]{0:T(128)S(1)}, s32[2]{0:T(128)}, u32[]{:S(2)}) copy-start(s32[2]{0:T(128)} %header_ids.7) | copy-start | bytes 28
  60.2 11.9 %all-to-all-start.1 = ((bf16[4,768,128]{2,1,0:T(8,128)(2,1)}), bf16[4,768,128]{2,1,0:T(8,128)(2,1)S(1)}, u32[]{:S(2)}, u32[]{:S(2)}) async-start(bf16[4,768,128]{2,1,0:T(8,128)(2,1)} %shard_map.83), calls=%async_computation.1 | async-start | bytes 1572864 | tf_op jit(solution)/shard_map/all_to_all | solution.py:328
  113.5 31.3 %copy-start.4 = (s32[4]{0:T(128)S(1)}, s32[4]{0:T(128)}, u32[]{:S(2)}) copy-start(s32[4]{0:T(128)} %reach.1) | copy-start | bytes 52
  114.8 19.9 %all-to-all-start.3 = ((bf16[128,2,384]{2,1,0:T(2,128)(2,1)}), bf16[128,2,384]{2,1,0:T(2,128)(2,1)S(1)}, u32[]{:S(2)}, u32[]{:S(2)}) async-start(bf16[128,2,384]{2,1,0:T(2,128)(2,1)} %shard_map.85), calls=%async_computation.3 | async-start | bytes 393216 | tf_op jit(solution)/shard_map/all_to_all | solution.py:348
  120.4 14.9 %collective-permute-start = (bf16[256,256]{1,0:T(8,128)(2,1)S(1)}, bf16[256,256]{1,0:T(8,128)(2,1)S(1)}, u32[]{:S(2)}, u32[]{:S(2)}) collective-permute-start(bf16[256,256]{1,0:T(8,128)(2,1)S(1)} %get-tuple-element.30), channel_id=1, source_target_pairs={{0,1},{1,2},{2,3},{3,4},{4,5},{5,6},{6,7},{7,8},{8,9},{9,10},{10,1... | collective-permute-start | bytes 393224 | tf_op jit(solution)/shard_map/ppermute | solution.py:20
  123.9 11.4 %collective-permute-start.1 = (bf16[256,256]{1,0:T(8,128)(2,1)S(1)}, bf16[256,256]{1,0:T(8,128)(2,1)S(1)}, u32[]{:S(2)}, u32[]{:S(2)}) collective-permute-start(bf16[256,256]{1,0:T(8,128)(2,1)S(1)} %get-tuple-element.29), channel_id=1, source_target_pairs={{0,127},{1,0},{2,1},{3,2},{4,3},{5,4},{6,5},{7,6},{8,7},{9,8},{10,... | collective-permute-start | bytes 393224 | tf_op jit(solution)/shard_map/ppermute | solution.py:20
  136.0 21.4 %all-to-all-start.4 = ((bf16[128,2,256]{2,1,0:T(2,128)(2,1)}), bf16[128,2,256]{2,1,0:T(2,128)(2,1)S(1)}, u32[]{:S(2)}, u32[]{:S(2)}) async-start(bf16[128,2,256]{2,1,0:T(2,128)(2,1)} %reshape.32), calls=%async_computation.4 | async-start | bytes 262144 | tf_op jit(solution)/shard_map/all_to_all | solution.py:361
  144.6 30.8 %all-gather.3.cloned.1.call-start = ((), (), s32[]{:S(2)}) async-start(), calls=%async_computation.6 | async-start | bytes 1310720 | tf_op jit(solution)/shard_map/all_gather | solution.py:376
  158.7 17.9 %copy-start.1 = (bf16[512,1024]{1,0:T(8,128)(2,1)S(1)}, bf16[512,1024]{1,0:T(8,128)(2,1)}, u32[]{:S(2)}) copy-start(bf16[512,1024]{1,0:T(8,128)(2,1)} %weight.1) | copy-start | bytes 3145732
  158.7 25.7 %all-to-all-start.5 = ((bf16[512,2,128]{2,1,0:T(2,128)(2,1)}), bf16[512,2,128]{2,1,0:T(2,128)(2,1)S(1)}, u32[]{:S(2)}, u32[]{:S(2)}) async-start(bf16[512,2,128]{2,1,0:T(2,128)(2,1)} %shard_map.87), calls=%async_computation.5 | async-start | bytes 524288 | tf_op jit(solution)/shard_map/all_to_all | solution.py:373
Sparse Core Ops, SparseCore 0:
  147.8 27.5 all-gather.2

commit v9 on v8

--- a/solution.py
+++ b/solution.py
@@ -68,10 +68,12 @@
     out,
     x,
     keyval_weight,
+    stage,
     tail,
     rows16,
     block_sems,
     weight_sems,
+    stage_sems,
     direct_sems,
     tail_sem,
 ):
@@ -89,29 +91,34 @@
         )
         for b in range(count)
     ]
-    direct = [
+    staged = [
         pltpu.make_async_copy(
-            query_weight.at[pl.ds(t * part, part), :],
-            out.at[t, pl.ds(0, part), :],
-            direct_sems.at[t],
+            query_weight.at[pl.ds(t * part, part), :], stage.at[t], stage_sems.at[t]
         )
         for t in range(sections)
     ]
-    for copy in loads + blocks + direct:
+    direct = [
+        pltpu.make_async_copy(stage.at[t], out.at[t, pl.ds(0, part), :], direct_sems.at[t])
+        for t in range(sections)
+    ]
+    for copy in loads + blocks + staged:
         copy.start()
     rows16[...] = jnp.zeros_like(rows16)
+    factor = gain[...].astype(F32).reshape(1, part)
     for copy in loads:
         copy.wait()
     both_weights = jnp.concatenate([keyval_weight[0], keyval_weight[1]], axis=1)
     for b in range(count):
         blocks[b].wait()
+        staged[b].wait()
+        direct[b].start()
         block = x[b * size : (b + 1) * size, :].astype(F32)
         total = jnp.sum(block * block, axis=1, keepdims=True)
         line = jnp.transpose(jnp.broadcast_to(total, (size, size)))[0:1, :]
         high = line.astype(BF16).astype(F32)
         rows16[b : b + 1, :] = high
         rows16[count + b : count + b + 1, :] = line - high
-        block = block * gain[...]
+        block = block * factor
         high = block.astype(BF16)
         low = (block - high.astype(F32)).astype(BF16)
         both = jnp.dot(
@@ -124,9 +131,8 @@
         tail[t, 2 * size : 2 * size + 16, :] = rows16[...].astype(BF16)
     last = pltpu.make_async_copy(tail, out.at[:, pl.ds(part, 2 * size + 16), :], tail_sem)
     last.start()
-    for copy in direct:
+    for copy in direct + [last]:
         copy.wait()
-    last.wait()
 
 
 def partial_kernel(sections, place, x, gain, arrived, cosine, sine, out, squares, normed):
@@ -141,7 +147,7 @@
     for b in range(count):
         scale = spread_down(squares[b : b + 1, :], size)
         scale = jnp.concatenate([scale] * (part // size), axis=1)
-        block = x[b * size : (b + 1) * size, :].astype(F32) * scale * gain[...]
+        block = x[b * size : (b + 1) * size, :].astype(F32) * scale * gain[...].astype(F32)
         normed[b * size : (b + 1) * size, :] = block.astype(BF16)
     for k in range(0, sections, 2):
         pair = jnp.concatenate([arrived[k, 0:part, :], arrived[k + 1, 0:part, :]], axis=1)
@@ -290,7 +296,7 @@
     seq_place = lax.axis_index("seq")
     headers = header_ids.shape[0]
     mine = headers * BLOCK // shards
-    gain = norm_gain.astype(f32)[None, :]
+    gain = norm_gain[None, :]
 
     places = [place.astype(jnp.int32).reshape(1) for place in (section_place, seq_place)]
     tall = part + 2 * BLOCK + 16
@@ -303,14 +309,16 @@
         scratch_shapes=[
             pltpu.VMEM((rows, part), bf16),
             pltpu.VMEM((2, part, head_width), bf16),
-            pltpu.VMEM((sections, tall - part, head_width), bf16),
+            pltpu.VMEM((sections, part, head_width), bf16),
+            pltpu.VMEM((sections, 2 * BLOCK + 16, head_width), bf16),
             pltpu.VMEM((16, head_width), f32),
             pltpu.SemaphoreType.DMA((local_blocks,)),
             pltpu.SemaphoreType.DMA((2,)),
             pltpu.SemaphoreType.DMA((sections,)),
+            pltpu.SemaphoreType.DMA((sections,)),
             pltpu.SemaphoreType.DMA,
         ],
-    )(gain, hidden, query_weight, key_weight, value_weight)
+    )(norm_gain, hidden, query_weight, key_weight, value_weight)
     incoming = lax.all_to_all(outgoing, "section", 0, 0)
     own_positions = seq_place * rows + jnp.arange(rows, dtype=jnp.int32)
     own_tables = tables(own_positions, head_width)

time: 192 us -> 162 us (0.84)
  Pallas kernels: 42.5 us -> 13.6 us
    pallas_call x1, Pallas kernels: 33.7 us -> 4.79 us  [on_device(): pl.pallas_call(functools.partial(outgoing_kernel, sections), out_shape=ja...]
  transfers between devices with their start and end apart: 8 -> 8, of which waited for: 6 -> 6; matrix products, arithmetic and copies ran while one was open for 2% -> 3% of each run, Pallas kernels for 2% -> 3%
where the time goes in v9:
time: 162 us
  waiting for transfers between devices  51.8 us (32%)
  blocking collectives  40.5 us (25%)
  starting transfers between devices  37 us (23%)
  Pallas kernels  13.6 us (8%)
  between operations  13.6 us (8%)
  local copies, waits for them, and re-layouts  2.03 us (1%)
  matrix products  1.7 us (1%)
    all_to_all x1, blocking collectives, on_device(): lax.all_to_all(picked.reshape(shards, mine, 3 * head_width), 'seq', 0, 0)  40.5 us
    all_to_all x1, waiting for transfers between devices, on_device(): incoming = lax.all_to_all(outgoing, 'section', 0, 0)  11.1 us
    all_to_all x1, waiting for transfers between devices, on_device(): lax.all_to_all(partial.reshape(shards, mine, 2 * head_width), 'seq', 0, 0)  9.63 us
    all_to_all x1, waiting for transfers between devices, on_device(): lax.all_to_all(header_copies, 'seq', 0, 0).reshape(-1, 3 * head_width)  8.85 us
    all_to_all x1, starting transfers between devices, on_device(): lax.all_to_all(result_copies, ('section', 'seq'), 0, 0)  8.7 us
    all_to_all x1, starting transfers between devices, on_device(): lax.all_to_all(partial.reshape(shards, mine, 2 * head_width), 'seq', 0, 0)  8.62 us
    pallas_call x6, Pallas kernels, call(): pl.pallas_call(kernel, out_shape=[jax.ShapeDtypeStruct(shape, dtype) for...  8.28 us
    all_to_all x1, waiting for transfers between devices, on_device(): arrived = lax.all_to_all(payload, 'section', 0, 0)  8.09 us
  transfers between devices with their start and end apart: 8, of which 6 were waited for; matrix products, arithmetic and copies ran while one was open for 3% of the time, Pallas kernels for 3%

profile of v9, /device:TPU:1, one launch (start us, length us, event | category | flops | bytes accessed | tf_op | source)
XLA Modules:
  0.0 161.7 jit_solution(8924968457342011049)
XLA Ops:
  6.5 4.8 %shard_map.82 = bf16[4,1296,128]{2,1,0:T(8,128)(2,1)} custom-call(bf16[1024]{0:T(1024)(128)(2,1)} %gain.1, bf16[512,1024]{1,0:T(8,128)(2,1)} %x.1, bf16[4096,128]{1,0:T(8,128)(2,1)} %query_weight.1, bf16[1024,128]{1,0:T(8,128)(2,1)} %key_weight.1, bf16[1024,128]{1,0:T(8,128)(2,1)} %value_weight.1), custom_call_target="tpu_custom_call" | custom-call | tf_op jit(solution)/shard_map/pallas_call | solution.py:304
  11.3 4.9 %all-to-all-start = ((bf16[4,1296,128]{2,1,0:T(8,128)(2,1)}), bf16[4,1296,128]{2,1,0:T(8,128)(2,1)S(1)}, u32[]{:S(2)}, u32[]{:S(2)}) async-start(bf16[4,1296,128]{2,1,0:T(8,128)(2,1)} %shard_map.82), calls=%async_computation | async-start | bytes 2654208 | tf_op jit(solution)/shard_map/all_to_all | solution.py:322
  16.2 1.0 multiply_sine_fusion
  17.2 0.1 fusion.8
  17.4 11.1 %all-to-all-done.arrived = bf16[4,1296,128]{2,1,0:T(8,128)(2,1)S(1)} async-done(((bf16[4,1296,128]{2,1,0:T(8,128)(2,1)}), bf16[4,1296,128]{2,1,0:T(8,128)(2,1)S(1)}, u32[]{:S(2)}, u32[]{:S(2)}) %all-to-all-start) | async-done | bytes 1327136 | tf_op jit(solution)/shard_map/all_to_all | solution.py:322
  28.5 1.7 %shard_map.83 = bf16[4,768,128]{2,1,0:T(8,128)(2,1)} custom-call(s32[1]{0:T(128)} %bitcast.1.place, bf16[512,1024]{1,0:T(8,128)(2,1)S(1)} %copy-done, bf16[1,1024]{1,0:T(2,128)(2,1)S(1)} %broadcast_in_dim.2.gain, bf16[4,1296,128]{2,1,0:T(8,128)(2,1)S(1)} %all-to-all-done.arrived, f32[128,128]{1,0:T(8,128)S(1)} %get-tuple-element.35.cosine, ...), custom_call_target="tpu_custom_call" | custom-call | tf_op jit(solution)/shard_map/pallas_call | solution.py:40
  30.1 3.6 %all-to-all-start.1 = ((bf16[4,768,128]{2,1,0:T(8,128)(2,1)}), bf16[4,768,128]{2,1,0:T(8,128)(2,1)S(1)}, u32[]{:S(2)}, u32[]{:S(2)}) async-start(bf16[4,768,128]{2,1,0:T(8,128)(2,1)} %shard_map.83), calls=%async_computation.1 | async-start | bytes 1572864 | tf_op jit(solution)/shard_map/all_to_all | solution.py:336
  33.8 0.2 pad_maximum_fusion
  34.0 8.1 %all-to-all-done.1.arrived = bf16[4,768,128]{2,1,0:T(8,128)(2,1)S(1)} async-done(((bf16[4,768,128]{2,1,0:T(8,128)(2,1)}), bf16[4,768,128]{2,1,0:T(8,128)(2,1)S(1)}, u32[]{:S(2)}, u32[]{:S(2)}) %all-to-all-start.1) | async-done | bytes 786464 | tf_op jit(solution)/shard_map/all_to_all | solution.py:336
  42.1 0.7 shard_map.84
  42.8 0.1 reshape.30
  42.9 40.5 %all_to_all.30.spread = bf16[128,2,384]{2,1,0:T(2,128)(2,1)S(1)} all-to-all(bf16[128,2,384]{2,1,0:T(2,128)(2,1)S(1)} %reshape.30), channel_id=1, replica_groups=mesh['section'=4,'seq'=128] {'seq'}, dimensions={0} | all-to-all | bytes 393216 | tf_op jit(solution)/shard_map/all_to_all | solution.py:348
  83.4 1.3 shard_map.85
  84.6 5.6 %all-to-all-start.3 = ((bf16[128,2,384]{2,1,0:T(2,128)(2,1)}), bf16[128,2,384]{2,1,0:T(2,128)(2,1)S(1)}, u32[]{:S(2)}, u32[]{:S(2)}) async-start(bf16[128,2,384]{2,1,0:T(2,128)(2,1)} %shard_map.85), calls=%async_computation.3 | async-start | bytes 393216 | tf_op jit(solution)/shard_map/all_to_all | solution.py:356
  90.2 3.5 %collective-permute-start = (bf16[256,256]{1,0:T(8,128)(2,1)S(1)}, bf16[256,256]{1,0:T(8,128)(2,1)S(1)}, u32[]{:S(2)}, u32[]{:S(2)}) collective-permute-start(bf16[256,256]{1,0:T(8,128)(2,1)S(1)} %get-tuple-element.30), channel_id=1, source_target_pairs={{0,1},{1,2},{2,3},{3,4},{4,5},{5,6},{6,7},{7,8},{8,9},{9,10},{10,1... | collective-permute-start | bytes 393224 | tf_op jit(solution)/shard_map/ppermute | solution.py:20
  93.8 1.9 %collective-permute-start.1 = (bf16[256,256]{1,0:T(8,128)(2,1)S(1)}, bf16[256,256]{1,0:T(8,128)(2,1)S(1)}, u32[]{:S(2)}, u32[]{:S(2)}) collective-permute-start(bf16[256,256]{1,0:T(8,128)(2,1)S(1)} %get-tuple-element.29), channel_id=1, source_target_pairs={{0,127},{1,0},{2,1},{3,2},{4,3},{5,4},{6,5},{7,6},{8,7},{9,8},{10,... | collective-permute-start | bytes 393224 | tf_op jit(solution)/shard_map/ppermute | solution.py:20
  95.7 8.9 %all-to-all-done.3 = bf16[128,2,384]{2,1,0:T(2,128)(2,1)S(1)} async-done(((bf16[128,2,384]{2,1,0:T(2,128)(2,1)}), bf16[128,2,384]{2,1,0:T(2,128)(2,1)S(1)}, u32[]{:S(2)}, u32[]{:S(2)}) %all-to-all-start.3) | async-done | bytes 196640 | tf_op jit(solution)/shard_map/all_to_all | solution.py:356
  104.6 0.1 reshape.31.header
  104.7 0.5 shard_map.86
  105.2 0.7 reshape.32
  105.9 8.6 %all-to-all-start.4 = ((bf16[128,2,256]{2,1,0:T(2,128)(2,1)}), bf16[128,2,256]{2,1,0:T(2,128)(2,1)S(1)}, u32[]{:S(2)}, u32[]{:S(2)}) async-start(bf16[128,2,256]{2,1,0:T(2,128)(2,1)} %reshape.32), calls=%async_computation.4 | async-start | bytes 262144 | tf_op jit(solution)/shard_map/all_to_all | solution.py:369
  114.5 0.2 all-gather.3.cloned.1.call-start
  114.7 2.8 %shard_map.88 = bf16[512,256]{1,0:T(8,128)(2,1)} custom-call(s32[1]{0:T(128)} %bitcast.seq_place, s32[4]{0:T(128)S(1)} %copy-done.3, s32[2]{0:T(128)S(1)} %copy-done.2, bf16[512,128]{1,0:T(8,128)(2,1)S(1)} %get-tuple-element.21.queries, bf16[256,256]{1,0:T(8,128)(2,1)S(1)} %collective-permute-done.before, ...), custom_call_target="tpu_custom_call" | custom-call | tf_op jit(solution)/shard_map/pallas_call | solution.py:40
  117.6 0.0 all-gather.3.cloned.1.call-update
  117.6 9.6 %all-to-all-done.4.parts = bf16[128,2,256]{2,1,0:T(2,128)(2,1)S(1)} async-done(((bf16[128,2,256]{2,1,0:T(2,128)(2,1)}), bf16[128,2,256]{2,1,0:T(2,128)(2,1)S(1)}, u32[]{:S(2)}, u32[]{:S(2)}) %all-to-all-start.4) | async-done | bytes 131104 | tf_op jit(solution)/shard_map/all_to_all | solution.py:369
  127.2 1.3 shard_map.87
  128.5 8.7 %all-to-all-start.5 = ((bf16[512,2,128]{2,1,0:T(2,128)(2,1)}), bf16[512,2,128]{2,1,0:T(2,128)(2,1)S(1)}, u32[]{:S(2)}, u32[]{:S(2)}) async-start(bf16[512,2,128]{2,1,0:T(2,128)(2,1)} %shard_map.87), calls=%async_computation.5 | async-start | bytes 524288 | tf_op jit(solution)/shard_map/all_to_all | solution.py:381
  137.2 8.1 %all-gather.3.cloned.1.call-done = bf16[2048,256]{1,0:T(8,128)(2,1)} async-done(((bf16[512,256]{1,0:T(8,128)(2,1)}), bf16[2048,256]{1,0:T(8,128)(2,1)}) %all-gather.3.cloned.1.call-update) | async-done | bytes 1048592 | tf_op jit(solution)/shard_map/all_gather | solution.py:384
  145.3 1.1 slice_bitcast_fusion.3
  146.5 1.7 %convolution_convert_fusion._ = bf16[512,1024]{1,0:T(8,128)(2,1)} fusion(bf16[512,1024]{1,0:T(8,128)(2,1)S(1)} %copy-done.1, bf16[512,128]{1,0:T(8,128)(2,1)S(1)} %get-tuple-element.26, bf16[512,128]{1,0:T(8,128)(2,1)S(1)} %get-tuple-element.27, bf16[512,128]{1,0:T(8,128)(2,1)S(1)} %get-tuple-element.28, bf16[512,128]{1,0:T(8,128)(2,1)S(1)} %get-tuple-element.25), kind=kOutput, calls=%fused_computation | convolution fusion | flops 539492352 | bytes 2621440 | tf_op jit(solution)/shard_map/dot_general | solution.py:386
  148.2 6.1 %all-to-all-done.5 = bf16[512,2,128]{2,1,0:T(2,128)(2,1)S(1)} async-done(((bf16[512,2,128]{2,1,0:T(2,128)(2,1)}), bf16[512,2,128]{2,1,0:T(2,128)(2,1)S(1)}, u32[]{:S(2)}, u32[]{:S(2)}) %all-to-all-start.5) | async-done | bytes 262176 | tf_op jit(solution)/shard_map/all_to_all | solution.py:381
  154.2 0.6 shard_map.89
  (16 shorter events, 0.1 us)
Async XLA Ops:
  11.3 4.9 %copy-start.4 = (bf16[1024]{0:T(1024)(128)(2,1)S(1)}, bf16[1024]{0:T(1024)(128)(2,1)}, u32[]{:S(2)}) copy-start(bf16[1024]{0:T(1024)(128)(2,1)} %gain.1) | copy-start | bytes 6148
  11.3 17.1 %all-to-all-start = ((bf16[4,1296,128]{2,1,0:T(8,128)(2,1)}), bf16[4,1296,128]{2,1,0:T(8,128)(2,1)S(1)}, u32[]{:S(2)}, u32[]{:S(2)}) async-start(bf16[4,1296,128]{2,1,0:T(8,128)(2,1)} %shard_map.82), calls=%async_computation | async-start | bytes 2654208 | tf_op jit(solution)/shard_map/all_to_all | solution.py:322
  16.2 12.3 %copy-start = (bf16[512,1024]{1,0:T(8,128)(2,1)S(1)}, bf16[512,1024]{1,0:T(8,128)(2,1)}, u32[]{:S(2)}) copy-start(bf16[512,1024]{1,0:T(8,128)(2,1)} %x.1) | copy-start | bytes 3145732
  30.1 11.9 %copy-start.2 = (s32[2]{0:T(128)S(1)}, s32[2]{0:T(128)}, u32[]{:S(2)}) copy-start(s32[2]{0:T(128)} %header_ids.7) | copy-start | bytes 28
  30.1 11.9 %all-to-all-start.1 = ((bf16[4,768,128]{2,1,0:T(8,128)(2,1)}), bf16[4,768,128]{2,1,0:T(8,128)(2,1)S(1)}, u32[]{:S(2)}, u32[]{:S(2)}) async-start(bf16[4,768,128]{2,1,0:T(8,128)(2,1)} %shard_map.83), calls=%async_computation.1 | async-start | bytes 1572864 | tf_op jit(solution)/shard_map/all_to_all | solution.py:336
  83.4 31.3 %copy-start.3 = (s32[4]{0:T(128)S(1)}, s32[4]{0:T(128)}, u32[]{:S(2)}) copy-start(s32[4]{0:T(128)} %reach.1) | copy-start | bytes 52
  84.6 19.9 %all-to-all-start.3 = ((bf16[128,2,384]{2,1,0:T(2,128)(2,1)}), bf16[128,2,384]{2,1,0:T(2,128)(2,1)S(1)}, u32[]{:S(2)}, u32[]{:S(2)}) async-start(bf16[128,2,384]{2,1,0:T(2,128)(2,1)} %shard_map.85), calls=%async_computation.3 | async-start | bytes 393216 | tf_op jit(solution)/shard_map/all_to_all | solution.py:356
  90.2 14.9 %collective-permute-start = (bf16[256,256]{1,0:T(8,128)(2,1)S(1)}, bf16[256,256]{1,0:T(8,128)(2,1)S(1)}, u32[]{:S(2)}, u32[]{:S(2)}) collective-permute-start(bf16[256,256]{1,0:T(8,128)(2,1)S(1)} %get-tuple-element.30), channel_id=1, source_target_pairs={{0,1},{1,2},{2,3},{3,4},{4,5},{5,6},{6,7},{7,8},{8,9},{9,10},{10,1... | collective-permute-start | bytes 393224 | tf_op jit(solution)/shard_map/ppermute | solution.py:20
  93.8 11.4 %collective-permute-start.1 = (bf16[256,256]{1,0:T(8,128)(2,1)S(1)}, bf16[256,256]{1,0:T(8,128)(2,1)S(1)}, u32[]{:S(2)}, u32[]{:S(2)}) collective-permute-start(bf16[256,256]{1,0:T(8,128)(2,1)S(1)} %get-tuple-element.29), channel_id=1, source_target_pairs={{0,127},{1,0},{2,1},{3,2},{4,3},{5,4},{6,5},{7,6},{8,7},{9,8},{10,... | collective-permute-start | bytes 393224 | tf_op jit(solution)/shard_map/ppermute | solution.py:20
  105.9 21.4 %all-to-all-start.4 = ((bf16[128,2,256]{2,1,0:T(2,128)(2,1)}), bf16[128,2,256]{2,1,0:T(2,128)(2,1)S(1)}, u32[]{:S(2)}, u32[]{:S(2)}) async-start(bf16[128,2,256]{2,1,0:T(2,128)(2,1)} %reshape.32), calls=%async_computation.4 | async-start | bytes 262144 | tf_op jit(solution)/shard_map/all_to_all | solution.py:369
  114.5 30.8 %all-gather.3.cloned.1.call-start = ((), (), s32[]{:S(2)}) async-start(), calls=%async_computation.6 | async-start | bytes 1310720 | tf_op jit(solution)/shard_map/all_gather | solution.py:384
  128.5 17.9 %copy-start.1 = (bf16[512,1024]{1,0:T(8,128)(2,1)S(1)}, bf16[512,1024]{1,0:T(8,128)(2,1)}, u32[]{:S(2)}) copy-start(bf16[512,1024]{1,0:T(8,128)(2,1)} %weight.1) | copy-start | bytes 3145732
  128.5 25.7 %all-to-all-start.5 = ((bf16[512,2,128]{2,1,0:T(2,128)(2,1)}), bf16[512,2,128]{2,1,0:T(2,128)(2,1)S(1)}, u32[]{:S(2)}, u32[]{:S(2)}) async-start(bf16[512,2,128]{2,1,0:T(2,128)(2,1)} %shard_map.87), calls=%async_computation.5 | async-start | bytes 524288 | tf_op jit(solution)/shard_map/all_to_all | solution.py:381
Sparse Core Ops, SparseCore 0:
  117.7 27.5 all-gather.2

commit v10 on v9

--- a/solution.py
+++ b/solution.py
@@ -33,7 +33,7 @@
 VMEM_LIMIT = 24 * 1024 * 1024
 
 
-def call(kernel, outs, scalars, arrays, scratch=(), flops=0):
+def call(kernel, outs, scalars, arrays, scratch=()):
     whole = pl.BlockSpec(memory_space=pltpu.VMEM)
     specs = [pl.BlockSpec(memory_space=pltpu.SMEM)] * len(scalars)
     specs += [whole] * len(arrays)
@@ -44,9 +44,6 @@
         out_specs=[whole] * len(outs),
         scratch_shapes=list(scratch),
         compiler_params=pltpu.CompilerParams(vmem_limit_bytes=VMEM_LIMIT),
-        cost_estimate=(
-            pl.CostEstimate(flops=flops, bytes_accessed=0, transcendentals=0) if flops else None
-        ),
     )(*scalars, *arrays)
 
 
@@ -221,8 +218,7 @@
         weights = jnp.exp(scores - jnp.max(scores, axis=1, keepdims=True))
         total = jnp.sum(weights, axis=1, keepdims=True)
         mixed = jnp.dot(weights.astype(BF16), values, preferred_element_type=F32)
-        mixed = (mixed / total).astype(BF16)
-        out[b * size : (b + 1) * size, :] = jnp.concatenate([mixed, mixed], axis=1)
+        out[b * size : (b + 1) * size, :] = (mixed / total).astype(BF16)
 
 
 def far_kernel(header, keyval, out):
@@ -370,19 +366,18 @@
     everywhere = sections * shards
     (mixed,) = call(
         functools.partial(window_kernel, total_blocks),
-        [((rows, 2 * head_width), bf16)],
+        [((rows, head_width), bf16)],
         [places[1], block_reach, header_ids],
         [queries, before, stacked, after, header_pack],
     )
     (result_copies,) = call(
-        merge_kernel, [((everywhere, mine, head_width), bf16)], [], [parts], flops=10**11
-    )
-    result_copies, _ = lax.optimization_barrier((result_copies, mixed))
+        merge_kernel, [((everywhere, mine, head_width), bf16)], [], [parts]
+    )
+    result_copies, mixed = lax.optimization_barrier((result_copies, mixed))
     header_all = lax.all_to_all(result_copies, ("section", "seq"), 0, 0).reshape(
         sections, headers * BLOCK, head_width
     )
-    gathered = lax.all_gather(mixed, "section")
-    gathered = jnp.concatenate([gathered[k, :, :head_width] for k in range(sections)], axis=1)
+    gathered = lax.all_gather(mixed, "section", axis=1, tiled=True)
     result = jnp.dot(gathered, output_weight, preferred_element_type=f32).astype(bf16)
     whole = pl.BlockSpec(memory_space=pltpu.VMEM)
     scalar = pl.BlockSpec(memory_space=pltpu.SMEM)

time: 162 us -> 150 us (0.926)
  blocking collectives: 40.5 us -> 55.1 us
  between operations: 13.6 us -> 0.33 us
  waiting for transfers between devices: 51.8 us -> 39.3 us
    all_gather x0 -> x1, blocking collectives: none -> 14.6 us  [on_device(): gathered = lax.all_gather(mixed, 'section', axis=1, tiled=True)]
    all_gather x1 -> x0, waiting for transfers between devices: 8.07 us -> none  [on_device(): gathered = lax.all_gather(mixed, 'section')]
    all_to_all x1, waiting for transfers between devices: 6.07 us -> 0.64 us  [on_device(): lax.all_to_all(result_copies, ('section', 'seq'), 0, 0)]
  transfers between devices with their start and end apart: 8 -> 7, of which waited for: 6 -> 5; matrix products, arithmetic and copies ran while one was open for 3% -> 2% of each run, Pallas kernels for 3% -> 2%
where the time goes in v10:
time: 150 us; the launch traced here: 148 us
  blocking collectives  55.1 us (37%)
  waiting for transfers between devices  39.3 us (26%)
  starting transfers between devices  36.7 us (24%)
  Pallas kernels  12.9 us (9%)
  matrix products  1.68 us (1%)
    all_to_all x1, blocking collectives, on_device(): lax.all_to_all(picked.reshape(shards, mine, 3 * head_width), 'seq', 0, 0)  40.5 us
    all_gather x1, blocking collectives, on_device(): gathered = lax.all_gather(mixed, 'section', axis=1, tiled=True)  14.6 us
    all_to_all x1, waiting for transfers between devices, on_device(): incoming = lax.all_to_all(outgoing, 'section', 0, 0)  11.1 us
    all_to_all x1, waiting for transfers between devices, on_device(): lax.all_to_all(partial.reshape(shards, mine, 2 * head_width), 'seq', 0, 0)  10.6 us
    all_to_all x1, waiting for transfers between devices, on_device(): lax.all_to_all(header_copies, 'seq', 0, 0).reshape(-1, 3 * head_width)  8.85 us
    all_to_all x1, starting transfers between devices, on_device(): lax.all_to_all(partial.reshape(shards, mine, 2 * head_width), 'seq', 0, 0)  8.63 us
    all_to_all x1, starting transfers between devices, on_device(): lax.all_to_all(result_copies, ('section', 'seq'), 0, 0)  8.55 us
    all_to_all x1, waiting for transfers between devices, on_device(): arrived = lax.all_to_all(payload, 'section', 0, 0)  8.09 us
  transfers between devices with their start and end apart: 7, of which 5 were waited for; matrix products, arithmetic and copies ran while one was open for 2% of the time, Pallas kernels for 2%

profile of v10, /device:TPU:1, one launch (start us, length us, event | category | flops | bytes accessed | tf_op | source)
XLA Modules:
  0.0 148.2 jit_solution(10104376987592498704)
XLA Ops:
  0.0 4.7 %shard_map.82 = bf16[4,1296,128]{2,1,0:T(8,128)(2,1)} custom-call(bf16[1024]{0:T(1024)(128)(2,1)} %gain.1, bf16[512,1024]{1,0:T(8,128)(2,1)} %x.1, bf16[4096,128]{1,0:T(8,128)(2,1)} %query_weight.1, bf16[1024,128]{1,0:T(8,128)(2,1)} %key_weight.1, bf16[1024,128]{1,0:T(8,128)(2,1)} %value_weight.1), custom_call_target="tpu_custom_call" | custom-call | tf_op jit(solution)/shard_map/pallas_call | solution.py:300
  4.8 0.0 copy-start.4
  4.8 4.9 %all-to-all-start = ((bf16[4,1296,128]{2,1,0:T(8,128)(2,1)}), bf16[4,1296,128]{2,1,0:T(8,128)(2,1)S(1)}, u32[]{:S(2)}, u32[]{:S(2)}) async-start(bf16[4,1296,128]{2,1,0:T(8,128)(2,1)} %shard_map.82), calls=%async_computation | async-start | bytes 2654208 | tf_op jit(solution)/shard_map/all_to_all | solution.py:318
  9.7 1.0 multiply_sine_fusion
  10.7 0.1 fusion.1
  10.8 11.1 %all-to-all-done.arrived = bf16[4,1296,128]{2,1,0:T(8,128)(2,1)S(1)} async-done(((bf16[4,1296,128]{2,1,0:T(8,128)(2,1)}), bf16[4,1296,128]{2,1,0:T(8,128)(2,1)S(1)}, u32[]{:S(2)}, u32[]{:S(2)}) %all-to-all-start) | async-done | bytes 1327136 | tf_op jit(solution)/shard_map/all_to_all | solution.py:318
  21.9 1.7 %shard_map.83 = bf16[4,768,128]{2,1,0:T(8,128)(2,1)} custom-call(s32[1]{0:T(128)} %bitcast.1.place, bf16[512,1024]{1,0:T(8,128)(2,1)S(1)} %copy-done, bf16[1,1024]{1,0:T(2,128)(2,1)S(1)} %broadcast_in_dim.2.gain, bf16[4,1296,128]{2,1,0:T(8,128)(2,1)S(1)} %all-to-all-done.arrived, f32[128,128]{1,0:T(8,128)S(1)} %get-tuple-element.33.cosine, ...), custom_call_target="tpu_custom_call" | custom-call | tf_op jit(solution)/shard_map/pallas_call | solution.py:40
  23.6 3.6 %all-to-all-start.1 = ((bf16[4,768,128]{2,1,0:T(8,128)(2,1)}), bf16[4,768,128]{2,1,0:T(8,128)(2,1)S(1)}, u32[]{:S(2)}, u32[]{:S(2)}) async-start(bf16[4,768,128]{2,1,0:T(8,128)(2,1)} %shard_map.83), calls=%async_computation.1 | async-start | bytes 1572864 | tf_op jit(solution)/shard_map/all_to_all | solution.py:332
  27.2 0.2 pad_maximum_fusion
  27.4 8.1 %all-to-all-done.1.arrived = bf16[4,768,128]{2,1,0:T(8,128)(2,1)S(1)} async-done(((bf16[4,768,128]{2,1,0:T(8,128)(2,1)}), bf16[4,768,128]{2,1,0:T(8,128)(2,1)S(1)}, u32[]{:S(2)}, u32[]{:S(2)}) %all-to-all-start.1) | async-done | bytes 786464 | tf_op jit(solution)/shard_map/all_to_all | solution.py:332
  35.5 0.7 shard_map.84
  36.2 0.1 reshape.30
  36.3 40.5 %all_to_all.30.spread = bf16[128,2,384]{2,1,0:T(2,128)(2,1)S(1)} all-to-all(bf16[128,2,384]{2,1,0:T(2,128)(2,1)S(1)} %reshape.30), channel_id=1, replica_groups=mesh['section'=4,'seq'=128] {'seq'}, dimensions={0} | all-to-all | bytes 393216 | tf_op jit(solution)/shard_map/all_to_all | solution.py:344
  76.8 1.3 shard_map.85
  78.1 5.6 %all-to-all-start.3 = ((bf16[128,2,384]{2,1,0:T(2,128)(2,1)}), bf16[128,2,384]{2,1,0:T(2,128)(2,1)S(1)}, u32[]{:S(2)}, u32[]{:S(2)}) async-start(bf16[128,2,384]{2,1,0:T(2,128)(2,1)} %shard_map.85), calls=%async_computation.3 | async-start | bytes 393216 | tf_op jit(solution)/shard_map/all_to_all | solution.py:352
  83.7 3.5 %collective-permute-start = (bf16[256,256]{1,0:T(8,128)(2,1)S(1)}, bf16[256,256]{1,0:T(8,128)(2,1)S(1)}, u32[]{:S(2)}, u32[]{:S(2)}) collective-permute-start(bf16[256,256]{1,0:T(8,128)(2,1)S(1)} %get-tuple-element.28), channel_id=1, source_target_pairs={{0,1},{1,2},{2,3},{3,4},{4,5},{5,6},{6,7},{7,8},{8,9},{9,10},{10,1... | collective-permute-start | bytes 393224 | tf_op jit(solution)/shard_map/ppermute | solution.py:20
  87.2 1.9 %collective-permute-start.1 = (bf16[256,256]{1,0:T(8,128)(2,1)S(1)}, bf16[256,256]{1,0:T(8,128)(2,1)S(1)}, u32[]{:S(2)}, u32[]{:S(2)}) collective-permute-start(bf16[256,256]{1,0:T(8,128)(2,1)S(1)} %get-tuple-element.27), channel_id=1, source_target_pairs={{0,127},{1,0},{2,1},{3,2},{4,3},{5,4},{6,5},{7,6},{8,7},{9,8},{10,... | collective-permute-start | bytes 393224 | tf_op jit(solution)/shard_map/ppermute | solution.py:20
  89.1 8.9 %all-to-all-done.3 = bf16[128,2,384]{2,1,0:T(2,128)(2,1)S(1)} async-done(((bf16[128,2,384]{2,1,0:T(2,128)(2,1)}), bf16[128,2,384]{2,1,0:T(2,128)(2,1)S(1)}, u32[]{:S(2)}, u32[]{:S(2)}) %all-to-all-start.3) | async-done | bytes 196640 | tf_op jit(solution)/shard_map/all_to_all | solution.py:352
  98.0 0.1 reshape.31.header
  98.1 0.5 shard_map.86
  98.5 0.0 collective-permute-done.before
  98.6 0.7 reshape.32
  99.3 8.6 %all-to-all-start.4 = ((bf16[128,2,256]{2,1,0:T(2,128)(2,1)}), bf16[128,2,256]{2,1,0:T(2,128)(2,1)S(1)}, u32[]{:S(2)}, u32[]{:S(2)}) async-start(bf16[128,2,256]{2,1,0:T(2,128)(2,1)} %reshape.32), calls=%async_computation.4 | async-start | bytes 262144 | tf_op jit(solution)/shard_map/all_to_all | solution.py:365
  107.9 0.0 copy-start.1
  107.9 2.1 %shard_map.88 = bf16[512,128]{1,0:T(8,128)(2,1)S(1)} custom-call(s32[1]{0:T(128)} %bitcast.seq_place, s32[4]{0:T(128)S(1)} %copy-done.3, s32[2]{0:T(128)S(1)} %copy-done.2, bf16[512,128]{1,0:T(8,128)(2,1)S(1)} %get-tuple-element.22.queries, bf16[256,256]{1,0:T(8,128)(2,1)S(1)} %collective-permute-done.before, ...), custom_call_target="tpu_custom_call" | custom-call | tf_op jit(solution)/shard_map/pallas_call | solution.py:40
  110.1 10.6 %all-to-all-done.4.parts = bf16[128,2,256]{2,1,0:T(2,128)(2,1)S(1)} async-done(((bf16[128,2,256]{2,1,0:T(2,128)(2,1)}), bf16[128,2,256]{2,1,0:T(2,128)(2,1)S(1)}, u32[]{:S(2)}, u32[]{:S(2)}) %all-to-all-start.4) | async-done | bytes 131104 | tf_op jit(solution)/shard_map/all_to_all | solution.py:365
  120.6 1.3 shard_map.87
  122.0 8.6 %all-to-all-start.5 = ((bf16[512,2,128]{2,1,0:T(2,128)(2,1)}), bf16[512,2,128]{2,1,0:T(2,128)(2,1)S(1)}, u32[]{:S(2)}, u32[]{:S(2)}) async-start(bf16[512,2,128]{2,1,0:T(2,128)(2,1)} %shard_map.87), calls=%async_computation.5 | async-start | bytes 524288 | tf_op jit(solution)/shard_map/all_to_all | solution.py:377
  130.5 14.6 %all_gather.3 = bf16[512,512]{1,0:T(8,128)(2,1)S(1)} all-gather(bf16[512,128]{1,0:T(8,128)(2,1)S(1)} %shard_map.88), channel_id=1, replica_groups=mesh['section'=4,'seq'=128] {'section'}, dimensions={1}, use_global_device_ids=true | all-gather | bytes 655360 | tf_op jit(solution)/shard_map/all_gather | solution.py:380
  145.2 1.7 %convolution_convert_fusion._ = bf16[512,1024]{1,0:T(8,128)(2,1)} fusion(bf16[512,512]{1,0:T(8,128)(2,1)S(1)} %all_gather.3, bf16[512,1024]{1,0:T(8,128)(2,1)S(1)} %copy-done.1), kind=kOutput, calls=%fused_computation | convolution fusion | flops 537395200 | bytes 2621440 | tf_op jit(solution)/shard_map/dot_general | solution.py:381
  146.9 0.6 all-to-all-done.5
  147.5 0.6 shard_map.89
  (13 shorter events, 0.1 us)
Async XLA Ops:
  4.8 4.9 %copy-start.4 = (bf16[1024]{0:T(1024)(128)(2,1)S(1)}, bf16[1024]{0:T(1024)(128)(2,1)}, u32[]{:S(2)}) copy-start(bf16[1024]{0:T(1024)(128)(2,1)} %gain.1) | copy-start | bytes 6148
  4.8 17.1 %all-to-all-start = ((bf16[4,1296,128]{2,1,0:T(8,128)(2,1)}), bf16[4,1296,128]{2,1,0:T(8,128)(2,1)S(1)}, u32[]{:S(2)}, u32[]{:S(2)}) async-start(bf16[4,1296,128]{2,1,0:T(8,128)(2,1)} %shard_map.82), calls=%async_computation | async-start | bytes 2654208 | tf_op jit(solution)/shard_map/all_to_all | solution.py:318
  9.6 12.3 %copy-start = (bf16[512,1024]{1,0:T(8,128)(2,1)S(1)}, bf16[512,1024]{1,0:T(8,128)(2,1)}, u32[]{:S(2)}) copy-start(bf16[512,1024]{1,0:T(8,128)(2,1)} %x.1) | copy-start | bytes 3145732
  23.6 11.9 %copy-start.2 = (s32[2]{0:T(128)S(1)}, s32[2]{0:T(128)}, u32[]{:S(2)}) copy-start(s32[2]{0:T(128)} %header_ids.7) | copy-start | bytes 28
  23.6 11.9 %all-to-all-start.1 = ((bf16[4,768,128]{2,1,0:T(8,128)(2,1)}), bf16[4,768,128]{2,1,0:T(8,128)(2,1)S(1)}, u32[]{:S(2)}, u32[]{:S(2)}) async-start(bf16[4,768,128]{2,1,0:T(8,128)(2,1)} %shard_map.83), calls=%async_computation.1 | async-start | bytes 1572864 | tf_op jit(solution)/shard_map/all_to_all | solution.py:332
  76.8 31.1 %copy-start.3 = (s32[4]{0:T(128)S(1)}, s32[4]{0:T(128)}, u32[]{:S(2)}) copy-start(s32[4]{0:T(128)} %reach.1) | copy-start | bytes 52
  78.1 19.9 %all-to-all-start.3 = ((bf16[128,2,384]{2,1,0:T(2,128)(2,1)}), bf16[128,2,384]{2,1,0:T(2,128)(2,1)S(1)}, u32[]{:S(2)}, u32[]{:S(2)}) async-start(bf16[128,2,384]{2,1,0:T(2,128)(2,1)} %shard_map.85), calls=%async_computation.3 | async-start | bytes 393216 | tf_op jit(solution)/shard_map/all_to_all | solution.py:352
  83.7 14.9 %collective-permute-start = (bf16[256,256]{1,0:T(8,128)(2,1)S(1)}, bf16[256,256]{1,0:T(8,128)(2,1)S(1)}, u32[]{:S(2)}, u32[]{:S(2)}) collective-permute-start(bf16[256,256]{1,0:T(8,128)(2,1)S(1)} %get-tuple-element.28), channel_id=1, source_target_pairs={{0,1},{1,2},{2,3},{3,4},{4,5},{5,6},{6,7},{7,8},{8,9},{9,10},{10,1... | collective-permute-start | bytes 393224 | tf_op jit(solution)/shard_map/ppermute | solution.py:20
  87.2 11.4 %collective-permute-start.1 = (bf16[256,256]{1,0:T(8,128)(2,1)S(1)}, bf16[256,256]{1,0:T(8,128)(2,1)S(1)}, u32[]{:S(2)}, u32[]{:S(2)}) collective-permute-start(bf16[256,256]{1,0:T(8,128)(2,1)S(1)} %get-tuple-element.27), channel_id=1, source_target_pairs={{0,127},{1,0},{2,1},{3,2},{4,3},{5,4},{6,5},{7,6},{8,7},{9,8},{10,... | collective-permute-start | bytes 393224 | tf_op jit(solution)/shard_map/ppermute | solution.py:20
  99.3 21.4 %all-to-all-start.4 = ((bf16[128,2,256]{2,1,0:T(2,128)(2,1)}), bf16[128,2,256]{2,1,0:T(2,128)(2,1)S(1)}, u32[]{:S(2)}, u32[]{:S(2)}) async-start(bf16[128,2,256]{2,1,0:T(2,128)(2,1)} %reshape.32), calls=%async_computation.4 | async-start | bytes 262144 | tf_op jit(solution)/shard_map/all_to_all | solution.py:365
  107.9 37.2 %copy-start.1 = (bf16[512,1024]{1,0:T(8,128)(2,1)S(1)}, bf16[512,1024]{1,0:T(8,128)(2,1)}, u32[]{:S(2)}) copy-start(bf16[512,1024]{1,0:T(8,128)(2,1)} %weight.1) | copy-start | bytes 3145732
  122.0 25.5 %all-to-all-start.5 = ((bf16[512,2,128]{2,1,0:T(2,128)(2,1)}), bf16[512,2,128]{2,1,0:T(2,128)(2,1)S(1)}, u32[]{:S(2)}, u32[]{:S(2)}) async-start(bf16[512,2,128]{2,1,0:T(2,128)(2,1)} %shard_map.87), calls=%async_computation.5 | async-start | bytes 524288 | tf_op jit(solution)/shard_map/all_to_all | solution.py:377

commit v11 on v10

--- a/solution.py
+++ b/solution.py
@@ -348,10 +348,10 @@
         [places[1], header_ids, jnp.full((1,), local_blocks, jnp.int32)],
         [spread],
     )
-    header_copies, edges = lax.optimization_barrier((header_copies, stacked))
+    margin_rows = REACH * BLOCK
+    before = shift(stacked[rows - margin_rows :], "seq", 1)
+    header_copies, edges, before = lax.optimization_barrier((header_copies, stacked, before))
     header_pack = lax.all_to_all(header_copies, "seq", 0, 0).reshape(-1, 3 * head_width)
-    margin_rows = REACH * BLOCK
-    before = shift(edges[rows - margin_rows :], "seq", 1)
     after = shift(edges[:margin_rows], "seq", -1)
     (partial,) = call(
         far_kernel,
@@ -359,9 +359,7 @@
         [],
         [header_pack, stacked],
     )
-    partial, queries, before, after = lax.optimization_barrier(
-        (partial, queries, before, after)
-    )
+    partial, queries, after = lax.optimization_barrier((partial, queries, after))
     parts = lax.all_to_all(partial.reshape(shards, mine, 2 * head_width), "seq", 0, 0)
     everywhere = sections * shards
     (mixed,) = call(

time: 150 us -> 148 us (0.987)
  blocking collectives: 55.1 us -> 14.7 us
  starting transfers between devices: 36.7 us -> 61.4 us
  waiting for transfers between devices: 39.3 us -> 52.3 us
    all_to_all x1 -> x0, blocking collectives: 40.5 us -> none  [on_device(): lax.all_to_all(picked.reshape(shards, mine, 3 * head_width), 'seq', 0, 0)]
    all_to_all x0 -> x1, starting transfers between devices: none -> 26.7 us  [on_device(): lax.all_to_all(picked.reshape(shards, mine, 3 * head_width), 'seq', 0, 0)]
    all_to_all x0 -> x1, waiting for transfers between devices: none -> 10.7 us  [on_device(): lax.all_to_all(picked.reshape(shards, mine, 3 * head_width), 'seq', 0, 0)]
    all_to_all x1, starting transfers between devices: 8.63 us -> 5.57 us  [on_device(): lax.all_to_all(partial.reshape(shards, mine, 2 * head_width), 'seq', 0, 0)]
    all_to_all x1, waiting for transfers between devices: 8.85 us -> 11.2 us  [on_device(): lax.all_to_all(header_copies, 'seq', 0, 0).reshape(-1, 3 * head_width)]
  transfers between devices with their start and end apart: 7 -> 8, of which waited for: 5 -> 6; matrix products, arithmetic and copies ran while one was open for 2% -> 2% of each run, Pallas kernels for 2% -> 3%
where the time goes in v11:
time: 148 us; the launch traced here: 146 us
  starting transfers between devices  61.4 us (41%)
  waiting for transfers between devices  52.3 us (35%)
  blocking collectives  14.7 us (10%)
  Pallas kernels  12.9 us (9%)
  matrix products  1.71 us (1%)
  local copies, waits for them, and re-layouts  1.59 us (1%)
    all_to_all x1, starting transfers between devices, on_device(): lax.all_to_all(picked.reshape(shards, mine, 3 * head_width), 'seq', 0, 0)  26.7 us
    all_gather x1, blocking collectives, on_device(): gathered = lax.all_gather(mixed, 'section', axis=1, tiled=True)  14.7 us
    all_to_all x1, waiting for transfers between devices, on_device(): lax.all_to_all(header_copies, 'seq', 0, 0).reshape(-1, 3 * head_width)  11.2 us
    all_to_all x1, waiting for transfers between devices, on_device(): incoming = lax.all_to_all(outgoing, 'section', 0, 0)  11.1 us
    all_to_all x1, waiting for transfers between devices, on_device(): lax.all_to_all(partial.reshape(shards, mine, 2 * head_width), 'seq', 0, 0)  10.7 us
    all_to_all x1, waiting for transfers between devices, on_device(): lax.all_to_all(picked.reshape(shards, mine, 3 * head_width), 'seq', 0, 0)  10.7 us
    all_to_all x1, starting transfers between devices, on_device(): lax.all_to_all(result_copies, ('section', 'seq'), 0, 0)  8.58 us
    all_to_all x1, waiting for transfers between devices, on_device(): arrived = lax.all_to_all(payload, 'section', 0, 0)  8.09 us
  transfers between devices with their start and end apart: 8, of which 6 were waited for; matrix products, arithmetic and copies ran while one was open for 2% of the time, Pallas kernels for 3%

profile of v11, /device:TPU:1, one launch (start us, length us, event | category | flops | bytes accessed | tf_op | source)
XLA Modules:
  0.0 146.3 jit_solution(1264227160864140434)
XLA Ops:
  0.0 4.8 %shard_map.82 = bf16[4,1296,128]{2,1,0:T(8,128)(2,1)} custom-call(bf16[1024]{0:T(1024)(128)(2,1)} %gain.1, bf16[512,1024]{1,0:T(8,128)(2,1)} %x.1, bf16[4096,128]{1,0:T(8,128)(2,1)} %query_weight.1, bf16[1024,128]{1,0:T(8,128)(2,1)} %key_weight.1, bf16[1024,128]{1,0:T(8,128)(2,1)} %value_weight.1), custom_call_target="tpu_custom_call" | custom-call | tf_op jit(solution)/shard_map/pallas_call | solution.py:300
  4.8 0.0 copy-start.4
  4.8 4.9 %all-to-all-start = ((bf16[4,1296,128]{2,1,0:T(8,128)(2,1)}), bf16[4,1296,128]{2,1,0:T(8,128)(2,1)S(1)}, u32[]{:S(2)}, u32[]{:S(2)}) async-start(bf16[4,1296,128]{2,1,0:T(8,128)(2,1)} %shard_map.82), calls=%async_computation | async-start | bytes 2654208 | tf_op jit(solution)/shard_map/all_to_all | solution.py:318
  9.7 1.0 multiply_sine_fusion
  10.7 0.1 fusion.1
  10.8 11.1 %all-to-all-done.arrived = bf16[4,1296,128]{2,1,0:T(8,128)(2,1)S(1)} async-done(((bf16[4,1296,128]{2,1,0:T(8,128)(2,1)}), bf16[4,1296,128]{2,1,0:T(8,128)(2,1)S(1)}, u32[]{:S(2)}, u32[]{:S(2)}) %all-to-all-start) | async-done | bytes 1327136 | tf_op jit(solution)/shard_map/all_to_all | solution.py:318
  21.9 1.7 %shard_map.83 = bf16[4,768,128]{2,1,0:T(8,128)(2,1)} custom-call(s32[1]{0:T(128)} %bitcast.1.place, bf16[512,1024]{1,0:T(8,128)(2,1)S(1)} %copy-done, bf16[1,1024]{1,0:T(2,128)(2,1)S(1)} %broadcast_in_dim.2.gain, bf16[4,1296,128]{2,1,0:T(8,128)(2,1)S(1)} %all-to-all-done.arrived, f32[128,128]{1,0:T(8,128)S(1)} %get-tuple-element.31.cosine, ...), custom_call_target="tpu_custom_call" | custom-call | tf_op jit(solution)/shard_map/pallas_call | solution.py:40
  23.6 3.6 %all-to-all-start.1 = ((bf16[4,768,128]{2,1,0:T(8,128)(2,1)}), bf16[4,768,128]{2,1,0:T(8,128)(2,1)S(1)}, u32[]{:S(2)}, u32[]{:S(2)}) async-start(bf16[4,768,128]{2,1,0:T(8,128)(2,1)} %shard_map.83), calls=%async_computation.1 | async-start | bytes 1572864 | tf_op jit(solution)/shard_map/all_to_all | solution.py:332
  27.2 0.2 pad_maximum_fusion
  27.4 8.1 %all-to-all-done.1.arrived = bf16[4,768,128]{2,1,0:T(8,128)(2,1)S(1)} async-done(((bf16[4,768,128]{2,1,0:T(8,128)(2,1)}), bf16[4,768,128]{2,1,0:T(8,128)(2,1)S(1)}, u32[]{:S(2)}, u32[]{:S(2)}) %all-to-all-start.1) | async-done | bytes 786464 | tf_op jit(solution)/shard_map/all_to_all | solution.py:332
  35.5 0.7 shard_map.84
  36.2 0.8 reshape.30
  37.0 26.7 %all-to-all-start.2 = ((bf16[128,2,384]{2,1,0:T(2,128)(2,1)}), bf16[128,2,384]{2,1,0:T(2,128)(2,1)S(1)}, u32[]{:S(2)}, u32[]{:S(2)}) async-start(bf16[128,2,384]{2,1,0:T(2,128)(2,1)} %reshape.30), calls=%async_computation.2 | async-start | bytes 393216 | tf_op jit(solution)/shard_map/all_to_all | solution.py:344
  63.7 0.0 copy-start.3
  63.7 3.5 %collective-permute-start = (bf16[256,256]{1,0:T(8,128)(2,1)S(1)}, bf16[256,256]{1,0:T(8,128)(2,1)S(1)}, u32[]{:S(2)}, u32[]{:S(2)}) collective-permute-start(bf16[256,256]{1,0:T(8,128)(2,1)S(1)} %slice.6), channel_id=1, source_target_pairs={{0,1},{1,2},{2,3},{3,4},{4,5},{5,6},{6,7},{7,8},{8,9},{9,10},{10,1... | collective-permute-start | bytes 393224 | tf_op jit(solution)/shard_map/ppermute | solution.py:20
  67.3 10.7 %all-to-all-done.2.spread = bf16[128,2,384]{2,1,0:T(2,128)(2,1)S(1)} async-done(((bf16[128,2,384]{2,1,0:T(2,128)(2,1)}), bf16[128,2,384]{2,1,0:T(2,128)(2,1)S(1)}, u32[]{:S(2)}, u32[]{:S(2)}) %all-to-all-start.2) | async-done | bytes 196640 | tf_op jit(solution)/shard_map/all_to_all | solution.py:344
  78.0 1.3 shard_map.85
  79.2 5.7 %all-to-all-start.3 = ((bf16[128,2,384]{2,1,0:T(2,128)(2,1)}), bf16[128,2,384]{2,1,0:T(2,128)(2,1)S(1)}, u32[]{:S(2)}, u32[]{:S(2)}) async-start(bf16[128,2,384]{2,1,0:T(2,128)(2,1)} %shard_map.85), calls=%async_computation.3 | async-start | bytes 393216 | tf_op jit(solution)/shard_map/all_to_all | solution.py:354
  85.0 2.8 %collective-permute-start.1 = (bf16[256,256]{1,0:T(8,128)(2,1)S(1)}, bf16[256,256]{1,0:T(8,128)(2,1)S(1)}, u32[]{:S(2)}, u32[]{:S(2)}) collective-permute-start(bf16[256,256]{1,0:T(8,128)(2,1)S(1)} %slice.7), channel_id=1, source_target_pairs={{0,127},{1,0},{2,1},{3,2},{4,3},{5,4},{6,5},{7,6},{8,7},{9,8},{10,... | collective-permute-start | bytes 393224 | tf_op jit(solution)/shard_map/ppermute | solution.py:20
  87.8 11.2 %all-to-all-done.3 = bf16[128,2,384]{2,1,0:T(2,128)(2,1)S(1)} async-done(((bf16[128,2,384]{2,1,0:T(2,128)(2,1)}), bf16[128,2,384]{2,1,0:T(2,128)(2,1)S(1)}, u32[]{:S(2)}, u32[]{:S(2)}) %all-to-all-start.3) | async-done | bytes 196640 | tf_op jit(solution)/shard_map/all_to_all | solution.py:354
  98.9 0.1 reshape.31.header
  99.0 0.5 shard_map.86
  99.5 0.7 reshape.32
  100.2 5.6 %all-to-all-start.4 = ((bf16[128,2,256]{2,1,0:T(2,128)(2,1)}), bf16[128,2,256]{2,1,0:T(2,128)(2,1)S(1)}, u32[]{:S(2)}, u32[]{:S(2)}) async-start(bf16[128,2,256]{2,1,0:T(2,128)(2,1)} %reshape.32), calls=%async_computation.4 | async-start | bytes 262144 | tf_op jit(solution)/shard_map/all_to_all | solution.py:363
  105.8 2.1 %shard_map.88 = bf16[512,128]{1,0:T(8,128)(2,1)S(1)} custom-call(s32[1]{0:T(128)} %bitcast.seq_place, s32[4]{0:T(128)S(1)} %copy-done.3, s32[2]{0:T(128)S(1)} %copy-done.2, bf16[512,128]{1,0:T(8,128)(2,1)S(1)} %get-tuple-element.22.queries, bf16[256,256]{1,0:T(8,128)(2,1)S(1)} %collective-permute-done.before, ...), custom_call_target="tpu_custom_call" | custom-call | tf_op jit(solution)/shard_map/pallas_call | solution.py:40
  108.0 10.7 %all-to-all-done.4.parts = bf16[128,2,256]{2,1,0:T(2,128)(2,1)S(1)} async-done(((bf16[128,2,256]{2,1,0:T(2,128)(2,1)}), bf16[128,2,256]{2,1,0:T(2,128)(2,1)S(1)}, u32[]{:S(2)}, u32[]{:S(2)}) %all-to-all-start.4) | async-done | bytes 131104 | tf_op jit(solution)/shard_map/all_to_all | solution.py:363
  118.6 1.3 shard_map.87
  120.0 8.6 %all-to-all-start.5 = ((bf16[512,2,128]{2,1,0:T(2,128)(2,1)}), bf16[512,2,128]{2,1,0:T(2,128)(2,1)S(1)}, u32[]{:S(2)}, u32[]{:S(2)}) async-start(bf16[512,2,128]{2,1,0:T(2,128)(2,1)} %shard_map.87), calls=%async_computation.5 | async-start | bytes 524288 | tf_op jit(solution)/shard_map/all_to_all | solution.py:375
  128.6 14.7 %all_gather.3 = bf16[512,512]{1,0:T(8,128)(2,1)S(1)} all-gather(bf16[512,128]{1,0:T(8,128)(2,1)S(1)} %shard_map.88), channel_id=1, replica_groups=mesh['section'=4,'seq'=128] {'section'}, dimensions={1}, use_global_device_ids=true | all-gather | bytes 655360 | tf_op jit(solution)/shard_map/all_gather | solution.py:378
  143.2 1.7 %convolution_convert_fusion._ = bf16[512,1024]{1,0:T(8,128)(2,1)} fusion(bf16[512,512]{1,0:T(8,128)(2,1)S(1)} %all_gather.3, bf16[512,1024]{1,0:T(8,128)(2,1)S(1)} %copy-done.1), kind=kOutput, calls=%fused_computation | convolution fusion | flops 537395200 | bytes 2621440 | tf_op jit(solution)/shard_map/dot_general | solution.py:379
  145.0 0.6 all-to-all-done.5
  145.5 0.6 shard_map.89
  (15 shorter events, 0.1 us)
Async XLA Ops:
  4.8 4.9 %copy-start.4 = (bf16[1024]{0:T(1024)(128)(2,1)S(1)}, bf16[1024]{0:T(1024)(128)(2,1)}, u32[]{:S(2)}) copy-start(bf16[1024]{0:T(1024)(128)(2,1)} %gain.1) | copy-start | bytes 6148
  4.8 17.1 %all-to-all-start = ((bf16[4,1296,128]{2,1,0:T(8,128)(2,1)}), bf16[4,1296,128]{2,1,0:T(8,128)(2,1)S(1)}, u32[]{:S(2)}, u32[]{:S(2)}) async-start(bf16[4,1296,128]{2,1,0:T(8,128)(2,1)} %shard_map.82), calls=%async_computation | async-start | bytes 2654208 | tf_op jit(solution)/shard_map/all_to_all | solution.py:318
  9.6 12.3 %copy-start = (bf16[512,1024]{1,0:T(8,128)(2,1)S(1)}, bf16[512,1024]{1,0:T(8,128)(2,1)}, u32[]{:S(2)}) copy-start(bf16[512,1024]{1,0:T(8,128)(2,1)} %x.1) | copy-start | bytes 3145732
  23.6 11.9 %copy-start.2 = (s32[2]{0:T(128)S(1)}, s32[2]{0:T(128)}, u32[]{:S(2)}) copy-start(s32[2]{0:T(128)} %header_ids.7) | copy-start | bytes 28
  23.6 11.9 %all-to-all-start.1 = ((bf16[4,768,128]{2,1,0:T(8,128)(2,1)}), bf16[4,768,128]{2,1,0:T(8,128)(2,1)S(1)}, u32[]{:S(2)}, u32[]{:S(2)}) async-start(bf16[4,768,128]{2,1,0:T(8,128)(2,1)} %shard_map.83), calls=%async_computation.1 | async-start | bytes 1572864 | tf_op jit(solution)/shard_map/all_to_all | solution.py:332
  37.0 41.0 %all-to-all-start.2 = ((bf16[128,2,384]{2,1,0:T(2,128)(2,1)}), bf16[128,2,384]{2,1,0:T(2,128)(2,1)S(1)}, u32[]{:S(2)}, u32[]{:S(2)}) async-start(bf16[128,2,384]{2,1,0:T(2,128)(2,1)} %reshape.30), calls=%async_computation.2 | async-start | bytes 393216 | tf_op jit(solution)/shard_map/all_to_all | solution.py:344
  63.7 42.1 %copy-start.3 = (s32[4]{0:T(128)S(1)}, s32[4]{0:T(128)}, u32[]{:S(2)}) copy-start(s32[4]{0:T(128)} %reach.1) | copy-start | bytes 52
  63.7 15.5 %collective-permute-start = (bf16[256,256]{1,0:T(8,128)(2,1)S(1)}, bf16[256,256]{1,0:T(8,128)(2,1)S(1)}, u32[]{:S(2)}, u32[]{:S(2)}) collective-permute-start(bf16[256,256]{1,0:T(8,128)(2,1)S(1)} %slice.6), channel_id=1, source_target_pairs={{0,1},{1,2},{2,3},{3,4},{4,5},{5,6},{6,7},{7,8},{8,9},{9,10},{10,1... | collective-permute-start | bytes 393224 | tf_op jit(solution)/shard_map/ppermute | solution.py:20
  79.2 19.7 %all-to-all-start.3 = ((bf16[128,2,384]{2,1,0:T(2,128)(2,1)}), bf16[128,2,384]{2,1,0:T(2,128)(2,1)S(1)}, u32[]{:S(2)}, u32[]{:S(2)}) async-start(bf16[128,2,384]{2,1,0:T(2,128)(2,1)} %shard_map.85), calls=%async_computation.3 | async-start | bytes 393216 | tf_op jit(solution)/shard_map/all_to_all | solution.py:354
  85.0 14.5 %collective-permute-start.1 = (bf16[256,256]{1,0:T(8,128)(2,1)S(1)}, bf16[256,256]{1,0:T(8,128)(2,1)S(1)}, u32[]{:S(2)}, u32[]{:S(2)}) collective-permute-start(bf16[256,256]{1,0:T(8,128)(2,1)S(1)} %slice.7), channel_id=1, source_target_pairs={{0,127},{1,0},{2,1},{3,2},{4,3},{5,4},{6,5},{7,6},{8,7},{9,8},{10,... | collective-permute-start | bytes 393224 | tf_op jit(solution)/shard_map/ppermute | solution.py:20
  100.2 18.4 %all-to-all-start.4 = ((bf16[128,2,256]{2,1,0:T(2,128)(2,1)}), bf16[128,2,256]{2,1,0:T(2,128)(2,1)S(1)}, u32[]{:S(2)}, u32[]{:S(2)}) async-start(bf16[128,2,256]{2,1,0:T(2,128)(2,1)} %reshape.32), calls=%async_computation.4 | async-start | bytes 262144 | tf_op jit(solution)/shard_map/all_to_all | solution.py:363
  105.8 37.4 %copy-start.1 = (bf16[512,1024]{1,0:T(8,128)(2,1)S(1)}, bf16[512,1024]{1,0:T(8,128)(2,1)}, u32[]{:S(2)}) copy-start(bf16[512,1024]{1,0:T(8,128)(2,1)} %weight.1) | copy-start | bytes 3145732
  120.0 25.6 %all-to-all-start.5 = ((bf16[512,2,128]{2,1,0:T(2,128)(2,1)}), bf16[512,2,128]{2,1,0:T(2,128)(2,1)S(1)}, u32[]{:S(2)}, u32[]{:S(2)}) async-start(bf16[512,2,128]{2,1,0:T(2,128)(2,1)} %shard_map.87), calls=%async_computation.5 | async-start | bytes 524288 | tf_op jit(solution)/shard_map/all_to_all | solution.py:375

commit v12 on v11

--- a/solution.py
+++ b/solution.py
@@ -177,10 +177,13 @@
         picked[h * size : (h + 1) * size, head_width:] = keyval[pl.ds(start, size), :]
 
 
-def repeat_kernel(seq_place, header_ids, local_blocks, spread, out):
+def repeat_kernel(seq_place, header_ids, local_blocks, spread, out, own, semaphore):
     header = lax.div(seq_place[0] * spread.shape[1], BLOCK)
-    rows = spread[lax.div(header_ids[header], local_blocks[0])]
-    out[...] = jnp.broadcast_to(rows[None], out.shape)
+    owner = lax.div(header_ids[header], local_blocks[0])
+    copy = pltpu.make_async_copy(spread.at[owner], own, semaphore)
+    copy.start()
+    copy.wait()
+    out[...] = jnp.broadcast_to(own[...][None], out.shape)
 
 
 def window_kernel(
@@ -342,12 +345,15 @@
     )
 
     spread = lax.all_to_all(picked.reshape(shards, mine, 3 * head_width), "seq", 0, 0)
-    (header_copies,) = call(
+    scalar = pl.BlockSpec(memory_space=pltpu.SMEM)
+    header_copies = pl.pallas_call(
         repeat_kernel,
-        [((shards, mine, 3 * head_width), bf16)],
-        [places[1], header_ids, jnp.full((1,), local_blocks, jnp.int32)],
-        [spread],
-    )
+        out_shape=jax.ShapeDtypeStruct(spread.shape, bf16),
+        in_specs=[scalar] * 3 + [pl.BlockSpec(memory_space=pl.ANY)],
+        out_specs=pl.BlockSpec(memory_space=pltpu.VMEM),
+        scratch_shapes=[pltpu.VMEM(spread.shape[1:], bf16), pltpu.SemaphoreType.DMA],
+        compiler_params=pltpu.CompilerParams(vmem_limit_bytes=VMEM_LIMIT),
+    )(places[1], header_ids, jnp.full((1,), local_blocks, jnp.int32), spread)
     margin_rows = REACH * BLOCK
     before = shift(stacked[rows - margin_rows :], "seq", 1)
     header_copies, edges, before = lax.optimization_barrier((header_copies, stacked, before))

time: 148 us -> 148 us (level)
    pallas_call x6 -> x5, Pallas kernels: 7.58 us -> 6.32 us  [call(): pl.pallas_call(kernel, out_shape=[jax.ShapeDtypeStruct(shape, dtype) for...]
where the time goes in v12:
time: 148 us; the launch traced here: 146 us
  starting transfers between devices  61.4 us (41%)
  waiting for transfers between devices  52.3 us (35%)
  blocking collectives  14.7 us (10%)
  Pallas kernels  12.9 us (9%)
  matrix products  1.71 us (1%)
  local copies, waits for them, and re-layouts  1.59 us (1%)
    all_to_all x1, starting transfers between devices, on_device(): lax.all_to_all(picked.reshape(shards, mine, 3 * head_width), 'seq', 0, 0)  26.7 us
    all_gather x1, blocking collectives, on_device(): gathered = lax.all_gather(mixed, 'section', axis=1, tiled=True)  14.7 us
    all_to_all x1, waiting for transfers between devices, on_device(): lax.all_to_all(header_copies, 'seq', 0, 0).reshape(-1, 3 * head_width)  11.2 us
    all_to_all x1, waiting for transfers between devices, on_device(): incoming = lax.all_to_all(outgoing, 'section', 0, 0)  11.1 us
    all_to_all x1, waiting for transfers between devices, on_device(): lax.all_to_all(partial.reshape(shards, mine, 2 * head_width), 'seq', 0, 0)  10.7 us
    all_to_all x1, waiting for transfers between devices, on_device(): lax.all_to_all(picked.reshape(shards, mine, 3 * head_width), 'seq', 0, 0)  10.7 us
    all_to_all x1, starting transfers between devices, on_device(): lax.all_to_all(result_copies, ('section', 'seq'), 0, 0)  8.58 us
    all_to_all x1, waiting for transfers between devices, on_device(): arrived = lax.all_to_all(payload, 'section', 0, 0)  8.09 us
  transfers between devices with their start and end apart: 8, of which 6 were waited for; matrix products, arithmetic and copies ran while one was open for 2% of the time, Pallas kernels for 3%

profile of v12, /device:TPU:1, one launch (start us, length us, event | category | flops | bytes accessed | tf_op | source)
XLA Modules:
  0.0 146.3 jit_solution(18162651811415069629)
XLA Ops:
  0.0 4.8 %shard_map.82 = bf16[4,1296,128]{2,1,0:T(8,128)(2,1)} custom-call(bf16[1024]{0:T(1024)(128)(2,1)} %gain.1, bf16[512,1024]{1,0:T(8,128)(2,1)} %x.1, bf16[4096,128]{1,0:T(8,128)(2,1)} %query_weight.1, bf16[1024,128]{1,0:T(8,128)(2,1)} %key_weight.1, bf16[1024,128]{1,0:T(8,128)(2,1)} %value_weight.1), custom_call_target="tpu_custom_call" | custom-call | tf_op jit(solution)/shard_map/pallas_call | solution.py:303
  4.8 0.0 copy-start.4
  4.8 4.9 %all-to-all-start = ((bf16[4,1296,128]{2,1,0:T(8,128)(2,1)}), bf16[4,1296,128]{2,1,0:T(8,128)(2,1)S(1)}, u32[]{:S(2)}, u32[]{:S(2)}) async-start(bf16[4,1296,128]{2,1,0:T(8,128)(2,1)} %shard_map.82), calls=%async_computation | async-start | bytes 2654208 | tf_op jit(solution)/shard_map/all_to_all | solution.py:321
  9.7 1.0 multiply_sine_fusion
  10.7 0.1 fusion.1
  10.8 11.1 %all-to-all-done.arrived = bf16[4,1296,128]{2,1,0:T(8,128)(2,1)S(1)} async-done(((bf16[4,1296,128]{2,1,0:T(8,128)(2,1)}), bf16[4,1296,128]{2,1,0:T(8,128)(2,1)S(1)}, u32[]{:S(2)}, u32[]{:S(2)}) %all-to-all-start) | async-done | bytes 1327136 | tf_op jit(solution)/shard_map/all_to_all | solution.py:321
  21.9 1.7 %shard_map.83 = bf16[4,768,128]{2,1,0:T(8,128)(2,1)} custom-call(s32[1]{0:T(128)} %bitcast.1.place, bf16[512,1024]{1,0:T(8,128)(2,1)S(1)} %copy-done, bf16[1,1024]{1,0:T(2,128)(2,1)S(1)} %broadcast_in_dim.2.gain, bf16[4,1296,128]{2,1,0:T(8,128)(2,1)S(1)} %all-to-all-done.arrived, f32[128,128]{1,0:T(8,128)S(1)} %get-tuple-element.31.cosine, ...), custom_call_target="tpu_custom_call" | custom-call | tf_op jit(solution)/shard_map/pallas_call | solution.py:40
  23.6 3.6 %all-to-all-start.1 = ((bf16[4,768,128]{2,1,0:T(8,128)(2,1)}), bf16[4,768,128]{2,1,0:T(8,128)(2,1)S(1)}, u32[]{:S(2)}, u32[]{:S(2)}) async-start(bf16[4,768,128]{2,1,0:T(8,128)(2,1)} %shard_map.83), calls=%async_computation.1 | async-start | bytes 1572864 | tf_op jit(solution)/shard_map/all_to_all | solution.py:335
  27.2 0.2 pad_maximum_fusion
  27.4 8.1 %all-to-all-done.1.arrived = bf16[4,768,128]{2,1,0:T(8,128)(2,1)S(1)} async-done(((bf16[4,768,128]{2,1,0:T(8,128)(2,1)}), bf16[4,768,128]{2,1,0:T(8,128)(2,1)S(1)}, u32[]{:S(2)}, u32[]{:S(2)}) %all-to-all-start.1) | async-done | bytes 786464 | tf_op jit(solution)/shard_map/all_to_all | solution.py:335
  35.5 0.7 shard_map.84
  36.2 0.8 reshape.30
  37.0 26.7 %all-to-all-start.2 = ((bf16[128,2,384]{2,1,0:T(2,128)(2,1)}), bf16[128,2,384]{2,1,0:T(2,128)(2,1)S(1)}, u32[]{:S(2)}, u32[]{:S(2)}) async-start(bf16[128,2,384]{2,1,0:T(2,128)(2,1)} %reshape.30), calls=%async_computation.2 | async-start | bytes 393216 | tf_op jit(solution)/shard_map/all_to_all | solution.py:347
  63.7 0.0 copy-start.3
  63.7 3.5 %collective-permute-start = (bf16[256,256]{1,0:T(8,128)(2,1)S(1)}, bf16[256,256]{1,0:T(8,128)(2,1)S(1)}, u32[]{:S(2)}, u32[]{:S(2)}) collective-permute-start(bf16[256,256]{1,0:T(8,128)(2,1)S(1)} %slice.6), channel_id=1, source_target_pairs={{0,1},{1,2},{2,3},{3,4},{4,5},{5,6},{6,7},{7,8},{8,9},{9,10},{10,1... | collective-permute-start | bytes 393224 | tf_op jit(solution)/shard_map/ppermute | solution.py:20
  67.3 10.7 %all-to-all-done.2.spread = bf16[128,2,384]{2,1,0:T(2,128)(2,1)S(1)} async-done(((bf16[128,2,384]{2,1,0:T(2,128)(2,1)}), bf16[128,2,384]{2,1,0:T(2,128)(2,1)S(1)}, u32[]{:S(2)}, u32[]{:S(2)}) %all-to-all-start.2) | async-done | bytes 196640 | tf_op jit(solution)/shard_map/all_to_all | solution.py:347
  77.9 1.3 shard_map.85
  79.2 5.7 %all-to-all-start.3 = ((bf16[128,2,384]{2,1,0:T(2,128)(2,1)}), bf16[128,2,384]{2,1,0:T(2,128)(2,1)S(1)}, u32[]{:S(2)}, u32[]{:S(2)}) async-start(bf16[128,2,384]{2,1,0:T(2,128)(2,1)} %shard_map.85), calls=%async_computation.3 | async-start | bytes 393216 | tf_op jit(solution)/shard_map/all_to_all | solution.py:360
  85.0 2.8 %collective-permute-start.1 = (bf16[256,256]{1,0:T(8,128)(2,1)S(1)}, bf16[256,256]{1,0:T(8,128)(2,1)S(1)}, u32[]{:S(2)}, u32[]{:S(2)}) collective-permute-start(bf16[256,256]{1,0:T(8,128)(2,1)S(1)} %slice.7), channel_id=1, source_target_pairs={{0,127},{1,0},{2,1},{3,2},{4,3},{5,4},{6,5},{7,6},{8,7},{9,8},{10,... | collective-permute-start | bytes 393224 | tf_op jit(solution)/shard_map/ppermute | solution.py:20
  87.8 11.2 %all-to-all-done.3 = bf16[128,2,384]{2,1,0:T(2,128)(2,1)S(1)} async-done(((bf16[128,2,384]{2,1,0:T(2,128)(2,1)}), bf16[128,2,384]{2,1,0:T(2,128)(2,1)S(1)}, u32[]{:S(2)}, u32[]{:S(2)}) %all-to-all-start.3) | async-done | bytes 196640 | tf_op jit(solution)/shard_map/all_to_all | solution.py:360
  98.9 0.1 reshape.31.header
  99.0 0.5 shard_map.86
  99.5 0.7 reshape.32
  100.2 5.6 %all-to-all-start.4 = ((bf16[128,2,256]{2,1,0:T(2,128)(2,1)}), bf16[128,2,256]{2,1,0:T(2,128)(2,1)S(1)}, u32[]{:S(2)}, u32[]{:S(2)}) async-start(bf16[128,2,256]{2,1,0:T(2,128)(2,1)} %reshape.32), calls=%async_computation.4 | async-start | bytes 262144 | tf_op jit(solution)/shard_map/all_to_all | solution.py:369
  105.8 2.1 %shard_map.88 = bf16[512,128]{1,0:T(8,128)(2,1)S(1)} custom-call(s32[1]{0:T(128)} %bitcast.seq_place, s32[4]{0:T(128)S(1)} %copy-done.3, s32[2]{0:T(128)S(1)} %copy-done.2, bf16[512,128]{1,0:T(8,128)(2,1)S(1)} %get-tuple-element.22.queries, bf16[256,256]{1,0:T(8,128)(2,1)S(1)} %collective-permute-done.before, ...), custom_call_target="tpu_custom_call" | custom-call | tf_op jit(solution)/shard_map/pallas_call | solution.py:40
  108.0 10.7 %all-to-all-done.4.parts = bf16[128,2,256]{2,1,0:T(2,128)(2,1)S(1)} async-done(((bf16[128,2,256]{2,1,0:T(2,128)(2,1)}), bf16[128,2,256]{2,1,0:T(2,128)(2,1)S(1)}, u32[]{:S(2)}, u32[]{:S(2)}) %all-to-all-start.4) | async-done | bytes 131104 | tf_op jit(solution)/shard_map/all_to_all | solution.py:369
  118.6 1.3 shard_map.87
  120.0 8.6 %all-to-all-start.5 = ((bf16[512,2,128]{2,1,0:T(2,128)(2,1)}), bf16[512,2,128]{2,1,0:T(2,128)(2,1)S(1)}, u32[]{:S(2)}, u32[]{:S(2)}) async-start(bf16[512,2,128]{2,1,0:T(2,128)(2,1)} %shard_map.87), calls=%async_computation.5 | async-start | bytes 524288 | tf_op jit(solution)/shard_map/all_to_all | solution.py:381
  128.6 14.7 %all_gather.3 = bf16[512,512]{1,0:T(8,128)(2,1)S(1)} all-gather(bf16[512,128]{1,0:T(8,128)(2,1)S(1)} %shard_map.88), channel_id=1, replica_groups=mesh['section'=4,'seq'=128] {'section'}, dimensions={1}, use_global_device_ids=true | all-gather | bytes 655360 | tf_op jit(solution)/shard_map/all_gather | solution.py:384
  143.3 1.7 %convolution_convert_fusion._ = bf16[512,1024]{1,0:T(8,128)(2,1)} fusion(bf16[512,512]{1,0:T(8,128)(2,1)S(1)} %all_gather.3, bf16[512,1024]{1,0:T(8,128)(2,1)S(1)} %copy-done.1), kind=kOutput, calls=%fused_computation | convolution fusion | flops 537395200 | bytes 2621440 | tf_op jit(solution)/shard_map/dot_general | solution.py:385
  145.0 0.6 all-to-all-done.5
  145.5 0.6 shard_map.89
  (15 shorter events, 0.1 us)
Async XLA Ops:
  4.8 4.9 %copy-start.4 = (bf16[1024]{0:T(1024)(128)(2,1)S(1)}, bf16[1024]{0:T(1024)(128)(2,1)}, u32[]{:S(2)}) copy-start(bf16[1024]{0:T(1024)(128)(2,1)} %gain.1) | copy-start | bytes 6148
  4.8 17.1 %all-to-all-start = ((bf16[4,1296,128]{2,1,0:T(8,128)(2,1)}), bf16[4,1296,128]{2,1,0:T(8,128)(2,1)S(1)}, u32[]{:S(2)}, u32[]{:S(2)}) async-start(bf16[4,1296,128]{2,1,0:T(8,128)(2,1)} %shard_map.82), calls=%async_computation | async-start | bytes 2654208 | tf_op jit(solution)/shard_map/all_to_all | solution.py:321
  9.6 12.3 %copy-start = (bf16[512,1024]{1,0:T(8,128)(2,1)S(1)}, bf16[512,1024]{1,0:T(8,128)(2,1)}, u32[]{:S(2)}) copy-start(bf16[512,1024]{1,0:T(8,128)(2,1)} %x.1) | copy-start | bytes 3145732
  23.6 11.9 %copy-start.2 = (s32[2]{0:T(128)S(1)}, s32[2]{0:T(128)}, u32[]{:S(2)}) copy-start(s32[2]{0:T(128)} %header_ids.7) | copy-start | bytes 28
  23.6 11.9 %all-to-all-start.1 = ((bf16[4,768,128]{2,1,0:T(8,128)(2,1)}), bf16[4,768,128]{2,1,0:T(8,128)(2,1)S(1)}, u32[]{:S(2)}, u32[]{:S(2)}) async-start(bf16[4,768,128]{2,1,0:T(8,128)(2,1)} %shard_map.83), calls=%async_computation.1 | async-start | bytes 1572864 | tf_op jit(solution)/shard_map/all_to_all | solution.py:335
  37.0 41.0 %all-to-all-start.2 = ((bf16[128,2,384]{2,1,0:T(2,128)(2,1)}), bf16[128,2,384]{2,1,0:T(2,128)(2,1)S(1)}, u32[]{:S(2)}, u32[]{:S(2)}) async-start(bf16[128,2,384]{2,1,0:T(2,128)(2,1)} %reshape.30), calls=%async_computation.2 | async-start | bytes 393216 | tf_op jit(solution)/shard_map/all_to_all | solution.py:347
  63.7 42.1 %copy-start.3 = (s32[4]{0:T(128)S(1)}, s32[4]{0:T(128)}, u32[]{:S(2)}) copy-start(s32[4]{0:T(128)} %reach.1) | copy-start | bytes 52
  63.7 15.5 %collective-permute-start = (bf16[256,256]{1,0:T(8,128)(2,1)S(1)}, bf16[256,256]{1,0:T(8,128)(2,1)S(1)}, u32[]{:S(2)}, u32[]{:S(2)}) collective-permute-start(bf16[256,256]{1,0:T(8,128)(2,1)S(1)} %slice.6), channel_id=1, source_target_pairs={{0,1},{1,2},{2,3},{3,4},{4,5},{5,6},{6,7},{7,8},{8,9},{9,10},{10,1... | collective-permute-start | bytes 393224 | tf_op jit(solution)/shard_map/ppermute | solution.py:20
  79.2 19.7 %all-to-all-start.3 = ((bf16[128,2,384]{2,1,0:T(2,128)(2,1)}), bf16[128,2,384]{2,1,0:T(2,128)(2,1)S(1)}, u32[]{:S(2)}, u32[]{:S(2)}) async-start(bf16[128,2,384]{2,1,0:T(2,128)(2,1)} %shard_map.85), calls=%async_computation.3 | async-start | bytes 393216 | tf_op jit(solution)/shard_map/all_to_all | solution.py:360
  85.0 14.5 %collective-permute-start.1 = (bf16[256,256]{1,0:T(8,128)(2,1)S(1)}, bf16[256,256]{1,0:T(8,128)(2,1)S(1)}, u32[]{:S(2)}, u32[]{:S(2)}) collective-permute-start(bf16[256,256]{1,0:T(8,128)(2,1)S(1)} %slice.7), channel_id=1, source_target_pairs={{0,127},{1,0},{2,1},{3,2},{4,3},{5,4},{6,5},{7,6},{8,7},{9,8},{10,... | collective-permute-start | bytes 393224 | tf_op jit(solution)/shard_map/ppermute | solution.py:20
  100.2 18.4 %all-to-all-start.4 = ((bf16[128,2,256]{2,1,0:T(2,128)(2,1)}), bf16[128,2,256]{2,1,0:T(2,128)(2,1)S(1)}, u32[]{:S(2)}, u32[]{:S(2)}) async-start(bf16[128,2,256]{2,1,0:T(2,128)(2,1)} %reshape.32), calls=%async_computation.4 | async-start | bytes 262144 | tf_op jit(solution)/shard_map/all_to_all | solution.py:369
  105.8 37.4 %copy-start.1 = (bf16[512,1024]{1,0:T(8,128)(2,1)S(1)}, bf16[512,1024]{1,0:T(8,128)(2,1)}, u32[]{:S(2)}) copy-start(bf16[512,1024]{1,0:T(8,128)(2,1)} %weight.1) | copy-start | bytes 3145732
  120.0 25.6 %all-to-all-start.5 = ((bf16[512,2,128]{2,1,0:T(2,128)(2,1)}), bf16[512,2,128]{2,1,0:T(2,128)(2,1)S(1)}, u32[]{:S(2)}, u32[]{:S(2)}) async-start(bf16[512,2,128]{2,1,0:T(2,128)(2,1)} %shard_map.87), calls=%async_computation.5 | async-start | bytes 524288 | tf_op jit(solution)/shard_map/all_to_all | solution.py:381
